TPU v7x, 256 devices: a whole 4x4x8 slice. The times are simulated.
256 devices in a mesh: dp: 2 (over y_lo), lat: 16 (over y_hi, x, core), lon: 8 (over z).
Axes of the slice: x: 4, y: 4 (y_hi: 2, y_lo: 2; y = y_hi * 2 + y_lo), z: 8, core: 2. Of those that a mesh axis runs over, the one named last changes fastest.
Arguments:
- inputs: bfloat16 [2, 2, 96, 192, 512], P('dp', None, 'lat', 'lon'), may hold values from -6 to 6
- cotangent: bfloat16 [2, 2, 96, 192, 512], P('dp', None, 'lat', 'lon'), may hold values from -6 to 6
- mask_ids: int32 [96, 192], P('lat', 'lon'), may hold values from 0 to 3
- w_qkv: bfloat16 [512, 1536], replicated, may hold values from -4 to 4
- w_proj: bfloat16 [512, 512], replicated, may hold values from -0.25 to 0.25
Outputs:
- output: bfloat16 [2, 2, 96, 192, 512], P('dp', None, 'lat', 'lon')
- grad_inputs: bfloat16 [2, 2, 96, 192, 512], P('dp', None, 'lat', 'lon')
- grad_qkv: float32 [512, 1536], P(('lat', 'lon'))
- grad_proj: float32 [512, 512], P(('lat', 'lon'))
All inputs are finite; a program needn't handle non-finite values.
Results may differ from a plain program's by a relative error of at most 0.011.
Values may be sent and summed in bfloat16 or wider, within the bound.
No kernel may reach another device: no remote copies, remote signals or barrier semaphores. Data moves between devices by JAX's collectives and lax.ppermute only.
A program may use at most 64 MiB of HBM per device.

v0:
```python
import math

import jax
import jax.numpy as jnp
from jax import lax
from jax.sharding import PartitionSpec as P

HEADS = 16
HD = 32
WLAT = 6
WLON = 12
SLAT = 3
SLON = 6


def passed_along(value, axis, steps):
    count = lax.axis_size(axis)
    pairs = [(source, (source + steps) % count) for source in range(count)]
    return lax.ppermute(value, axis, pairs)


def product(form, left, right):
    return jnp.einsum(form, left, right, preferred_element_type=jnp.float32)


def to_windows(array, n_rows, n_cols):
    batch, levels, rows, cols, width = array.shape
    shaped = array.reshape(batch, levels, n_rows, WLAT, n_cols, WLON, width)
    shaped = shaped.transpose(0, 2, 4, 1, 3, 5, 6)
    return shaped.reshape(batch * n_rows * n_cols, levels * WLAT * WLON, width)


def from_windows(array, batch, levels, n_rows, n_cols):
    width = array.shape[-1]
    shaped = array.reshape(batch, n_rows, n_cols, levels, WLAT, WLON, width)
    shaped = shaped.transpose(0, 3, 1, 4, 2, 5, 6)
    return shaped.reshape(batch, levels, n_rows * WLAT, n_cols * WLON, width)


def window_pass(rolled, grad_in, w_qkv, w_proj, groups):
    batch, levels, rows, cols, width = rolled.shape
    n_rows = rows // WLAT
    n_cols = cols // WLON
    labels = groups.reshape(n_rows, WLAT, n_cols, WLON).transpose(0, 2, 1, 3)
    labels = labels.reshape(n_rows * n_cols, 1, WLAT * WLON)
    labels = jnp.broadcast_to(labels, (n_rows * n_cols, levels, WLAT * WLON))
    labels = jnp.tile(labels.reshape(n_rows * n_cols, levels * WLAT * WLON), (batch, 1))
    allowed = (labels[:, :, None] == labels[:, None, :])[:, None]
    tokens = to_windows(rolled, n_rows, n_cols)
    upstream = to_windows(grad_in, n_rows, n_cols)
    windows, tok_count = (tokens.shape[0], tokens.shape[1])
    floats = tokens.astype(jnp.float32)
    center = jnp.mean(floats, -1, keepdims=True)
    shifted = floats - center
    inverse = lax.rsqrt(jnp.mean(shifted * shifted, -1, keepdims=True) + 1e-05)
    normed = shifted * inverse
    normed_low = normed.astype(jnp.bfloat16)
    projected = product("wnd,de->wne", normed_low, w_qkv).astype(jnp.bfloat16)
    split = projected.reshape(windows, tok_count, 3, HEADS, HD)
    queries = split[:, :, 0]
    keyset = split[:, :, 1]
    values = split[:, :, 2]
    factor = 1.0 / math.sqrt(HD)
    scores = product("wqhe,wkhe->whqk", queries, keyset) * factor
    scores = jnp.where(allowed, scores, jnp.float32(-1e30))
    highest = jnp.max(scores, -1, keepdims=True)
    exponent = jnp.exp(scores - highest)
    attention = exponent / jnp.sum(exponent, -1, keepdims=True)
    attention_low = attention.astype(jnp.bfloat16)
    mixed = product("whqk,wkhe->wqhe", attention_low, values).astype(jnp.bfloat16)
    mixed = mixed.reshape(windows, tok_count, width)
    result = (floats + product("wnd,de->wne", mixed, w_proj)).astype(jnp.bfloat16)
    grad_proj = product("wnd,wne->de", mixed, upstream)
    grad_mixed = product("wne,de->wnd", upstream, w_proj).astype(jnp.bfloat16)
    grad_mixed = grad_mixed.reshape(windows, tok_count, HEADS, HD)
    grad_attn = product("wqhe,wkhe->whqk", grad_mixed, values)
    grad_scores = attention * (grad_attn - jnp.sum(grad_attn * attention, -1, keepdims=True))
    grad_low = (grad_scores * factor).astype(jnp.bfloat16)
    grad_values = product("whqk,wqhe->wkhe", attention_low, grad_mixed).astype(jnp.bfloat16)
    grad_queries = product("whqk,wkhe->wqhe", grad_low, keyset).astype(jnp.bfloat16)
    grad_keys = product("whqk,wqhe->wkhe", grad_low, queries).astype(jnp.bfloat16)
    grad_projected = jnp.stack([grad_queries, grad_keys, grad_values], 2)
    grad_projected = grad_projected.reshape(windows, tok_count, 3 * width)
    grad_qkv = product("wnd,wne->de", normed_low, grad_projected)
    grad_normed = product("wne,de->wnd", grad_projected, w_qkv)
    grad_tokens = inverse * (
        grad_normed
        - jnp.mean(grad_normed, -1, keepdims=True)
        - normed * jnp.mean(grad_normed * normed, -1, keepdims=True)
    )
    grad_total = (upstream.astype(jnp.float32) + grad_tokens).astype(jnp.bfloat16)
    return (
        from_windows(result, batch, levels, n_rows, n_cols),
        from_windows(grad_total, batch, levels, n_rows, n_cols),
        grad_qkv,
        grad_proj,
    )


def move_one(array):
    side = passed_along(array[:, :, :, -SLON:, :], "lon", 1)
    array = jnp.concatenate([side, array[:, :, :, :-SLON, :]], axis=3)
    upper = passed_along(array[:, :, -SLAT:], "lat", 1)
    return jnp.concatenate([upper, array[:, :, :-SLAT]], axis=2)


def move_back(array):
    side = passed_along(array[:, :, :, :SLON, :], "lon", -1)
    array = jnp.concatenate([array[:, :, :, SLON:, :], side], axis=3)
    upper = passed_along(array[:, :, :SLAT], "lat", -1)
    return jnp.concatenate([array[:, :, SLAT:], upper], axis=2)


def per_device(inputs, cotangent, mask_ids, w_qkv, w_proj):
    rolled = move_one(inputs)
    grad_in = move_one(cotangent)
    row_count = mask_ids.shape[0]
    first_band = lax.axis_index("lat") == 0
    wrapped = jnp.logical_and(first_band, jnp.arange(row_count) < SLAT).astype(jnp.int32)
    groups = mask_ids + 4 * wrapped[:, None]
    result, grad_total, grad_qkv, grad_proj = window_pass(rolled, grad_in, w_qkv, w_proj, groups)
    output = move_back(result)
    grad_inputs = move_back(grad_total)
    whole = (
        lax.psum(grad_qkv.astype(jnp.bfloat16), "dp").astype(jnp.float32),
        lax.psum(grad_proj.astype(jnp.bfloat16), "dp").astype(jnp.float32),
    )
    shares = (
        lax.psum_scatter(whole[0], ("lat", "lon"), scatter_dimension=0, tiled=True),
        lax.psum_scatter(whole[1], ("lat", "lon"), scatter_dimension=0, tiled=True),
    )
    return (output, grad_inputs, shares[0], shares[1])


def solution(mesh):
    placed = (
        P("dp", None, "lat", "lon", None),
        P("dp", None, "lat", "lon", None),
        P("lat", "lon"),
        P(),
        P(),
    )
    return jax.shard_map(
        per_device,
        mesh=mesh,
        in_specs=placed,
        out_specs=(
            P("dp", None, "lat", "lon", None),
            P("dp", None, "lat", "lon", None),
            P(("lat", "lon"), None),
            P(("lat", "lon"), None),
        ),
        check_vma=False,
    )
```

profile of v0, /device:TPU:32, one launch (start us, length us, event | category | flops | bytes accessed | tf_op | source)
XLA Modules:
  0.0 845.7 jit_solution(15523501408232207230)
XLA Ops:
  7.2 1.0 slice.57
  8.3 2.0 collective-permute-start
  10.3 0.9 slice.68
  11.2 2.0 collective-permute-start.4
  13.2 0.8 broadcast_add_fusion
  14.2 1.0 fusion.53
  15.9 1.6 fusion.52
  17.5 1.1 collective-permute-start.5
  18.6 4.8 collective-permute-done.1
  23.4 1.0 fusion.47
  26.7 0.7 convolution_convert_fusion
  27.3 1.7 copy.95
  29.1 1.0 fusion.45
  30.6 1.4 convolution_convert_fusion.3
  32.2 4.0 fusion.42
  36.2 5.2 fusion.63
  41.4 8.9 %fusion.31 = bf16[2,144,1,16,32]{1,4,3,0,2:T(8,128)(2,1)} fusion(f32[2,16,144,144]{2,3,1,0:T(8,128)} %fusion.42, bf16[2,144,3,16,32]{1,4,3,2,0:T(8,128)(2,1)} %bitcast.112, f32[2,16,144,144]{2,3,1,0:T(8,128)} %get-tuple-element.27, f32[2,16,144]{2,1,0:T(8,128)S(1)} %get-tuple-element.26), kind=kOutput, calls=%fused_computation.31 | convolution fusion | flops 47264400 | bytes 19759104 | tf_op jit(solution)/shard_map/whqk,wkhe->wqhe/dot_general | solution.py:23
  50.4 8.8 %fusion.28 = bf16[2,144,1,16,32]{1,4,3,0,2:T(8,128)(2,1)} fusion(f32[2,16,144,144]{2,3,1,0:T(8,128)} %fusion.42, bf16[2,144,3,16,32]{1,4,3,2,0:T(8,128)(2,1)} %bitcast.113, f32[2,16,144,144]{2,3,1,0:T(8,128)} %get-tuple-element.27, f32[2,16,144]{2,1,0:T(8,128)S(1)} %get-tuple-element.26), kind=kOutput, calls=%fused_computation.30 | convolution fusion | flops 47264400 | bytes 19759104 | tf_op jit(solution)/shard_map/whqk,wqhe->wkhe/dot_general | solution.py:23
  59.2 3.3 fusion.34
  63.0 1.6 convolution_convert_fusion.2
  65.2 1.1 copy-done.1
  66.3 2.4 fusion.6
  68.7 1.3 fusion.27
  70.0 2.7 fusion.62
  73.7 4.0 collective-permute-start.6
  79.1 2.0 collective-permute-start.2
  81.7 1.9 collective-permute-done.2
  85.7 0.7 copy.121
  87.1 0.7 copy.120
  87.8 60.5 %all-reduce.7.cloned.1.call-done = (bf16[512,1536]{1,0:T(8,128)(2,1)}, bf16[512,512]{1,0:T(8,128)(2,1)}) async-done(((bf16[512,1536]{1,0:T(8,128)(2,1)}, bf16[512,512]{1,0:T(8,128)(2,1)}), (bf16[512,1536]{1,0:T(8,128)(2,1)}, bf16[512,512]{1,0:T(8,128)(2,1)})) %all-reduce.7.cloned.1.call-update) | async-done | bytes 2097168 | tf_op jit(solution)/shard_map/psum | solution.py:125
  148.4 688.4 %all-reduce.8 = (f32[512,1536]{1,0:T(8,128)}, f32[512,512]{1,0:T(8,128)S(1)}) all-reduce(bf16[512,1536]{1,0:T(8,128)(2,1)} %get-tuple-element.20, bf16[512,512]{1,0:T(8,128)(2,1)} %get-tuple-element.21), channel_id=2, replica_groups=mesh['dp'=2,'lat'=16,'lon'=8] {'lat','lon'}, use_global_device_ids=true, to_apply=%region_8.9.clone | all-reduce | flops 1048576 | bytes 6291456
  836.8 1.4 constant_dynamic-slice_fusion.1
  (65 shorter events, 10.4 us)
Async XLA Ops:
  7.2 19.5 %copy-start = (bf16[512,1536]{1,0:T(8,128)(2,1)S(1)}, bf16[512,1536]{1,0:T(8,128)(2,1)}, u32[]{:S(2)}) copy-start(bf16[512,1536]{1,0:T(8,128)(2,1)} %param.8) | copy-start | bytes 4718596
  7.2 141.2 %all-reduce.7.cloned.1.call-start = ((), (), s32[]{:S(2)}) async-start(), calls=%async_computation | async-start | bytes 4194304 | tf_op jit(solution)/shard_map/psum | solution.py:125
  8.3 5.9 collective-permute-start
  11.2 4.7 collective-permute-start.4
  15.2 8.3 collective-permute-start.1
  17.5 11.6 %collective-permute-start.5 = (bf16[1,2,3,24,512]{4,3,2,1,0:T(8,128)(2,1)}, bf16[1,2,3,24,512]{4,3,2,1,0:T(8,128)(2,1)}, u32[]{:S(2)}, u32[]{:S(2)}) collective-permute-start(bf16[1,2,3,24,512]{4,3,2,1,0:T(8,128)(2,1)} %fusion.52), channel_id=1, source_target_pairs={{0,8},{8,16},{16,24},{24,32},{32,40},{40,48},{48,56},{56,64},{64,7... | collective-permute-start | bytes 442376 | tf_op jit(solution)/shard_map/ppermute | solution.py:19
  24.4 4.7 copy-start.3
  59.2 3.8 copy-start.7
  63.0 1.7 copy-start.4
  63.0 1.7 copy-start.5
  65.2 1.2 copy-start.1
  70.0 7.8 copy-start.2
  72.7 11.3 %copy-start.6 = (u32[256]{0:T(256)S(1)}, u32[256]{0:T(256)}, u32[]{:S(2)}) copy-start(u32[256]{0:T(256)} %constant.34) | copy-start | bytes 3076
  73.7 7.5 collective-permute-start.6
  79.1 4.4 collective-permute-start.2
  81.6 3.7 collective-permute-start.7
  83.9 2.8 collective-permute-start.3
Sparse Core Ops, SparseCore 0:
  70.1 78.2 all-reduce.6
where the time goes:
time: 852 us; the launch traced here: 846 us
  blocking collectives  688 us (81%)
  waiting for transfers between devices  68.1 us (8%)
  matrix products  40.8 us (5%)
  between operations  15 us (2%)
  local copies, waits for them, and re-layouts  13.6 us (2%)
  starting transfers between devices  11.5 us (1%)
    unnamed x1, blocking collectives  688 us
    psum x1, waiting for transfers between devices, per_device(): lax.psum(grad_qkv.astype(jnp.bfloat16), 'dp').astype(jnp.float32)  60.5 us
    dot_general x11, matrix products, product(): return jnp.einsum(form, left, right, preferred_element_type=jnp.float32)  35.6 us
  transfers between devices with their start and end apart: 9, of which 5 were waited for; matrix products, arithmetic and copies ran while one was open for 2% of the time, Pallas kernels for 0%

commit v1 on v0

v1 whole, which is shorter than its diff:
```python
import functools
import math

import jax
import jax.numpy as jnp
from jax import lax
from jax.experimental import pallas as pl
from jax.experimental.pallas import tpu as pltpu
from jax.sharding import Mesh
from jax.sharding import PartitionSpec as P

D = 512
HEADS = 16
HD = 32
LEV = 2
WLAT = 6
WLON = 12
SLAT = 3
SLON = 6
WT = LEV * WLAT * WLON
PER = 4
LANES = PER * HD
UNITS = D // LANES
FACTOR = 1.0 / math.sqrt(HD)
LOG2E = 1.4426950408889634

NN = (((1,), (0,)), ((), ()))
NT = (((1,), (1,)), ((), ()))


def dot(left, right, dims=NN):
    return lax.dot_general(left, right, dims, preferred_element_type=jnp.float32)


def statistics(x_ref):
    x = x_ref[...].astype(jnp.float32)
    center = jnp.mean(x, -1, keepdims=True)
    shifted = x - center
    inverse = lax.rsqrt(jnp.mean(shifted * shifted, -1, keepdims=True) + 1e-05)
    return shifted * inverse, inverse


def store_shares(target_ref, grads, added_ref=None):
    count = grads.shape[0]
    first = lax.broadcasted_iota(jnp.int32, (count, 128), 0) % 8 < 4
    for quad in range(4):
        shares = ([], [])
        for pair in (2 * quad, 2 * quad + 1):
            left = grads[:, pair * 256:pair * 256 + 128]
            right = grads[:, pair * 256 + 128:pair * 256 + 256]
            shares[0].append(jnp.where(first, left, pltpu.roll(right, 4, 0)))
            shares[1].append(jnp.where(first, pltpu.roll(left, count - 4, 0), right))
        rows = slice(quad * 16, quad * 16 + 16)
        for which in range(2):
            piece = jnp.concatenate([p.reshape(count // 8, 8, 128) for p in shares[which]], axis=1)
            if added_ref is not None:
                piece = piece + added_ref[:, which, rows, :].astype(jnp.float32)
            target_ref[:, which, rows, :] = piece.astype(jnp.bfloat16)


def attention_kernel(
    x_ref, u_ref, lrow_ref, lcol_ref, wqkv_ref, wproj_ref,
    send_ref, gp_ref, mix_ref, nkeep_ref, mkeep_ref,
    proj_ref, gm_ref, nt_ref, mt_ref, mixt_ref, al_ref, gl_ref, s_ref, da_ref,
):
    windows = x_ref.shape[0] // WT
    core = lax.axis_index("core")
    half = D // 2
    normed, _ = statistics(x_ref)
    normed_low = normed.astype(jnp.bfloat16)
    proj_ref[...] = dot(normed_low, wqkv_ref[...]).astype(jnp.bfloat16)
    gm_ref[...] = dot(u_ref[...], wproj_ref[...], NT).astype(jnp.bfloat16)

    def place(target_ref, array):
        for b in range(D // 32):
            slot = lax.bitwise_xor(core, b % 2)
            row = pl.multiple_of(slot * half + (b // 2) * 32, 32)
            target_ref[pl.ds(row, 32), :] = array[b * 32:(b + 1) * 32, :]

    place(nt_ref, normed_low.T)

    lane = lax.broadcasted_iota(jnp.int32, (1, LANES), 1) // HD
    masks = [(lane == h).astype(jnp.float32) for h in range(PER)]
    low_masks = [m.astype(jnp.bfloat16) for m in masks]

    def stacked(array):
        return jnp.concatenate([array * m for m in low_masks], axis=0)

    def unstacked(array):
        total = array[:WT] * masks[0]
        for h in range(1, PER):
            total = total + array[h * WT:(h + 1) * WT] * masks[h]
        return total.astype(jnp.bfloat16)

    for w in range(windows):
        rows = slice(w * WT, (w + 1) * WT)
        allowed = lcol_ref[rows, :] == lrow_ref[w:w + 1, :]
        for g in range(UNITS):
            q_cols, k_cols, v_cols = (
                slice(part * D + g * LANES, part * D + (g + 1) * LANES) for part in range(3)
            )
            q = proj_ref[rows, q_cols]
            k = proj_ref[rows, k_cols]
            v = proj_ref[rows, v_cols]
            gm = gm_ref[rows, q_cols]
            s_ref[...] = dot(stacked(k), q, NT)
            da_ref[...] = dot(stacked(v), gm, NT)
            vt = v.T
            kt = k.T
            for h in range(PER):
                part = slice(h * WT, (h + 1) * WT)
                s = jnp.where(allowed, s_ref[part, :], jnp.float32(-1e30))
                e = jnp.exp2((s - jnp.max(s, 0, keepdims=True)) * jnp.float32(FACTOR * LOG2E))
                a = e * (1.0 / jnp.sum(e, 0, keepdims=True))
                al = a.astype(jnp.bfloat16)
                al_ref[part, :] = al
                ga = da_ref[part, :] * a
                gl = ((ga - a * jnp.sum(ga, 0, keepdims=True)) * jnp.float32(FACTOR)).astype(jnp.bfloat16)
                gl_ref[part, :] = gl
                chan = slice(g * LANES + h * HD, g * LANES + (h + 1) * HD)
                mixt_ref[chan, :] = dot(vt[h * HD:(h + 1) * HD, :], al)
                s_ref[h * HD:(h + 1) * HD, :] = dot(kt[h * HD:(h + 1) * HD, :], gl)
            gp_ref[rows, q_cols] = s_ref[:LANES, :].T.astype(jnp.bfloat16)
            gp_ref[rows, k_cols] = unstacked(dot(gl_ref[...], q))
            gp_ref[rows, v_cols] = unstacked(dot(al_ref[...], gm))
        mix_ref[rows, :] = mixt_ref[...].T.astype(jnp.bfloat16)

    place(mt_ref, mix_ref[...].T)
    nkeep_ref[...] = nt_ref[:half, :]
    mkeep_ref[...] = mt_ref[:half, :]
    grads = jnp.concatenate([dot(nt_ref[half:, :], gp_ref[...]), dot(mt_ref[half:, :], u_ref[...])], axis=1)
    store_shares(send_ref, grads)


def gradient_kernel(n_ref, m_ref, gp_ref, u_ref, got_ref, sum_ref):
    grads = jnp.concatenate([dot(n_ref[...], gp_ref[...]), dot(m_ref[...], u_ref[...])], axis=1)
    store_shares(sum_ref, grads, got_ref)


def token_kernel(x_ref, u_ref, mix_ref, gp_ref, wqkv_ref, wproj_ref, out_ref, gin_ref):
    out_ref[...] = (x_ref[...].astype(jnp.float32) + dot(mix_ref[...], wproj_ref[...])).astype(jnp.bfloat16)
    grad_normed = dot(gp_ref[...], wqkv_ref[...], NT)
    normed, inverse = statistics(x_ref)
    grad_tokens = inverse * (
        grad_normed
        - jnp.mean(grad_normed, -1, keepdims=True)
        - normed * jnp.mean(grad_normed * normed, -1, keepdims=True)
    )
    gin_ref[...] = (u_ref[...].astype(jnp.float32) + grad_tokens).astype(jnp.bfloat16)


def call(kernel, name, outs, scratch, flops, *args):
    vmem = pl.BlockSpec(memory_space=pltpu.VMEM)
    size = sum(2 * math.prod(shape) for shape in outs)
    return pl.pallas_call(
        kernel,
        out_shape=tuple(jax.ShapeDtypeStruct(shape, jnp.bfloat16) for shape in outs),
        in_specs=[vmem] * len(args),
        out_specs=(vmem,) * len(outs),
        scratch_shapes=[pltpu.VMEM(shape, dtype) for shape, dtype in scratch],
        compiler_params=pltpu.CompilerParams(vmem_limit_bytes=40 * 1024 * 1024),
        cost_estimate=pl.CostEstimate(flops=flops, bytes_accessed=2 * size, transcendentals=0),
        name=name,
    )(*args)


def attention(x, u, lrow, lcol, w_qkv, w_proj):
    tokens = x.shape[0]
    low, full = jnp.bfloat16, jnp.float32
    return call(
        attention_kernel,
        "window_attention",
        ((32, 2, 64, 128), (tokens, 3 * D), (tokens, D), (D // 2, tokens), (D // 2, tokens)),
        (
            ((tokens, 3 * D), low),
            ((tokens, D), low),
            ((D, tokens), low),
            ((D, tokens), low),
            ((D, WT), full),
            ((PER * WT, WT), low),
            ((PER * WT, WT), low),
            ((PER * WT, WT), full),
            ((PER * WT, WT), full),
        ),
        5_000_000_000,
        x, u, lrow, lcol, w_qkv, w_proj,
    )


def to_windows(array):
    batch, levels, rows, cols, width = array.shape
    shaped = array.reshape(levels, rows, cols // WLON, WLON, width)
    return shaped.transpose(2, 0, 1, 3, 4).reshape(cols // WLON * WT, width)


def from_windows(array):
    windows = array.shape[0] // WT
    shaped = array.reshape(windows, LEV, WLAT, WLON, D).transpose(1, 2, 0, 3, 4)
    return shaped.reshape(1, LEV, WLAT, windows * WLON, D)


LAT = ("yh", "x", "core")


def passed_along(value, axis, steps):
    count = lax.axis_size(axis)
    pairs = [(source, (source + steps) % count) for source in range(count)]
    return lax.ppermute(value, axis, pairs)


def diagonal(value, steps):
    n_lat, n_lon = lax.axis_size(LAT), lax.axis_size("lon")
    pairs = [
        (a * n_lon + b, (a + steps) % n_lat * n_lon + (b + steps) % n_lon)
        for a in range(n_lat)
        for b in range(n_lon)
    ]
    return lax.ppermute(value, (*LAT, "lon"), pairs)


def move_one(inputs, cotangent):
    def cut(rows, cols):
        return jnp.concatenate([inputs[:, :, rows, cols], cotangent[:, :, rows, cols]], axis=0)

    head, last, body, side = slice(0, SLAT), slice(SLAT, None), slice(0, -SLON), slice(-SLON, None)
    corner = diagonal(cut(last, side), 1)
    upper = passed_along(cut(last, body), LAT, 1)
    left = passed_along(cut(head, side), "lon", 1)
    outs = []
    for at, own in enumerate((inputs, cotangent)):
        top = jnp.concatenate([corner[at:at + 1], upper[at:at + 1]], axis=3)
        bottom = jnp.concatenate([left[at:at + 1], own[:, :, head, body]], axis=3)
        outs.append(jnp.concatenate([top, bottom], axis=2))
    return outs


def move_back(both):
    head, last, side, body = slice(0, SLAT), slice(SLAT, None), slice(0, SLON), slice(SLON, None)
    corner = diagonal(both[:, :, head, side], -1)
    lower = passed_along(both[:, :, head, body], LAT, -1)
    right = passed_along(both[:, :, last, side], "lon", -1)
    top = jnp.concatenate([both[:, :, last, body], right], axis=3)
    bottom = jnp.concatenate([lower, corner], axis=3)
    return jnp.concatenate([top, bottom], axis=2)


def per_device(inputs, cotangent, mask_ids, w_qkv, w_proj):
    rolled, grad_in = move_one(inputs, cotangent)
    x = to_windows(rolled)
    u = to_windows(grad_in)
    first_band = lax.axis_index(LAT) == 0
    wrapped = jnp.logical_and(first_band, jnp.arange(WLAT) < SLAT).astype(jnp.int32)
    groups = mask_ids + 4 * wrapped[:, None]
    windows = groups.shape[1] // WLON
    labels = groups.reshape(WLAT, windows, WLON).transpose(1, 0, 2).reshape(windows, WLAT * WLON)
    lrow = jnp.tile(labels, (1, LEV))
    lcol = lrow.reshape(windows * WT, 1)
    send, gp, mix, nkeep, mkeep = attention(x, u, lrow, lcol, w_qkv, w_proj)
    got = passed_along(send, "core", 1)
    result, grad_total = call(
        token_kernel, "token_outputs", (x.shape, x.shape), (), 2_000_000_000,
        x, u, mix, gp, w_qkv, w_proj,
    )
    (sums,) = call(
        gradient_kernel, "gradient_sum", (send.shape,), (), 600_000_000,
        nkeep, mkeep, gp, u, got,
    )
    spread = lax.all_to_all(sums.reshape(64, 64, 128), ("yh", "x", "lon"), 0, 0, tiled=True)
    share = jnp.sum(spread.astype(jnp.float32), 0)
    share = share + passed_along(share, "dp", 1)
    share = share.reshape(16, 4, 128).transpose(1, 0, 2).reshape(4, 4 * D)
    back = move_back(jnp.concatenate([from_windows(result), from_windows(grad_total)], axis=0))
    return (back[:1], back[1:], share[:, :3 * D], share[:, 3 * D:])


def solution(mesh):
    mesh = Mesh(mesh.devices.reshape(2, 2, 4, 2, 8), ("dp", "yh", "x", "core", "lon"))
    tokens = P("dp", None, LAT, "lon", None)
    return jax.shard_map(
        per_device,
        mesh=mesh,
        in_specs=(tokens, tokens, P(LAT, "lon"), P(), P()),
        out_specs=(tokens, tokens, P((*LAT, "lon"), None), P((*LAT, "lon"), None)),
        check_vma=False,
    )
```

time: 852 us -> 81.1 us (0.10)
  blocking collectives: 688 us -> 0 us
  matrix products: 40.8 us -> 0 us
  waiting for transfers between devices: 68.1 us -> 30 us
  between operations: 15 us -> 0.88 us
  starting transfers between devices: 11.5 us -> 25.4 us
  Pallas kernels: 0 us -> 10.4 us
    unnamed x1 -> x0, blocking collectives: 688 us -> none
    psum x1 -> x0, waiting for transfers between devices: 60.5 us -> none  [per_device(): lax.psum(grad_qkv.astype(jnp.bfloat16), 'dp').astype(jnp.float32)]
    dot_general x11 -> x0, matrix products: 35.6 us -> none  [product(): return jnp.einsum(form, left, right, preferred_element_type=jnp.float32)]
    ppermute x8 -> x6, waiting for transfers between devices: 7.5 us -> 21.1 us  [passed_along(): return lax.ppermute(value, axis, pairs)]
    all_to_all x0 -> x1, starting transfers between devices: none -> 11.2 us  [per_device(): lax.all_to_all(sums.reshape(64, 64, 128), ('yh', 'x', 'lon'), 0, 0, tiled...]
    pallas_call x0 -> x3, Pallas kernels: none -> 10.4 us  [call(): pl.pallas_call(kernel, out_shape=tuple((jax.ShapeDtypeStruct(shape, jnp.b...]
  transfers between devices with their start and end apart: 9 -> 9, of which waited for: 5 -> 6; matrix products, arithmetic and copies ran while one was open for 2% -> 8% of each run, Pallas kernels for 0% -> 1%
where the time goes in v1:
time: 81.1 us; the launch traced here: 80.7 us
  waiting for transfers between devices  30 us (37%)
  starting transfers between devices  25.4 us (31%)
  local copies, waits for them, and re-layouts  10.6 us (13%)
  Pallas kernels  10.4 us (13%)
  other arithmetic  3.47 us (4%)
  between operations  0.88 us (1%)
    ppermute x6, waiting for transfers between devices, passed_along(): return lax.ppermute(value, axis, pairs)  21.1 us
    all_to_all x1, starting transfers between devices, per_device(): lax.all_to_all(sums.reshape(64, 64, 128), ('yh', 'x', 'lon'), 0, 0, tiled...  11.2 us
    pallas_call x3, Pallas kernels, call(): pl.pallas_call(kernel, out_shape=tuple((jax.ShapeDtypeStruct(shape, jnp.b...  10.4 us
    ppermute x6, starting transfers between devices, passed_along(): return lax.ppermute(value, axis, pairs)  10.2 us
    ppermute x2, waiting for transfers between devices, diagonal(): return lax.ppermute(value, (*LAT, 'lon'), pairs)  4.8 us
    unnamed x12, local copies, waits for them, and re-layouts  4.76 us
    all_to_all x1, waiting for transfers between devices, per_device(): lax.all_to_all(sums.reshape(64, 64, 128), ('yh', 'x', 'lon'), 0, 0, tiled...  4.14 us
    ppermute x2, starting transfers between devices, diagonal(): return lax.ppermute(value, (*LAT, 'lon'), pairs)  3.95 us
  transfers between devices with their start and end apart: 9, of which 6 were waited for; matrix products, arithmetic and copies ran while one was open for 8% of the time, Pallas kernels for 1%

profile of v1, /device:TPU:32, one launch (start us, length us, event | category | flops | bytes accessed | tf_op | source)
XLA Modules:
  0.0 80.7 jit_solution(463339579566983851)
XLA Ops:
  0.6 0.9 %fusion.6 = (bf16[1,2,3,6,512]{4,3,2,1,0:T(8,128)(2,1)S(1)}, bf16[1,2,3,6,512]{4,3,2,1,0:T(8,128)(2,1)S(1)}, bf16[1,2,3,6,512]{4,3,2,1,0:T(8,128)(2,1)S(1)}, bf16[1,2,3,6,512]{4,3,2,1,0:T(8,128)(2,1)S(1)}) fusion(bf16[1,2,6,24,512]{4,3,2,1,0:T(8,128)(2,1)} %param.5, bf16[1,2,6,24,512]{4,3,2,1,0:T(8,128)(2,1)} %param.6), kind=kLoop, calls=%fused_computation.23 | loop fusion | bytes 294912 | tf_op jit(solution)/shard_map/slice | solution.py:223
  1.6 2.0 %collective-permute-start.2 = (bf16[2,2,3,6,512]{4,3,2,1,0:T(8,128)(2,1)S(1)}, bf16[2,2,3,6,512]{4,3,2,1,0:T(8,128)(2,1)S(1)}, u32[]{:S(2)}, u32[]{:S(2)}) collective-permute-start(bf16[2,2,3,6,512]{4,3,2,1,0:T(8,128)(2,1)S(1)} %pad_maximum_fusion.2), channel_id=1, source_target_pairs={{0,1},{1,2},{2,3},{3,4},{4,5},{5,6},{6,7},{7,0},{8,9},{9,10},{10,1... | collective-permute-start | bytes 221192 | tf_op jit(solution)/shard_map/ppermute | solution.py:208
  3.6 1.2 %collective-permute-start = (bf16[2,2,3,6,512]{4,3,2,1,0:T(8,128)(2,1)S(1)}, bf16[2,2,3,6,512]{4,3,2,1,0:T(8,128)(2,1)S(1)}, u32[]{:S(2)}, u32[]{:S(2)}) collective-permute-start(bf16[2,2,3,6,512]{4,3,2,1,0:T(8,128)(2,1)S(1)} %pad_maximum_fusion.1), channel_id=1, source_target_pairs={{0,9},{1,10},{2,11},{3,12},{4,13},{5,14},{6,15},{7,8},{8,17},{9,18... | collective-permute-start | bytes 221192 | tf_op jit(solution)/shard_map/ppermute | solution.py:218
  4.8 1.2 %fusion.5 = (bf16[1,2,3,18,512]{4,3,2,1,0:T(8,128)(2,1)S(1)}, bf16[1,2,3,18,512]{4,3,2,1,0:T(8,128)(2,1)S(1)}, bf16[1,2,3,18,512]{4,3,2,1,0:T(8,128)(2,1)S(1)}, bf16[1,2,3,18,512]{4,3,2,1,0:T(8,128)(2,1)S(1)}) fusion(bf16[1,2,6,24,512]{4,3,2,1,0:T(8,128)(2,1)} %param.6, bf16[1,2,6,24,512]{4,3,2,1,0:T(8,128)(2,1)} %param.5), kind=kLoop, calls=%fused_computation.22 | loop fusion | bytes 884736 | tf_op jit(solution)/shard_map/slice | solution.py:232
  6.0 2.0 %collective-permute-start.1 = (bf16[2,2,3,18,512]{4,3,2,1,0:T(8,128)(2,1)S(1)}, bf16[2,2,3,18,512]{4,3,2,1,0:T(8,128)(2,1)S(1)}, u32[]{:S(2)}, u32[]{:S(2)}) collective-permute-start(bf16[2,2,3,18,512]{4,3,2,1,0:T(8,128)(2,1)S(1)} %pad_maximum_fusion), channel_id=1, source_target_pairs={{0,8},{8,16},{16,24},{24,32},{32,40},{40,48},{48,56},{56,64},{64,7... | collective-permute-start | bytes 663560 | tf_op jit(solution)/shard_map/ppermute | solution.py:208
  8.5 4.8 %collective-permute-done = bf16[2,2,3,6,512]{4,3,2,1,0:T(8,128)(2,1)S(1)} collective-permute-done((bf16[2,2,3,6,512]{4,3,2,1,0:T(8,128)(2,1)S(1)}, bf16[2,2,3,6,512]{4,3,2,1,0:T(8,128)(2,1)S(1)}, u32[]{:S(2)}, u32[]{:S(2)}) %collective-permute-start) | collective-permute-done | bytes 73760 | tf_op jit(solution)/shard_map/ppermute | solution.py:218
  13.3 3.0 %collective-permute-done.1 = bf16[2,2,3,18,512]{4,3,2,1,0:T(8,128)(2,1)S(1)} collective-permute-done((bf16[2,2,3,18,512]{4,3,2,1,0:T(8,128)(2,1)S(1)}, bf16[2,2,3,18,512]{4,3,2,1,0:T(8,128)(2,1)S(1)}, u32[]{:S(2)}, u32[]{:S(2)}) %collective-permute-start.1) | collective-permute-done | bytes 221216 | tf_op jit(solution)/shard_map/ppermute | solution.py:208
  17.4 0.8 %copy-done = bf16[512,1536]{1,0:T(8,128)(2,1)S(1)} copy-done((bf16[512,1536]{1,0:T(8,128)(2,1)S(1)}, bf16[512,1536]{1,0:T(8,128)(2,1)}, u32[]{:S(2)}) %copy-start) | copy-done | bytes 1572888
  18.2 1.0 %copy-done.2 = bf16[512,512]{1,0:T(8,128)(2,1)S(1)} copy-done((bf16[512,512]{1,0:T(8,128)(2,1)S(1)}, bf16[512,512]{1,0:T(8,128)(2,1)}, u32[]{:S(2)}) %copy-start.2) | copy-done | bytes 524312
  19.3 7.7 %window_attention.1 = (bf16[32,2,64,128]{3,2,1,0:T(8,128)(2,1)S(1)}, bf16[288,1536]{1,0:T(8,128)(2,1)S(1)}, bf16[288,512]{1,0:T(8,128)(2,1)S(1)}, bf16[256,288]{1,0:T(8,128)(2,1)S(1)}, bf16[256,288]{1,0:T(8,128)(2,1)S(1)}) custom-call(bf16[288,512]{1,0:T(8,128)(2,1)S(1)} %reshape.59.x_ref, bf16[288,512]{1,0:T(8,128)(2,1)S(1)} %reshape.61.u_ref, ...), custom_call_target="tpu_custom_call" | custom-call | flops 5000000000 | bytes 5046272 | tf_op jit(solution)/shard_map/window_attention/pallas_call | solution.py:155
  27.3 2.6 %collective-permute-done.6.got_ref = bf16[32,2,64,128]{3,2,1,0:T(8,128)(2,1)S(1)} collective-permute-done((bf16[32,2,64,128]{3,2,1,0:T(8,128)(2,1)S(1)}, bf16[32,2,64,128]{3,2,1,0:T(8,128)(2,1)S(1)}, u32[]{:S(2)}, u32[]{:S(2)}) %collective-permute-start.6) | collective-permute-done | bytes 1048608 | tf_op jit(solution)/shard_map/ppermute | solution.py:208
  29.9 1.8 %gradient_sum.1 = bf16[32,2,64,128]{3,2,1,0:T(8,128)(2,1)} custom-call(bf16[256,288]{1,0:T(8,128)(2,1)S(1)} %get-tuple-element.15.n_ref, bf16[256,288]{1,0:T(8,128)(2,1)S(1)} %get-tuple-element.16.m_ref, bf16[288,1536]{1,0:T(8,128)(2,1)S(1)} %get-tuple-element.12.gp_ref, bf16[288,512]{1,0:T(8,128)(2,1)S(1)} %reshape.61.u_ref, ...), custom_call_target="tpu_custom_call" | custom-call | flops 600000000 | bytes 2097152 | tf_op jit(solution)/shard_map/gradient_sum/pallas_call | solution.py:155
  31.7 11.2 %all-to-all-start = ((bf16[64,64,128]{2,1,0:T(8,128)(2,1)}), bf16[64,64,128]{2,1,0:T(8,128)(2,1)}, u32[]{:S(2)}, u32[]{:S(2)}) async-start(bf16[64,64,128]{2,1,0:T(8,128)(2,1)} %bitcast.9), calls=%async_computation | async-start | bytes 2097152 | tf_op jit(solution)/shard_map/all_to_all | solution.py:268
  42.9 1.4 %copy-done.1 = bf16[512,1536]{1,0:T(8,128)(2,1)S(1)} copy-done((bf16[512,1536]{1,0:T(8,128)(2,1)S(1)}, bf16[512,1536]{1,0:T(8,128)(2,1)}, u32[]{:S(2)}) %copy-start.1) | copy-done | bytes 1572888
  44.3 0.9 %token_outputs.1 = (bf16[288,512]{1,0:T(8,128)(2,1)S(1)}, bf16[288,512]{1,0:T(8,128)(2,1)S(1)}) custom-call(bf16[288,512]{1,0:T(8,128)(2,1)S(1)} %reshape.59.x_ref, bf16[288,512]{1,0:T(8,128)(2,1)S(1)} %reshape.61.u_ref, bf16[288,512]{1,0:T(8,128)(2,1)S(1)} %get-tuple-element.11.mix_ref, bf16[288,1536]{1,0:T(8,128)(2,1)S(1)} %get-tuple-element.12.gp_ref, ...), custom_call_target="tpu_custom_call" | custom-call | flops 2000000000 | bytes 1179648 | tf_op jit(solution)/shard_map/token_outputs/pallas_call | solution.py:155
  45.3 0.3 copy.19
  45.7 0.3 copy.20
  46.0 0.6 fusion.1
  46.7 4.6 %collective-permute-start.4 = (bf16[2,2,3,18,512]{4,1,3,2,0:T(2,128)(2,1)S(1)}, bf16[2,2,3,18,512]{4,1,3,2,0:T(2,128)(2,1)S(1)}, u32[]{:S(2)}, u32[]{:S(2)}) collective-permute-start(bf16[2,2,3,18,512]{4,1,3,2,0:T(2,128)(2,1)S(1)} %get-tuple-element.25), channel_id=1, source_target_pairs={{0,120},{8,0},{16,8},{24,16},{32,24},{40,32},{48,40},{56,48},{64,5... | collective-permute-start | bytes 663560 | tf_op jit(solution)/shard_map/ppermute | solution.py:208
  51.5 0.6 collective-permute-start.3
  52.1 2.8 %collective-permute-start.5 = (bf16[2,2,3,6,512]{4,1,3,2,0:T(2,128)(2,1)S(1)}, bf16[2,2,3,6,512]{4,1,3,2,0:T(2,128)(2,1)S(1)}, u32[]{:S(2)}, u32[]{:S(2)}) collective-permute-start(bf16[2,2,3,6,512]{4,1,3,2,0:T(2,128)(2,1)S(1)} %get-tuple-element.27), channel_id=1, source_target_pairs={{0,127},{1,120},{2,121},{3,122},{4,123},{5,124},{6,125},{7,126},{8... | collective-permute-start | bytes 221192 | tf_op jit(solution)/shard_map/ppermute | solution.py:218
  54.9 14.2 %collective-permute-done.3 = bf16[2,2,3,6,512]{4,1,3,2,0:T(2,128)(2,1)S(1)} collective-permute-done((bf16[2,2,3,6,512]{4,1,3,2,0:T(2,128)(2,1)S(1)}, bf16[2,2,3,6,512]{4,1,3,2,0:T(2,128)(2,1)S(1)}, u32[]{:S(2)}, u32[]{:S(2)}) %collective-permute-start.3) | collective-permute-done | bytes 73760 | tf_op jit(solution)/shard_map/ppermute | solution.py:208
  69.1 0.8 %maximum_maximum_fusion = bf16[2,2,6,24,512]{4,1,3,2,0:T(2,128)(2,1)S(1)} fusion(bf16[2,2,3,6,512]{4,1,3,2,0:T(2,128)(2,1)S(1)} %collective-permute-done.5, bf16[2,2,3,18,512]{4,1,3,2,0:T(2,128)(2,1)S(1)} %collective-permute-done.4, bf16[2,2,3,6,512]{4,1,3,2,0:T(2,128)(2,1)S(1)} %collective-permute-done.3, bf16[2,2,3,18,512]{4,1,3,2,0:T(2,128)(2,1)S(1)} %get-tuple-element.24), kind=kLoop, calls=%fused_computation.1 | loop fusion | flops 884736 | bytes 1179648 | tf_op jit(solution)/shard_map/concatenate | solution.py:244
  70.0 4.1 %all-to-all-done = bf16[64,64,128]{2,1,0:T(8,128)(2,1)} async-done(((bf16[64,64,128]{2,1,0:T(8,128)(2,1)}), bf16[64,64,128]{2,1,0:T(8,128)(2,1)}, u32[]{:S(2)}, u32[]{:S(2)}) %all-to-all-start) | async-done | bytes 1048608 | tf_op jit(solution)/shard_map/all_to_all | solution.py:268
  74.1 1.4 %convert_reduce_fusion = f32[64,128]{1,0:T(8,128)S(1)} fusion(bf16[64,64,128]{2,1,0:T(8,128)(2,1)} %all-to-all-done), kind=kLoop, calls=%fused_computation | loop fusion | flops 1040384 | bytes 1081344 | tf_op jit(solution)/shard_map/reduce_sum | solution.py:269
  75.5 0.8 collective-permute-start.7
  76.3 0.5 fusion.3
  76.8 0.7 copy.22
  77.5 0.7 copy.21
  78.2 1.2 %collective-permute-done.7 = f32[64,128]{1,0:T(8,128)S(1)} collective-permute-done((f32[64,128]{1,0:T(8,128)S(1)}, f32[64,128]{1,0:T(8,128)S(1)}, u32[]{:S(2)}, u32[]{:S(2)}) %collective-permute-start.7) | collective-permute-done | bytes 32800 | tf_op jit(solution)/shard_map/ppermute | solution.py:208
  79.5 0.6 slice.103
  80.1 0.6 slice.102
  (37 shorter events, 2.3 us)
Async XLA Ops:
  0.6 7.3 %copy-start.4 = (s32[6,24]{1,0:T(8,128)S(1)}, s32[6,24]{1,0:T(8,128)}, u32[]{:S(2)}) copy-start(s32[6,24]{1,0:T(8,128)} %param.7) | copy-start | bytes 1732
  1.6 6.8 %collective-permute-start.2 = (bf16[2,2,3,6,512]{4,3,2,1,0:T(8,128)(2,1)S(1)}, bf16[2,2,3,6,512]{4,3,2,1,0:T(8,128)(2,1)S(1)}, u32[]{:S(2)}, u32[]{:S(2)}) collective-permute-start(bf16[2,2,3,6,512]{4,3,2,1,0:T(8,128)(2,1)S(1)} %pad_maximum_fusion.2), channel_id=1, source_target_pairs={{0,1},{1,2},{2,3},{3,4},{4,5},{5,6},{6,7},{7,0},{8,9},{9,10},{10,1... | collective-permute-start | bytes 221192 | tf_op jit(solution)/shard_map/ppermute | solution.py:208
  3.6 9.6 %collective-permute-start = (bf16[2,2,3,6,512]{4,3,2,1,0:T(8,128)(2,1)S(1)}, bf16[2,2,3,6,512]{4,3,2,1,0:T(8,128)(2,1)S(1)}, u32[]{:S(2)}, u32[]{:S(2)}) collective-permute-start(bf16[2,2,3,6,512]{4,3,2,1,0:T(8,128)(2,1)S(1)} %pad_maximum_fusion.1), channel_id=1, source_target_pairs={{0,9},{1,10},{2,11},{3,12},{4,13},{5,14},{6,15},{7,8},{8,17},{9,18... | collective-permute-start | bytes 221192 | tf_op jit(solution)/shard_map/ppermute | solution.py:218
  6.0 10.3 %collective-permute-start.1 = (bf16[2,2,3,18,512]{4,3,2,1,0:T(8,128)(2,1)S(1)}, bf16[2,2,3,18,512]{4,3,2,1,0:T(8,128)(2,1)S(1)}, u32[]{:S(2)}, u32[]{:S(2)}) collective-permute-start(bf16[2,2,3,18,512]{4,3,2,1,0:T(8,128)(2,1)S(1)} %pad_maximum_fusion), channel_id=1, source_target_pairs={{0,8},{8,16},{16,24},{24,32},{32,40},{40,48},{48,56},{56,64},{64,7... | collective-permute-start | bytes 663560 | tf_op jit(solution)/shard_map/ppermute | solution.py:208
  16.8 1.4 %copy-start = (bf16[512,1536]{1,0:T(8,128)(2,1)S(1)}, bf16[512,1536]{1,0:T(8,128)(2,1)}, u32[]{:S(2)}) copy-start(bf16[512,1536]{1,0:T(8,128)(2,1)} %wqkv_ref.3) | copy-start | bytes 4718596
  18.2 1.0 %copy-start.2 = (bf16[512,512]{1,0:T(8,128)(2,1)S(1)}, bf16[512,512]{1,0:T(8,128)(2,1)}, u32[]{:S(2)}) copy-start(bf16[512,512]{1,0:T(8,128)(2,1)} %wproj_ref.3) | copy-start | bytes 1572868
  27.0 2.9 %collective-permute-start.6 = (bf16[32,2,64,128]{3,2,1,0:T(8,128)(2,1)S(1)}, bf16[32,2,64,128]{3,2,1,0:T(8,128)(2,1)S(1)}, u32[]{:S(2)}, u32[]{:S(2)}) collective-permute-start(bf16[32,2,64,128]{3,2,1,0:T(8,128)(2,1)S(1)} %get-tuple-element.17), channel_id=1, source_target_pairs={{0,8},{8,0},{1,9},{9,1},{2,10},{10,2},{3,11},{11,3},{4,12},{12,4},... | collective-permute-start | bytes 3145736 | tf_op jit(solution)/shard_map/ppermute | solution.py:208
  31.7 11.2 %copy-start.3 = (bf16[512,512]{1,0:T(8,128)(2,1)S(1)}, bf16[512,512]{1,0:T(8,128)(2,1)}, u32[]{:S(2)}) copy-start(bf16[512,512]{1,0:T(8,128)(2,1)} %wproj_ref.3) | copy-start | bytes 1572868
  31.7 42.4 %all-to-all-start = ((bf16[64,64,128]{2,1,0:T(8,128)(2,1)}), bf16[64,64,128]{2,1,0:T(8,128)(2,1)}, u32[]{:S(2)}, u32[]{:S(2)}) async-start(bf16[64,64,128]{2,1,0:T(8,128)(2,1)} %bitcast.9), calls=%async_computation | async-start | bytes 2097152 | tf_op jit(solution)/shard_map/all_to_all | solution.py:268
  42.9 1.4 %copy-start.1 = (bf16[512,1536]{1,0:T(8,128)(2,1)S(1)}, bf16[512,1536]{1,0:T(8,128)(2,1)}, u32[]{:S(2)}) copy-start(bf16[512,1536]{1,0:T(8,128)(2,1)} %wqkv_ref.3) | copy-start | bytes 4718596
  46.7 22.4 %collective-permute-start.4 = (bf16[2,2,3,18,512]{4,1,3,2,0:T(2,128)(2,1)S(1)}, bf16[2,2,3,18,512]{4,1,3,2,0:T(2,128)(2,1)S(1)}, u32[]{:S(2)}, u32[]{:S(2)}) collective-permute-start(bf16[2,2,3,18,512]{4,1,3,2,0:T(2,128)(2,1)S(1)} %get-tuple-element.25), channel_id=1, source_target_pairs={{0,120},{8,0},{16,8},{24,16},{32,24},{40,32},{48,40},{56,48},{64,5... | collective-permute-start | bytes 663560 | tf_op jit(solution)/shard_map/ppermute | solution.py:208
  51.5 17.6 %collective-permute-start.3 = (bf16[2,2,3,6,512]{4,1,3,2,0:T(2,128)(2,1)S(1)}, bf16[2,2,3,6,512]{4,1,3,2,0:T(2,128)(2,1)S(1)}, u32[]{:S(2)}, u32[]{:S(2)}) collective-permute-start(bf16[2,2,3,6,512]{4,1,3,2,0:T(2,128)(2,1)S(1)} %get-tuple-element.26), channel_id=1, source_target_pairs={{0,7},{1,0},{2,1},{3,2},{4,3},{5,4},{6,5},{7,6},{8,15},{9,8},{10,9... | collective-permute-start | bytes 221192 | tf_op jit(solution)/shard_map/ppermute | solution.py:208
  52.1 17.0 %collective-permute-start.5 = (bf16[2,2,3,6,512]{4,1,3,2,0:T(2,128)(2,1)S(1)}, bf16[2,2,3,6,512]{4,1,3,2,0:T(2,128)(2,1)S(1)}, u32[]{:S(2)}, u32[]{:S(2)}) collective-permute-start(bf16[2,2,3,6,512]{4,1,3,2,0:T(2,128)(2,1)S(1)} %get-tuple-element.27), channel_id=1, source_target_pairs={{0,127},{1,120},{2,121},{3,122},{4,123},{5,124},{6,125},{7,126},{8... | collective-permute-start | bytes 221192 | tf_op jit(solution)/shard_map/ppermute | solution.py:218
  75.5 4.0 %collective-permute-start.7 = (f32[64,128]{1,0:T(8,128)S(1)}, f32[64,128]{1,0:T(8,128)S(1)}, u32[]{:S(2)}, u32[]{:S(2)}) collective-permute-start(f32[64,128]{1,0:T(8,128)S(1)} %convert_reduce_fusion), channel_id=1, source_target_pairs={{0,128},{128,0},{1,129},{129,1},{2,130},{130,2},{3,131},{131,3},{4... | collective-permute-start | bytes 98312 | tf_op jit(solution)/shard_map/ppermute | solution.py:208

commit v2 on v1

--- a/solution.py
+++ b/solution.py
@@ -40,7 +40,7 @@
     return shifted * inverse, inverse
 
 
-def store_shares(target_ref, grads, added_ref=None):
+def store_shares(target_ref, grads):
     count = grads.shape[0]
     first = lax.broadcasted_iota(jnp.int32, (count, 128), 0) % 8 < 4
     for quad in range(4):
@@ -53,9 +53,7 @@
         rows = slice(quad * 16, quad * 16 + 16)
         for which in range(2):
             piece = jnp.concatenate([p.reshape(count // 8, 8, 128) for p in shares[which]], axis=1)
-            if added_ref is not None:
-                piece = piece + added_ref[:, which, rows, :].astype(jnp.float32)
-            target_ref[:, which, rows, :] = piece.astype(jnp.bfloat16)
+            target_ref[:, which, rows, :] = piece.astype(target_ref.dtype)
 
 
 def attention_kernel(
@@ -132,9 +130,57 @@
     store_shares(send_ref, grads)
 
 
-def gradient_kernel(n_ref, m_ref, gp_ref, u_ref, got_ref, sum_ref):
+def own_half_kernel(n_ref, m_ref, gp_ref, u_ref, own_ref):
     grads = jnp.concatenate([dot(n_ref[...], gp_ref[...]), dot(m_ref[...], u_ref[...])], axis=1)
-    store_shares(sum_ref, grads, got_ref)
+    store_shares(own_ref, grads)
+
+
+def add_kernel(own_ref, got_ref, sum_ref):
+    sum_ref[...] = (own_ref[...] + got_ref[...].astype(jnp.float32)).astype(jnp.bfloat16)
+
+
+def sum_kernel(parts_ref, sum_ref):
+    total = parts_ref[0].astype(jnp.float32)
+    for part in range(1, parts_ref.shape[0]):
+        total = total + parts_ref[part].astype(jnp.float32)
+    sum_ref[...] = total.astype(sum_ref.dtype)
+
+
+def last_kernel(share_ref, other_ref, qkv_ref, proj_ref):
+    total = share_ref[...] + other_ref[...]
+    for tile in range(16):
+        piece = total[tile * 4:tile * 4 + 4, :]
+        if tile < 12:
+            qkv_ref[:, tile * 128:(tile + 1) * 128] = piece
+        else:
+            proj_ref[:, (tile - 12) * 128:(tile - 11) * 128] = piece
+
+
+def stage_kernel(qkv_ref, proj_ref, qkv_out, proj_out, sems):
+    copies = [
+        pltpu.make_async_copy(qkv_ref, qkv_out, sems.at[0]),
+        pltpu.make_async_copy(proj_ref, proj_out, sems.at[1]),
+    ]
+    for copy in copies:
+        copy.start()
+    for copy in copies:
+        copy.wait()
+
+
+def staged(w_qkv, w_proj):
+    return pl.pallas_call(
+        stage_kernel,
+        out_shape=(
+            pltpu.VMEM(w_qkv.shape, w_qkv.dtype),
+            pltpu.VMEM(w_proj.shape, w_proj.dtype),
+        ),
+        in_specs=[pl.BlockSpec(memory_space=pl.ANY)] * 2,
+        out_specs=(pl.BlockSpec(memory_space=pltpu.VMEM),) * 2,
+        scratch_shapes=[pltpu.SemaphoreType.DMA((2,))],
+        compiler_params=pltpu.CompilerParams(vmem_limit_bytes=40 * 1024 * 1024),
+        cost_estimate=pl.CostEstimate(flops=0, bytes_accessed=4 * 1024 * 1024, transcendentals=0),
+        name="stage_weights",
+    )(w_qkv, w_proj)
 
 
 def token_kernel(x_ref, u_ref, mix_ref, gp_ref, wqkv_ref, wproj_ref, out_ref, gin_ref):
@@ -149,15 +195,15 @@
     gin_ref[...] = (u_ref[...].astype(jnp.float32) + grad_tokens).astype(jnp.bfloat16)
 
 
-def call(kernel, name, outs, scratch, flops, *args):
+def call(kernel, name, outs, scratch, flops, *args, dtype=jnp.bfloat16):
     vmem = pl.BlockSpec(memory_space=pltpu.VMEM)
     size = sum(2 * math.prod(shape) for shape in outs)
     return pl.pallas_call(
         kernel,
-        out_shape=tuple(jax.ShapeDtypeStruct(shape, jnp.bfloat16) for shape in outs),
+        out_shape=tuple(jax.ShapeDtypeStruct(shape, dtype) for shape in outs),
         in_specs=[vmem] * len(args),
         out_specs=(vmem,) * len(outs),
-        scratch_shapes=[pltpu.VMEM(shape, dtype) for shape, dtype in scratch],
+        scratch_shapes=[pltpu.VMEM(shape, kind) for shape, kind in scratch],
         compiler_params=pltpu.CompilerParams(vmem_limit_bytes=40 * 1024 * 1024),
         cost_estimate=pl.CostEstimate(flops=flops, bytes_accessed=2 * size, transcendentals=0),
         name=name,
@@ -255,22 +301,29 @@
     labels = groups.reshape(WLAT, windows, WLON).transpose(1, 0, 2).reshape(windows, WLAT * WLON)
     lrow = jnp.tile(labels, (1, LEV))
     lcol = lrow.reshape(windows * WT, 1)
+    w_qkv, w_proj = staged(w_qkv, w_proj)
     send, gp, mix, nkeep, mkeep = attention(x, u, lrow, lcol, w_qkv, w_proj)
     got = passed_along(send, "core", 1)
+    (own,) = call(
+        own_half_kernel, "own_half", (send.shape,), (), 600_000_000,
+        nkeep, mkeep, gp, u, dtype=jnp.float32,
+    )
+    (sums,) = call(add_kernel, "add_halves", (send.shape,), (), 1_000_000, own, got)
     result, grad_total = call(
         token_kernel, "token_outputs", (x.shape, x.shape), (), 2_000_000_000,
         x, u, mix, gp, w_qkv, w_proj,
     )
-    (sums,) = call(
-        gradient_kernel, "gradient_sum", (send.shape,), (), 600_000_000,
-        nkeep, mkeep, gp, u, got,
-    )
-    spread = lax.all_to_all(sums.reshape(64, 64, 128), ("yh", "x", "lon"), 0, 0, tiled=True)
+    result, grad_total, sums = lax.optimization_barrier((result, grad_total, sums))
+    spread = lax.all_to_all(sums.reshape(8, 512, 128), ("yh", "x"), 0, 0, tiled=True)
+    (sums,) = call(sum_kernel, "sum_parts", ((512, 128),), (), 1_000_000, spread)
+    spread = lax.all_to_all(sums.reshape(8, 64, 128), "lon", 0, 0, tiled=True)
     share = jnp.sum(spread.astype(jnp.float32), 0)
-    share = share + passed_along(share, "dp", 1)
-    share = share.reshape(16, 4, 128).transpose(1, 0, 2).reshape(4, 4 * D)
+    other = passed_along(share, "dp", 1)
+    grad_qkv, grad_proj = call(
+        last_kernel, "last_sum", ((4, 3 * D), (4, D)), (), 1000, share, other, dtype=jnp.float32
+    )
     back = move_back(jnp.concatenate([from_windows(result), from_windows(grad_total)], axis=0))
-    return (back[:1], back[1:], share[:, :3 * D], share[:, 3 * D:])
+    return (back[:1], back[1:], grad_qkv, grad_proj)
 
 
 def solution(mesh):

time: 81.1 us -> 77.2 us (0.952)
  the two profiles are of different devices: /device:TPU:32 before, /device:TPU:2 now
where the time goes in v2:
time: 77.2 us; the launch traced here: 76.8 us
  waiting for transfers between devices  25.7 us (33%)
  starting transfers between devices  25.5 us (33%)
  Pallas kernels  12.1 us (16%)
  local copies, waits for them, and re-layouts  8.49 us (11%)
  other arithmetic  4.07 us (5%)
  between operations  0.91 us (1%)
    pallas_call x6, Pallas kernels, call(): pl.pallas_call(kernel, out_shape=tuple((jax.ShapeDtypeStruct(shape, dtype...  12 us
    all_to_all x1, waiting for transfers between devices, per_device(): lax.all_to_all(sums.reshape(8, 512, 128), ('yh', 'x'), 0, 0, tiled=True)  11.9 us
    all_to_all x1, starting transfers between devices, per_device(): lax.all_to_all(sums.reshape(8, 512, 128), ('yh', 'x'), 0, 0, tiled=True)  8.35 us
    all_to_all x1, waiting for transfers between devices, per_device(): spread = lax.all_to_all(sums.reshape(8, 64, 128), 'lon', 0, 0, tiled=True)  8.2 us
    ppermute x6, starting transfers between devices, passed_along(): return lax.ppermute(value, axis, pairs)  7.73 us
    all_to_all x1, starting transfers between devices, per_device(): spread = lax.all_to_all(sums.reshape(8, 64, 128), 'lon', 0, 0, tiled=True)  7.09 us
    ppermute x6, waiting for transfers between devices, passed_along(): return lax.ppermute(value, axis, pairs)  5.11 us
    unnamed x12, local copies, waits for them, and re-layouts  2.91 us
  transfers between devices with their start and end apart: 10, of which 7 were waited for; matrix products, arithmetic and copies ran while one was open for 11% of the time, Pallas kernels for 3%

profile of v2, /device:TPU:2, one launch (start us, length us, event | category | flops | bytes accessed | tf_op | source)
XLA Modules:
  0.0 76.8 jit_solution(17200388224314930052)
XLA Ops:
  0.7 1.1 %fusion.6 = (bf16[1,2,3,6,512]{4,3,2,1,0:T(8,128)(2,1)S(1)}, bf16[1,2,3,6,512]{4,3,2,1,0:T(8,128)(2,1)S(1)}, bf16[1,2,3,6,512]{4,3,2,1,0:T(8,128)(2,1)S(1)}, bf16[1,2,3,6,512]{4,3,2,1,0:T(8,128)(2,1)S(1)}) fusion(bf16[1,2,6,24,512]{4,3,2,1,0:T(8,128)(2,1)} %param.5, bf16[1,2,6,24,512]{4,3,2,1,0:T(8,128)(2,1)} %param.6), kind=kLoop, calls=%fused_computation.23 | loop fusion | bytes 294912 | tf_op jit(solution)/shard_map/slice | solution.py:269
  1.7 0.7 pad_maximum_fusion.2
  2.4 1.9 %collective-permute-start.2 = (bf16[2,2,3,6,512]{4,3,2,1,0:T(8,128)(2,1)}, bf16[2,2,3,6,512]{4,3,2,1,0:T(8,128)(2,1)S(1)}, u32[]{:S(2)}, u32[]{:S(2)}) collective-permute-start(bf16[2,2,3,6,512]{4,3,2,1,0:T(8,128)(2,1)} %pad_maximum_fusion.2), channel_id=1, source_target_pairs={{0,1},{1,2},{2,3},{3,4},{4,5},{5,6},{6,7},{7,0},{8,9},{9,10},{10,1... | collective-permute-start | bytes 221192 | tf_op jit(solution)/shard_map/ppermute | solution.py:254
  4.3 0.7 pad_maximum_fusion.1
  5.0 1.1 %collective-permute-start = (bf16[2,2,3,6,512]{4,3,2,1,0:T(8,128)(2,1)}, bf16[2,2,3,6,512]{4,3,2,1,0:T(8,128)(2,1)}, u32[]{:S(2)}, u32[]{:S(2)}) collective-permute-start(bf16[2,2,3,6,512]{4,3,2,1,0:T(8,128)(2,1)} %pad_maximum_fusion.1), channel_id=1, source_target_pairs={{0,9},{1,10},{2,11},{3,12},{4,13},{5,14},{6,15},{7,8},{8,17},{9,18... | collective-permute-start | bytes 221192 | tf_op jit(solution)/shard_map/ppermute | solution.py:264
  6.1 1.2 %fusion.5 = (bf16[1,2,3,18,512]{4,3,2,1,0:T(8,128)(2,1)S(1)}, bf16[1,2,3,18,512]{4,3,2,1,0:T(8,128)(2,1)S(1)}, bf16[1,2,3,18,512]{4,3,2,1,0:T(8,128)(2,1)S(1)}, bf16[1,2,3,18,512]{4,3,2,1,0:T(8,128)(2,1)S(1)}) fusion(bf16[1,2,6,24,512]{4,3,2,1,0:T(8,128)(2,1)} %param.6, bf16[1,2,6,24,512]{4,3,2,1,0:T(8,128)(2,1)} %param.5), kind=kLoop, calls=%fused_computation.22 | loop fusion | bytes 884736 | tf_op jit(solution)/shard_map/slice | solution.py:278
  7.2 0.7 pad_maximum_fusion
  8.0 1.9 %collective-permute-start.1 = (bf16[2,2,3,18,512]{4,3,2,1,0:T(8,128)(2,1)}, bf16[2,2,3,18,512]{4,3,2,1,0:T(8,128)(2,1)S(1)}, u32[]{:S(2)}, u32[]{:S(2)}) collective-permute-start(bf16[2,2,3,18,512]{4,3,2,1,0:T(8,128)(2,1)} %pad_maximum_fusion), channel_id=1, source_target_pairs={{0,8},{8,16},{16,24},{24,32},{32,40},{40,48},{48,56},{56,64},{64,7... | collective-permute-start | bytes 663560 | tf_op jit(solution)/shard_map/ppermute | solution.py:254
  10.5 1.5 %collective-permute-done.2 = bf16[2,2,3,6,512]{4,3,2,1,0:T(8,128)(2,1)S(1)} collective-permute-done((bf16[2,2,3,6,512]{4,3,2,1,0:T(8,128)(2,1)}, bf16[2,2,3,6,512]{4,3,2,1,0:T(8,128)(2,1)S(1)}, u32[]{:S(2)}, u32[]{:S(2)}) %collective-permute-start.2) | collective-permute-done | bytes 73760 | tf_op jit(solution)/shard_map/ppermute | solution.py:254
  12.1 0.5 collective-permute-done
  12.6 0.8 %fusion.9 = (bf16[1,2,3,6,512]{4,3,2,1,0:T(8,128)(2,1)S(1)}, bf16[1,2,3,6,512]{4,3,2,1,0:T(8,128)(2,1)S(1)}) fusion(bf16[2,2,3,6,512]{4,3,2,1,0:T(8,128)(2,1)} %collective-permute-done), kind=kLoop, calls=%fused_computation.26 | loop fusion | bytes 147456 | tf_op jit(solution)/shard_map/slice | solution.py:277
  13.4 1.7 %collective-permute-done.1 = bf16[2,2,3,18,512]{4,3,2,1,0:T(8,128)(2,1)S(1)} collective-permute-done((bf16[2,2,3,18,512]{4,3,2,1,0:T(8,128)(2,1)}, bf16[2,2,3,18,512]{4,3,2,1,0:T(8,128)(2,1)S(1)}, u32[]{:S(2)}, u32[]{:S(2)}) %collective-permute-start.1) | collective-permute-done | bytes 221216 | tf_op jit(solution)/shard_map/ppermute | solution.py:254
  16.3 1.4 %copy-done.3 = bf16[512,1536]{1,0:T(8,128)(2,1)S(1)} copy-done((bf16[512,1536]{1,0:T(8,128)(2,1)S(1)}, bf16[512,1536]{1,0:T(8,128)(2,1)}, u32[]{:S(2)}) %copy-start.3) | copy-done | bytes 1572888
  17.7 7.7 %window_attention.1 = (bf16[32,2,64,128]{3,2,1,0:T(8,128)(2,1)S(1)}, bf16[288,1536]{1,0:T(8,128)(2,1)S(1)}, bf16[288,512]{1,0:T(8,128)(2,1)S(1)}, bf16[256,288]{1,0:T(8,128)(2,1)S(1)}, bf16[256,288]{1,0:T(8,128)(2,1)S(1)}) custom-call(bf16[288,512]{1,0:T(8,128)(2,1)S(1)} %reshape.56.x_ref, bf16[288,512]{1,0:T(8,128)(2,1)S(1)} %reshape.58.u_ref, ...), custom_call_target="tpu_custom_call" | custom-call | flops 5000000000 | bytes 5046272 | tf_op jit(solution)/shard_map/window_attention/pallas_call | solution.py:201
  25.7 0.7 own_half.1.own_ref
  26.4 0.9 %token_outputs.1 = (bf16[288,512]{1,0:T(8,128)(2,1)S(1)}, bf16[288,512]{1,0:T(8,128)(2,1)S(1)}) custom-call(bf16[288,512]{1,0:T(8,128)(2,1)S(1)} %reshape.56.x_ref, bf16[288,512]{1,0:T(8,128)(2,1)S(1)} %reshape.58.u_ref, bf16[288,512]{1,0:T(8,128)(2,1)S(1)} %get-tuple-element.20.mix_ref, bf16[288,1536]{1,0:T(8,128)(2,1)S(1)} %get-tuple-element.21.gp_ref, ...), custom_call_target="tpu_custom_call" | custom-call | flops 2000000000 | bytes 1179648 | tf_op jit(solution)/shard_map/token_outputs/pallas_call | solution.py:201
  27.4 1.0 %collective-permute-done.3.got_ref = bf16[32,2,64,128]{3,2,1,0:T(8,128)(2,1)S(1)} collective-permute-done((bf16[32,2,64,128]{3,2,1,0:T(8,128)(2,1)S(1)}, bf16[32,2,64,128]{3,2,1,0:T(8,128)(2,1)S(1)}, u32[]{:S(2)}, u32[]{:S(2)}) %collective-permute-start.3) | collective-permute-done | bytes 1048608 | tf_op jit(solution)/shard_map/ppermute | solution.py:254
  28.4 1.2 %add_halves.1 = bf16[32,2,64,128]{3,2,1,0:T(8,128)(2,1)} custom-call(f32[32,2,64,128]{3,2,1,0:T(8,128)S(1)} %own_half.1.own_ref, bf16[32,2,64,128]{3,2,1,0:T(8,128)(2,1)S(1)} %collective-permute-done.3.got_ref), custom_call_target="tpu_custom_call" | custom-call | flops 1000000 | bytes 2097152 | tf_op jit(solution)/shard_map/add_halves/pallas_call | solution.py:201
  29.6 8.4 %all-to-all-start = ((bf16[8,512,128]{2,1,0:T(8,128)(2,1)}), bf16[8,512,128]{2,1,0:T(8,128)(2,1)S(1)}, u32[]{:S(2)}, u32[]{:S(2)}) async-start(bf16[8,512,128]{2,1,0:T(8,128)(2,1)} %bitcast.9), calls=%async_computation | async-start | bytes 2097152 | tf_op jit(solution)/shard_map/all_to_all | solution.py:317
  38.7 0.6 fusion.1
  39.6 2.4 %collective-permute-start.4 = (bf16[2,2,3,6,512]{4,1,3,2,0:T(2,128)(2,1)S(1)}, bf16[2,2,3,6,512]{4,1,3,2,0:T(2,128)(2,1)S(1)}, u32[]{:S(2)}, u32[]{:S(2)}) collective-permute-start(bf16[2,2,3,6,512]{4,1,3,2,0:T(2,128)(2,1)S(1)} %get-tuple-element.40), channel_id=1, source_target_pairs={{0,7},{1,0},{2,1},{3,2},{4,3},{5,4},{6,5},{7,6},{8,15},{9,8},{10,9... | collective-permute-start | bytes 221192 | tf_op jit(solution)/shard_map/ppermute | solution.py:254
  42.1 1.3 %collective-permute-start.6 = (bf16[2,2,3,6,512]{4,1,3,2,0:T(2,128)(2,1)S(1)}, bf16[2,2,3,6,512]{4,1,3,2,0:T(2,128)(2,1)S(1)}, u32[]{:S(2)}, u32[]{:S(2)}) collective-permute-start(bf16[2,2,3,6,512]{4,1,3,2,0:T(2,128)(2,1)S(1)} %get-tuple-element.41), channel_id=1, source_target_pairs={{0,127},{1,120},{2,121},{3,122},{4,123},{5,124},{6,125},{7,126},{8... | collective-permute-start | bytes 221192 | tf_op jit(solution)/shard_map/ppermute | solution.py:264
  43.3 11.9 %all-to-all-done.parts_ref = bf16[8,512,128]{2,1,0:T(8,128)(2,1)S(1)} async-done(((bf16[8,512,128]{2,1,0:T(8,128)(2,1)}), bf16[8,512,128]{2,1,0:T(8,128)(2,1)S(1)}, u32[]{:S(2)}, u32[]{:S(2)}) %all-to-all-start) | async-done | bytes 1048608 | tf_op jit(solution)/shard_map/all_to_all | solution.py:317
  55.2 0.8 %sum_parts.1 = bf16[512,128]{1,0:T(8,128)(2,1)} custom-call(bf16[8,512,128]{2,1,0:T(8,128)(2,1)S(1)} %all-to-all-done.parts_ref), custom_call_target="tpu_custom_call" | custom-call | flops 1000000 | bytes 262144 | tf_op jit(solution)/shard_map/sum_parts/pallas_call | solution.py:201
  56.0 7.1 %all-to-all-start.1 = ((bf16[8,64,128]{2,1,0:T(8,128)(2,1)}), bf16[8,64,128]{2,1,0:T(8,128)(2,1)S(1)}, u32[]{:S(2)}, u32[]{:S(2)}) async-start(bf16[8,64,128]{2,1,0:T(8,128)(2,1)} %bitcast.10), calls=%async_computation.1 | async-start | bytes 262144 | tf_op jit(solution)/shard_map/all_to_all | solution.py:319
  63.1 0.8 %maximum_maximum_fusion = bf16[2,2,6,24,512]{4,1,3,2,0:T(2,128)(2,1)S(1)} fusion(bf16[2,2,3,6,512]{4,1,3,2,0:T(2,128)(2,1)S(1)} %collective-permute-done.6, bf16[2,2,3,18,512]{4,1,3,2,0:T(2,128)(2,1)S(1)} %collective-permute-done.5, bf16[2,2,3,6,512]{4,1,3,2,0:T(2,128)(2,1)S(1)} %collective-permute-done.4, bf16[2,2,3,18,512]{4,1,3,2,0:T(2,128)(2,1)S(1)} %get-tuple-element.38), kind=kLoop, calls=%fused_computation | loop fusion | flops 884736 | bytes 1179648 | tf_op jit(solution)/shard_map/concatenate | solution.py:290
  64.0 8.2 %all-to-all-done.1 = bf16[8,64,128]{2,1,0:T(8,128)(2,1)S(1)} async-done(((bf16[8,64,128]{2,1,0:T(8,128)(2,1)}), bf16[8,64,128]{2,1,0:T(8,128)(2,1)S(1)}, u32[]{:S(2)}, u32[]{:S(2)}) %all-to-all-start.1) | async-done | bytes 131104 | tf_op jit(solution)/shard_map/all_to_all | solution.py:319
  72.2 1.1 %collective-permute-start.7 = (f32[64,128]{1,0:T(8,128)S(1)}, f32[64,128]{1,0:T(8,128)S(1)}, u32[]{:S(2)}, u32[]{:S(2)}) collective-permute-start(f32[64,128]{1,0:T(8,128)S(1)} %convert_reduce_fusion.share_ref), channel_id=1, source_target_pairs={{0,128},{128,0},{1,129},{129,1},{2,130},{130,2},{3,131},{131,3},{4... | collective-permute-start | bytes 98312 | tf_op jit(solution)/shard_map/ppermute | solution.py:254
  73.8 0.7 copy.22
  74.6 0.7 copy.21
  75.3 0.9 %collective-permute-done.7.other_ref = f32[64,128]{1,0:T(8,128)S(1)} collective-permute-done((f32[64,128]{1,0:T(8,128)S(1)}, f32[64,128]{1,0:T(8,128)S(1)}, u32[]{:S(2)}, u32[]{:S(2)}) %collective-permute-start.7) | collective-permute-done | bytes 32800 | tf_op jit(solution)/shard_map/ppermute | solution.py:254
  76.2 0.6 last_sum.1
  (40 shorter events, 3.6 us)
Async XLA Ops:
  0.6 9.2 %copy-start.4 = (s32[6,24]{1,0:T(8,128)S(1)}, s32[6,24]{1,0:T(8,128)}, u32[]{:S(2)}) copy-start(s32[6,24]{1,0:T(8,128)} %param.7) | copy-start | bytes 1732
  0.6 9.7 %copy-start.1 = (bf16[512,512]{1,0:T(8,128)(2,1)S(1)}, bf16[512,512]{1,0:T(8,128)(2,1)}, u32[]{:S(2)}) copy-start(bf16[512,512]{1,0:T(8,128)(2,1)} %proj_ref.1) | copy-start | bytes 1572868
  0.7 9.7 %copy-start = (bf16[512,1536]{1,0:T(8,128)(2,1)S(1)}, bf16[512,1536]{1,0:T(8,128)(2,1)}, u32[]{:S(2)}) copy-start(bf16[512,1536]{1,0:T(8,128)(2,1)} %qkv_ref.1) | copy-start | bytes 4718596
  2.4 9.7 %collective-permute-start.2 = (bf16[2,2,3,6,512]{4,3,2,1,0:T(8,128)(2,1)}, bf16[2,2,3,6,512]{4,3,2,1,0:T(8,128)(2,1)S(1)}, u32[]{:S(2)}, u32[]{:S(2)}) collective-permute-start(bf16[2,2,3,6,512]{4,3,2,1,0:T(8,128)(2,1)} %pad_maximum_fusion.2), channel_id=1, source_target_pairs={{0,1},{1,2},{2,3},{3,4},{4,5},{5,6},{6,7},{7,0},{8,9},{9,10},{10,1... | collective-permute-start | bytes 221192 | tf_op jit(solution)/shard_map/ppermute | solution.py:254
  5.0 7.6 %collective-permute-start = (bf16[2,2,3,6,512]{4,3,2,1,0:T(8,128)(2,1)}, bf16[2,2,3,6,512]{4,3,2,1,0:T(8,128)(2,1)}, u32[]{:S(2)}, u32[]{:S(2)}) collective-permute-start(bf16[2,2,3,6,512]{4,3,2,1,0:T(8,128)(2,1)} %pad_maximum_fusion.1), channel_id=1, source_target_pairs={{0,9},{1,10},{2,11},{3,12},{4,13},{5,14},{6,15},{7,8},{8,17},{9,18... | collective-permute-start | bytes 221192 | tf_op jit(solution)/shard_map/ppermute | solution.py:264
  8.0 7.2 %collective-permute-start.1 = (bf16[2,2,3,18,512]{4,3,2,1,0:T(8,128)(2,1)}, bf16[2,2,3,18,512]{4,3,2,1,0:T(8,128)(2,1)S(1)}, u32[]{:S(2)}, u32[]{:S(2)}) collective-permute-start(bf16[2,2,3,18,512]{4,3,2,1,0:T(8,128)(2,1)} %pad_maximum_fusion), channel_id=1, source_target_pairs={{0,8},{8,16},{16,24},{24,32},{32,40},{40,48},{48,56},{56,64},{64,7... | collective-permute-start | bytes 663560 | tf_op jit(solution)/shard_map/ppermute | solution.py:254
  10.5 5.5 %copy-start.2 = (bf16[512,1536]{1,0:T(8,128)(2,1)}, bf16[512,1536]{1,0:T(8,128)(2,1)S(1)}, u32[]{:S(2)}) copy-start(bf16[512,1536]{1,0:T(8,128)(2,1)S(1)} %get-tuple-element.18.wqkv_ref) | copy-start | bytes 4718596
  16.3 1.4 %copy-start.3 = (bf16[512,1536]{1,0:T(8,128)(2,1)S(1)}, bf16[512,1536]{1,0:T(8,128)(2,1)}, u32[]{:S(2)}) copy-start(bf16[512,1536]{1,0:T(8,128)(2,1)} %copy-done.2) | copy-start | bytes 4718596
  25.4 2.9 %collective-permute-start.3 = (bf16[32,2,64,128]{3,2,1,0:T(8,128)(2,1)S(1)}, bf16[32,2,64,128]{3,2,1,0:T(8,128)(2,1)S(1)}, u32[]{:S(2)}, u32[]{:S(2)}) collective-permute-start(bf16[32,2,64,128]{3,2,1,0:T(8,128)(2,1)S(1)} %get-tuple-element.26), channel_id=1, source_target_pairs={{0,8},{8,0},{1,9},{9,1},{2,10},{10,2},{3,11},{11,3},{4,12},{12,4},... | collective-permute-start | bytes 3145736 | tf_op jit(solution)/shard_map/ppermute | solution.py:254
  29.6 25.6 %all-to-all-start = ((bf16[8,512,128]{2,1,0:T(8,128)(2,1)}), bf16[8,512,128]{2,1,0:T(8,128)(2,1)S(1)}, u32[]{:S(2)}, u32[]{:S(2)}) async-start(bf16[8,512,128]{2,1,0:T(8,128)(2,1)} %bitcast.9), calls=%async_computation | async-start | bytes 2097152 | tf_op jit(solution)/shard_map/all_to_all | solution.py:317
  39.3 23.8 %collective-permute-start.5 = (bf16[2,2,3,18,512]{4,1,3,2,0:T(2,128)(2,1)S(1)}, bf16[2,2,3,18,512]{4,1,3,2,0:T(2,128)(2,1)S(1)}, u32[]{:S(2)}, u32[]{:S(2)}) collective-permute-start(bf16[2,2,3,18,512]{4,1,3,2,0:T(2,128)(2,1)S(1)} %get-tuple-element.39), channel_id=1, source_target_pairs={{0,120},{8,0},{16,8},{24,16},{32,24},{40,32},{48,40},{56,48},{64,5... | collective-permute-start | bytes 663560 | tf_op jit(solution)/shard_map/ppermute | solution.py:254
  39.6 23.4 %collective-permute-start.4 = (bf16[2,2,3,6,512]{4,1,3,2,0:T(2,128)(2,1)S(1)}, bf16[2,2,3,6,512]{4,1,3,2,0:T(2,128)(2,1)S(1)}, u32[]{:S(2)}, u32[]{:S(2)}) collective-permute-start(bf16[2,2,3,6,512]{4,1,3,2,0:T(2,128)(2,1)S(1)} %get-tuple-element.40), channel_id=1, source_target_pairs={{0,7},{1,0},{2,1},{3,2},{4,3},{5,4},{6,5},{7,6},{8,15},{9,8},{10,9... | collective-permute-start | bytes 221192 | tf_op jit(solution)/shard_map/ppermute | solution.py:254
  42.1 21.0 %collective-permute-start.6 = (bf16[2,2,3,6,512]{4,1,3,2,0:T(2,128)(2,1)S(1)}, bf16[2,2,3,6,512]{4,1,3,2,0:T(2,128)(2,1)S(1)}, u32[]{:S(2)}, u32[]{:S(2)}) collective-permute-start(bf16[2,2,3,6,512]{4,1,3,2,0:T(2,128)(2,1)S(1)} %get-tuple-element.41), channel_id=1, source_target_pairs={{0,127},{1,120},{2,121},{3,122},{4,123},{5,124},{6,125},{7,126},{8... | collective-permute-start | bytes 221192 | tf_op jit(solution)/shard_map/ppermute | solution.py:264
  56.0 16.2 %all-to-all-start.1 = ((bf16[8,64,128]{2,1,0:T(8,128)(2,1)}), bf16[8,64,128]{2,1,0:T(8,128)(2,1)S(1)}, u32[]{:S(2)}, u32[]{:S(2)}) async-start(bf16[8,64,128]{2,1,0:T(8,128)(2,1)} %bitcast.10), calls=%async_computation.1 | async-start | bytes 262144 | tf_op jit(solution)/shard_map/all_to_all | solution.py:319
  72.2 4.0 %collective-permute-start.7 = (f32[64,128]{1,0:T(8,128)S(1)}, f32[64,128]{1,0:T(8,128)S(1)}, u32[]{:S(2)}, u32[]{:S(2)}) collective-permute-start(f32[64,128]{1,0:T(8,128)S(1)} %convert_reduce_fusion.share_ref), channel_id=1, source_target_pairs={{0,128},{128,0},{1,129},{129,1},{2,130},{130,2},{3,131},{131,3},{4... | collective-permute-start | bytes 98312 | tf_op jit(solution)/shard_map/ppermute | solution.py:254

commit v3 on v2

--- a/solution.py
+++ b/solution.py
@@ -32,8 +32,56 @@
     return lax.dot_general(left, right, dims, preferred_element_type=jnp.float32)
 
 
-def statistics(x_ref):
-    x = x_ref[...].astype(jnp.float32)
+def cut_kernel(x_ref, u_ref, upper_ref, corner_ref, left_ref, held_ref, sems):
+    copies = []
+    for at, ref in enumerate((x_ref, u_ref)):
+        for level in range(LEV):
+            copies.append(pltpu.make_async_copy(ref.at[0, level], held_ref.at[at, level], sems.at[at, level]))
+    for copy in copies:
+        copy.start()
+    for copy in copies:
+        copy.wait()
+    for at in range(2):
+        for level in range(LEV):
+            for row in range(WLAT):
+                tokens = held_ref[at, level, row].astype(jnp.float32)
+                side = tokens[-SLON:].astype(jnp.bfloat16)
+                if row < SLAT:
+                    left_ref[at, level, row] = side
+                else:
+                    corner_ref[at, level, row - SLAT] = side
+                    upper_ref[at, level, row - SLAT] = tokens[:-SLON].astype(jnp.bfloat16)
+
+
+def join_kernel(own_ref, right_ref, lower_ref, corner_ref, out_ref, gin_ref):
+    for at, ref in enumerate((out_ref, gin_ref)):
+        for level in range(LEV):
+            for row in range(WLAT):
+                if row < SLAT:
+                    body, side = own_ref[at, level, row], right_ref[at, level, row]
+                else:
+                    body, side = lower_ref[at, level, row - SLAT], corner_ref[at, level, row - SLAT]
+                both = jnp.concatenate([body.astype(jnp.float32), side.astype(jnp.float32)], axis=0)
+                ref[0, level, row] = both.astype(jnp.bfloat16)
+
+
+def assemble(target_ref, at, own_ref, upper_ref, corner_ref, left_ref):
+    pieces = ([], [])
+    for level in range(LEV):
+        for row in range(WLAT):
+            if row < SLAT:
+                side, body = corner_ref[at, level, row], upper_ref[at, level, row]
+            else:
+                side, body = left_ref[at, level, row - SLAT], own_ref[0, level, row - SLAT]
+            side, body = side.astype(jnp.float32), body.astype(jnp.float32)
+            pieces[0].append(side)
+            pieces[0].append(body[:WLON - SLON])
+            pieces[1].append(body[WLON - SLON:2 * WLON - SLON])
+    for w in range(2):
+        target_ref[w * WT:(w + 1) * WT, :] = jnp.concatenate(pieces[w], axis=0)
+
+
+def statistics(x):
     center = jnp.mean(x, -1, keepdims=True)
     shifted = x - center
     inverse = lax.rsqrt(jnp.mean(shifted * shifted, -1, keepdims=True) + 1e-05)
@@ -57,14 +105,18 @@
 
 
 def attention_kernel(
-    x_ref, u_ref, lrow_ref, lcol_ref, wqkv_ref, wproj_ref,
-    send_ref, gp_ref, mix_ref, nkeep_ref, mkeep_ref,
-    proj_ref, gm_ref, nt_ref, mt_ref, mixt_ref, al_ref, gl_ref, s_ref, da_ref,
+    own_x_ref, own_u_ref, upper_ref, corner_ref, left_ref, lrow_ref, lcol_ref, wqkv_ref, wproj_ref,
+    send_ref, gp_ref, mix_ref, nkeep_ref, mkeep_ref, x_ref, u_ref,
+    full_ref, proj_ref, gm_ref, nt_ref, mt_ref, mixt_ref, al_ref, gl_ref, s_ref, da_ref,
 ):
     windows = x_ref.shape[0] // WT
     core = lax.axis_index("core")
     half = D // 2
-    normed, _ = statistics(x_ref)
+    assemble(full_ref, 1, own_u_ref, upper_ref, corner_ref, left_ref)
+    u_ref[...] = full_ref[...].astype(jnp.bfloat16)
+    assemble(full_ref, 0, own_x_ref, upper_ref, corner_ref, left_ref)
+    x_ref[...] = full_ref[...].astype(jnp.bfloat16)
+    normed, _ = statistics(full_ref[...])
     normed_low = normed.astype(jnp.bfloat16)
     proj_ref[...] = dot(normed_low, wqkv_ref[...]).astype(jnp.bfloat16)
     gm_ref[...] = dot(u_ref[...], wproj_ref[...], NT).astype(jnp.bfloat16)
@@ -130,11 +182,6 @@
     store_shares(send_ref, grads)
 
 
-def own_half_kernel(n_ref, m_ref, gp_ref, u_ref, own_ref):
-    grads = jnp.concatenate([dot(n_ref[...], gp_ref[...]), dot(m_ref[...], u_ref[...])], axis=1)
-    store_shares(own_ref, grads)
-
-
 def add_kernel(own_ref, got_ref, sum_ref):
     sum_ref[...] = (own_ref[...] + got_ref[...].astype(jnp.float32)).astype(jnp.bfloat16)
 
@@ -174,50 +221,92 @@
             pltpu.VMEM(w_qkv.shape, w_qkv.dtype),
             pltpu.VMEM(w_proj.shape, w_proj.dtype),
         ),
-        in_specs=[pl.BlockSpec(memory_space=pl.ANY)] * 2,
+        in_specs=[pl.BlockSpec(memory_space=pltpu.HBM)] * 2,
         out_specs=(pl.BlockSpec(memory_space=pltpu.VMEM),) * 2,
         scratch_shapes=[pltpu.SemaphoreType.DMA((2,))],
-        compiler_params=pltpu.CompilerParams(vmem_limit_bytes=40 * 1024 * 1024),
+        compiler_params=pltpu.CompilerParams(vmem_limit_bytes=4 * 1024 * 1024),
         cost_estimate=pl.CostEstimate(flops=0, bytes_accessed=4 * 1024 * 1024, transcendentals=0),
         name="stage_weights",
     )(w_qkv, w_proj)
 
 
-def token_kernel(x_ref, u_ref, mix_ref, gp_ref, wqkv_ref, wproj_ref, out_ref, gin_ref):
-    out_ref[...] = (x_ref[...].astype(jnp.float32) + dot(mix_ref[...], wproj_ref[...])).astype(jnp.bfloat16)
+def part(value, at, refs):
+    own_ref, left_ref, upper_ref, corner_ref = refs
+    for level in range(LEV):
+        for row in range(WLAT):
+            base = (level * WLAT + row) * WLON
+            tokens = jnp.concatenate([value[base:base + WLON], value[WT + base:WT + base + WLON]], axis=0)
+            side, body = tokens[:SLON].astype(jnp.bfloat16), tokens[SLON:].astype(jnp.bfloat16)
+            if row < SLAT:
+                corner_ref[at, level, row] = side
+                upper_ref[at, level, row] = body
+            else:
+                left_ref[at, level, row - SLAT] = side
+                own_ref[at, level, row - SLAT] = body
+
+
+def rest_kernel(
+    n_ref, m_ref, gp_ref, u_ref, x_ref, mix_ref, qkv_ref, proj_ref,
+    half_ref, own_ref, left_ref, upper_ref, corner_ref,
+    wqkv_ref, wproj_ref, sems,
+):
+    copies = [
+        pltpu.make_async_copy(proj_ref, wproj_ref, sems.at[0]),
+        pltpu.make_async_copy(qkv_ref, wqkv_ref, sems.at[1]),
+    ]
+    for copy in copies:
+        copy.start()
+    grads = jnp.concatenate([dot(n_ref[...], gp_ref[...]), dot(m_ref[...], u_ref[...])], axis=1)
+    store_shares(half_ref, grads)
+    refs = (own_ref, left_ref, upper_ref, corner_ref)
+    x = x_ref[...].astype(jnp.float32)
+    copies[0].wait()
+    part(x + dot(mix_ref[...], wproj_ref[...]), 0, refs)
+    normed, inverse = statistics(x)
+    copies[1].wait()
     grad_normed = dot(gp_ref[...], wqkv_ref[...], NT)
-    normed, inverse = statistics(x_ref)
     grad_tokens = inverse * (
         grad_normed
         - jnp.mean(grad_normed, -1, keepdims=True)
         - normed * jnp.mean(grad_normed * normed, -1, keepdims=True)
     )
-    gin_ref[...] = (u_ref[...].astype(jnp.float32) + grad_tokens).astype(jnp.bfloat16)
-
-
-def call(kernel, name, outs, scratch, flops, *args, dtype=jnp.bfloat16):
+    part(u_ref[...].astype(jnp.float32) + grad_tokens, 1, refs)
+
+
+def call(kernel, name, outs, scratch, flops, *args, dtypes=None, limit=12, placed=False, any_args=()):
     vmem = pl.BlockSpec(memory_space=pltpu.VMEM)
+    dtypes = dtypes or (jnp.bfloat16,) * len(outs)
+    make = pltpu.VMEM if placed else jax.ShapeDtypeStruct
     size = sum(2 * math.prod(shape) for shape in outs)
     return pl.pallas_call(
         kernel,
-        out_shape=tuple(jax.ShapeDtypeStruct(shape, dtype) for shape in outs),
-        in_specs=[vmem] * len(args),
+        out_shape=tuple(make(shape, dtype) for shape, dtype in zip(outs, dtypes)),
+        in_specs=[
+            pl.BlockSpec(memory_space=pltpu.HBM) if at in any_args else vmem for at in range(len(args))
+        ],
         out_specs=(vmem,) * len(outs),
-        scratch_shapes=[pltpu.VMEM(shape, kind) for shape, kind in scratch],
-        compiler_params=pltpu.CompilerParams(vmem_limit_bytes=40 * 1024 * 1024),
+        scratch_shapes=[
+            pltpu.SemaphoreType.DMA(shape) if kind is None else pltpu.VMEM(shape, kind)
+            for shape, kind in scratch
+        ],
+        compiler_params=pltpu.CompilerParams(vmem_limit_bytes=limit * 1024 * 1024),
         cost_estimate=pl.CostEstimate(flops=flops, bytes_accessed=2 * size, transcendentals=0),
         name=name,
     )(*args)
 
 
-def attention(x, u, lrow, lcol, w_qkv, w_proj):
-    tokens = x.shape[0]
+def attention(x, u, upper, corner, left, lrow, lcol, w_qkv, w_proj):
+    tokens = math.prod(x.shape[:-1])
     low, full = jnp.bfloat16, jnp.float32
     return call(
         attention_kernel,
         "window_attention",
-        ((32, 2, 64, 128), (tokens, 3 * D), (tokens, D), (D // 2, tokens), (D // 2, tokens)),
         (
+            (32, 2, 64, 128), (tokens, 3 * D), (tokens, D),
+            (D // 2, tokens), (D // 2, tokens), (tokens, D), (tokens, D),
+        ),
+        (
+            ((tokens, D), full),
             ((tokens, 3 * D), low),
             ((tokens, D), low),
             ((D, tokens), low),
@@ -229,20 +318,9 @@
             ((PER * WT, WT), full),
         ),
         5_000_000_000,
-        x, u, lrow, lcol, w_qkv, w_proj,
-    )
-
-
-def to_windows(array):
-    batch, levels, rows, cols, width = array.shape
-    shaped = array.reshape(levels, rows, cols // WLON, WLON, width)
-    return shaped.transpose(2, 0, 1, 3, 4).reshape(cols // WLON * WT, width)
-
-
-def from_windows(array):
-    windows = array.shape[0] // WT
-    shaped = array.reshape(windows, LEV, WLAT, WLON, D).transpose(1, 2, 0, 3, 4)
-    return shaped.reshape(1, LEV, WLAT, windows * WLON, D)
+        x, u, upper, corner, left, lrow, lcol, w_qkv, w_proj,
+        limit=20,
+    )
 
 
 LAT = ("yh", "x", "core")
@@ -264,36 +342,18 @@
     return lax.ppermute(value, (*LAT, "lon"), pairs)
 
 
-def move_one(inputs, cotangent):
-    def cut(rows, cols):
-        return jnp.concatenate([inputs[:, :, rows, cols], cotangent[:, :, rows, cols]], axis=0)
-
-    head, last, body, side = slice(0, SLAT), slice(SLAT, None), slice(0, -SLON), slice(-SLON, None)
-    corner = diagonal(cut(last, side), 1)
-    upper = passed_along(cut(last, body), LAT, 1)
-    left = passed_along(cut(head, side), "lon", 1)
-    outs = []
-    for at, own in enumerate((inputs, cotangent)):
-        top = jnp.concatenate([corner[at:at + 1], upper[at:at + 1]], axis=3)
-        bottom = jnp.concatenate([left[at:at + 1], own[:, :, head, body]], axis=3)
-        outs.append(jnp.concatenate([top, bottom], axis=2))
-    return outs
-
-
-def move_back(both):
-    head, last, side, body = slice(0, SLAT), slice(SLAT, None), slice(0, SLON), slice(SLON, None)
-    corner = diagonal(both[:, :, head, side], -1)
-    lower = passed_along(both[:, :, head, body], LAT, -1)
-    right = passed_along(both[:, :, last, side], "lon", -1)
-    top = jnp.concatenate([both[:, :, last, body], right], axis=3)
-    bottom = jnp.concatenate([lower, corner], axis=3)
-    return jnp.concatenate([top, bottom], axis=2)
-
-
 def per_device(inputs, cotangent, mask_ids, w_qkv, w_proj):
-    rolled, grad_in = move_one(inputs, cotangent)
-    x = to_windows(rolled)
-    u = to_windows(grad_in)
+    body = (2, LEV, SLAT, inputs.shape[3] - SLON, D)
+    side = (2, LEV, SLAT, SLON, D)
+    upper, corner, left = call(
+        cut_kernel, "cut_halos", (body, side, side),
+        (((2, *inputs.shape[1:]), jnp.bfloat16), ((2, LEV), None)), 1000,
+        *(pltpu.with_memory_space_constraint(array, pltpu.HBM) for array in (inputs, cotangent)),
+        limit=8, any_args=(0, 1),
+    )
+    upper = passed_along(upper, LAT, 1)
+    corner = diagonal(corner, 1)
+    left = passed_along(left, "lon", 1)
     first_band = lax.axis_index(LAT) == 0
     wrapped = jnp.logical_and(first_band, jnp.arange(WLAT) < SLAT).astype(jnp.int32)
     groups = mask_ids + 4 * wrapped[:, None]
@@ -301,29 +361,35 @@
     labels = groups.reshape(WLAT, windows, WLON).transpose(1, 0, 2).reshape(windows, WLAT * WLON)
     lrow = jnp.tile(labels, (1, LEV))
     lcol = lrow.reshape(windows * WT, 1)
-    w_qkv, w_proj = staged(w_qkv, w_proj)
-    send, gp, mix, nkeep, mkeep = attention(x, u, lrow, lcol, w_qkv, w_proj)
+    send, gp, mix, nkeep, mkeep, x, u = attention(
+        inputs, cotangent, upper, corner, left, lrow, lcol, *staged(w_qkv, w_proj)
+    )
     got = passed_along(send, "core", 1)
-    (own,) = call(
-        own_half_kernel, "own_half", (send.shape,), (), 600_000_000,
-        nkeep, mkeep, gp, u, dtype=jnp.float32,
-    )
-    (sums,) = call(add_kernel, "add_halves", (send.shape,), (), 1_000_000, own, got)
-    result, grad_total = call(
-        token_kernel, "token_outputs", (x.shape, x.shape), (), 2_000_000_000,
-        x, u, mix, gp, w_qkv, w_proj,
-    )
-    result, grad_total, sums = lax.optimization_barrier((result, grad_total, sums))
+    half, own, left, upper, corner = call(
+        rest_kernel, "own_half_and_outputs", (send.shape, body, side, body, side),
+        ((w_qkv.shape, jnp.bfloat16), (w_proj.shape, jnp.bfloat16), ((2,), None)), 600_000_000,
+        nkeep, mkeep, gp, u, x, mix, w_qkv, w_proj,
+        dtypes=(jnp.float32,) + (jnp.bfloat16,) * 4, any_args=(6, 7), limit=16,
+    )
+    (sums,) = call(add_kernel, "add_halves", (send.shape,), (), 1_000_000, half, got, placed=True)
+    own, left, upper, corner, sums = lax.optimization_barrier((own, left, upper, corner, sums))
     spread = lax.all_to_all(sums.reshape(8, 512, 128), ("yh", "x"), 0, 0, tiled=True)
-    (sums,) = call(sum_kernel, "sum_parts", ((512, 128),), (), 1_000_000, spread)
+    corner = diagonal(corner, -1)
+    lower = passed_along(upper, LAT, -1)
+    right = passed_along(left, "lon", -1)
+    (sums,) = call(sum_kernel, "sum_parts", ((512, 128),), (), 1_000_000, spread, placed=True)
     spread = lax.all_to_all(sums.reshape(8, 64, 128), "lon", 0, 0, tiled=True)
     share = jnp.sum(spread.astype(jnp.float32), 0)
     other = passed_along(share, "dp", 1)
     grad_qkv, grad_proj = call(
-        last_kernel, "last_sum", ((4, 3 * D), (4, D)), (), 1000, share, other, dtype=jnp.float32
-    )
-    back = move_back(jnp.concatenate([from_windows(result), from_windows(grad_total)], axis=0))
-    return (back[:1], back[1:], grad_qkv, grad_proj)
+        last_kernel, "last_sum", ((4, 3 * D), (4, D)), (), 1000, share, other,
+        dtypes=(jnp.float32,) * 2, limit=4,
+    )
+    output, grad_inputs = call(
+        join_kernel, "join_outputs", (inputs.shape, inputs.shape), (), 1000,
+        own, right, lower, corner, limit=8,
+    )
+    return (output, grad_inputs, grad_qkv, grad_proj)
 
 
 def solution(mesh):

time: 77.2 us -> 69.6 us (0.902)
  the two profiles are of different devices: /device:TPU:2 before, /device:TPU:32 now
where the time goes in v3:
time: 69.6 us; the launch traced here: 69.1 us
  blocking collectives  21.8 us (31%)
  starting transfers between devices  17.5 us (25%)
  Pallas kernels  13.7 us (20%)
  waiting for transfers between devices  11.7 us (17%)
  local copies, waits for them, and re-layouts  2.86 us (4%)
  other arithmetic  0.78 us (1%)
  between operations  0.75 us (1%)
    all_to_all x1, blocking collectives, per_device(): lax.all_to_all(sums.reshape(8, 512, 128), ('yh', 'x'), 0, 0, tiled=True)  21.8 us
    pallas_call x7, Pallas kernels, call(): pl.pallas_call(kernel, out_shape=tuple((make(shape, dtype) for shape, dty...  13.6 us
    all_to_all x1, starting transfers between devices, per_device(): spread = lax.all_to_all(sums.reshape(8, 64, 128), 'lon', 0, 0, tiled=True)  7.83 us
    ppermute x6, waiting for transfers between devices, passed_along(): return lax.ppermute(value, axis, pairs)  6.63 us
    ppermute x2, starting transfers between devices, diagonal(): return lax.ppermute(value, (*LAT, 'lon'), pairs)  5.31 us
    ppermute x6, starting transfers between devices, passed_along(): return lax.ppermute(value, axis, pairs)  4.37 us
    all_to_all x1, waiting for transfers between devices, per_device(): spread = lax.all_to_all(sums.reshape(8, 64, 128), 'lon', 0, 0, tiled=True)  4.18 us
    unnamed x12, local copies, waits for them, and re-layouts  2.46 us
  transfers between devices with their start and end apart: 9, of which 5 were waited for; matrix products, arithmetic and copies ran while one was open for 2% of the time, Pallas kernels for 5%

profile of v3, /device:TPU:32, one launch (start us, length us, event | category | flops | bytes accessed | tf_op | source)
XLA Modules:
  0.0 69.1 jit_solution(2777377465256651376)
XLA Ops:
  0.7 1.2 %cut_halos.1 = (bf16[2,2,3,18,512]{4,3,2,1,0:T(8,128)(2,1)S(1)}, bf16[2,2,3,6,512]{4,3,2,1,0:T(8,128)(2,1)S(1)}, bf16[2,2,3,6,512]{4,3,2,1,0:T(8,128)(2,1)S(1)}) custom-call(bf16[1,2,6,24,512]{4,3,2,1,0:T(8,128)(2,1)} %own_x_ref.1, bf16[1,2,6,24,512]{4,3,2,1,0:T(8,128)(2,1)} %own_u_ref.1), custom_call_target="tpu_custom_call" | custom-call | flops 1000 | bytes 737280 | tf_op jit(solution)/shard_map/cut_halos/pallas_call | solution.py:281
  1.9 1.4 %collective-permute-start.1 = (bf16[2,2,3,6,512]{4,3,2,1,0:T(8,128)(2,1)S(1)}, bf16[2,2,3,6,512]{4,3,2,1,0:T(8,128)(2,1)S(1)}, u32[]{:S(2)}, u32[]{:S(2)}) collective-permute-start(bf16[2,2,3,6,512]{4,3,2,1,0:T(8,128)(2,1)S(1)} %get-tuple-element.31), channel_id=1, source_target_pairs={{0,9},{1,10},{2,11},{3,12},{4,13},{5,14},{6,15},{7,8},{8,17},{9,18... | collective-permute-start | bytes 221192 | tf_op jit(solution)/shard_map/ppermute | solution.py:342
  3.3 1.9 %collective-permute-start.2 = (bf16[2,2,3,6,512]{4,3,2,1,0:T(8,128)(2,1)S(1)}, bf16[2,2,3,6,512]{4,3,2,1,0:T(8,128)(2,1)S(1)}, u32[]{:S(2)}, u32[]{:S(2)}) collective-permute-start(bf16[2,2,3,6,512]{4,3,2,1,0:T(8,128)(2,1)S(1)} %get-tuple-element.32), channel_id=1, source_target_pairs={{0,1},{1,2},{2,3},{3,4},{4,5},{5,6},{6,7},{7,0},{8,9},{9,10},{10,1... | collective-permute-start | bytes 221192 | tf_op jit(solution)/shard_map/ppermute | solution.py:332
  5.3 1.3 %collective-permute-start = (bf16[2,2,3,18,512]{4,3,2,1,0:T(8,128)(2,1)S(1)}, bf16[2,2,3,18,512]{4,3,2,1,0:T(8,128)(2,1)S(1)}, u32[]{:S(2)}, u32[]{:S(2)}) collective-permute-start(bf16[2,2,3,18,512]{4,3,2,1,0:T(8,128)(2,1)S(1)} %get-tuple-element.30), channel_id=1, source_target_pairs={{0,8},{8,16},{16,24},{24,32},{32,40},{40,48},{48,56},{56,64},{64,7... | collective-permute-start | bytes 663560 | tf_op jit(solution)/shard_map/ppermute | solution.py:332
  6.6 0.8 %broadcast_add_fusion = s32[6,24]{1,0:T(8,128)S(1)} fusion(s32[6,24]{1,0:T(8,128)} %param.7, s32[6]{0:T(128)S(1)} %and_select_fusion), kind=kLoop, calls=%fused_computation.2 | loop fusion | flops 144 | bytes 1176 | tf_op jit(solution)/shard_map/add | solution.py:359
  7.3 0.1 reshape.31
  7.4 0.1 tile.12
  7.5 0.1 tile.14.lrow_ref
  7.6 0.1 tile.16.lcol_ref
  7.8 0.0 copy-start
  7.8 1.4 %copy-done = bf16[512,1536]{1,0:T(8,128)(2,1)S(1)} copy-done((bf16[512,1536]{1,0:T(8,128)(2,1)S(1)}, bf16[512,1536]{1,0:T(8,128)(2,1)}, u32[]{:S(2)}) %copy-start) | copy-done | bytes 1572888
  9.2 1.0 %copy-done.2 = bf16[512,512]{1,0:T(8,128)(2,1)S(1)} copy-done((bf16[512,512]{1,0:T(8,128)(2,1)S(1)}, bf16[512,512]{1,0:T(8,128)(2,1)}, u32[]{:S(2)}) %copy-start.2) | copy-done | bytes 524312
  10.2 0.2 stage_weights.1
  10.4 0.9 %collective-permute-done.1.corner_ref = bf16[2,2,3,6,512]{4,3,2,1,0:T(8,128)(2,1)S(1)} collective-permute-done((bf16[2,2,3,6,512]{4,3,2,1,0:T(8,128)(2,1)S(1)}, bf16[2,2,3,6,512]{4,3,2,1,0:T(8,128)(2,1)S(1)}, u32[]{:S(2)}, u32[]{:S(2)}) %collective-permute-start.1) | collective-permute-done | bytes 73760 | tf_op jit(solution)/shard_map/ppermute | solution.py:342
  11.3 0.0 collective-permute-done.2.left_ref
  11.3 3.8 %collective-permute-done.upper_ref = bf16[2,2,3,18,512]{4,3,2,1,0:T(8,128)(2,1)S(1)} collective-permute-done((bf16[2,2,3,18,512]{4,3,2,1,0:T(8,128)(2,1)S(1)}, bf16[2,2,3,18,512]{4,3,2,1,0:T(8,128)(2,1)S(1)}, u32[]{:S(2)}, u32[]{:S(2)}) %collective-permute-start) | collective-permute-done | bytes 221216 | tf_op jit(solution)/shard_map/ppermute | solution.py:332
  15.0 7.8 %window_attention.1 = (bf16[32,2,64,128]{3,2,1,0:T(8,128)(2,1)S(1)}, bf16[288,1536]{1,0:T(8,128)(2,1)S(1)}, bf16[288,512]{1,0:T(8,128)(2,1)S(1)}, bf16[256,288]{...) custom-call(bf16[1,2,6,24,512]{4,3,2,1,0:T(8,128)(2,1)S(1)} %copy-do, ...), custom_call_target="tpu_custom_call" | custom-call | flops 5000000000 | bytes 6225920 | tf_op jit(solution)/shard_map/window_attention/pallas_call | solution.py:281
  22.8 0.3 collective-permute-start.3
  23.1 2.1 %own_half_and_outputs.1 = (f32[32,2,64,128]{3,2,1,0:T(8,128)S(1)}, bf16[2,2,3,18,512]{4,3,2,1,0:T(8,128)(2,1)S(1)}, bf16[2,2,3,6,512]{4,3,2,1,0:T(8,128)(2,1)S(1...) custom-call(bf16[256,288]{1,0:T(8,128)(2,1)S(1)} %get-tuple-element.35.n_ref, ...), custom_call_target="tpu_custom_call" | custom-call | flops 600000000 | bytes 3276800 | tf_op jit(solution)/shard_map/own_half_and_outputs/pallas_call | solution.py:281
  25.3 0.5 collective-permute-done.3.got_ref
  25.8 0.2 add_halves.1
  25.9 21.8 %all_to_all.10.parts_ref = bf16[8,512,128]{2,1,0:T(8,128)(2,1)S(1)} all-to-all(bf16[8,512,128]{2,1,0:T(8,128)(2,1)S(1)} %bitcast.5), channel_id=1, replica_groups=mesh['dp'=2,'yh'=2,'x'=4,'core'=2,'lon'=8] {'yh','x'}, dimensions={0} | all-to-all | bytes 2097152 | tf_op jit(solution)/shard_map/all_to_all | solution.py:376
  47.7 0.8 %sum_parts.1 = bf16[512,128]{1,0:T(8,128)(2,1)} custom-call(bf16[8,512,128]{2,1,0:T(8,128)(2,1)S(1)} %all_to_all.10.parts_ref), custom_call_target="tpu_custom_call" | custom-call | flops 1000000 | bytes 262144 | tf_op jit(solution)/shard_map/sum_parts/pallas_call | solution.py:281
  48.5 7.8 %all-to-all-start.1 = ((bf16[8,64,128]{2,1,0:T(8,128)(2,1)}), bf16[8,64,128]{2,1,0:T(8,128)(2,1)S(1)}, u32[]{:S(2)}, u32[]{:S(2)}) async-start(bf16[8,64,128]{2,1,0:T(8,128)(2,1)} %bitcast.2), calls=%async_computation.1 | async-start | bytes 262144 | tf_op jit(solution)/shard_map/all_to_all | solution.py:381
  56.3 0.1 collective-permute-start.4
  56.4 3.9 %collective-permute-start.6 = (bf16[2,2,3,6,512]{4,3,2,1,0:T(8,128)(2,1)S(1)}, bf16[2,2,3,6,512]{4,3,2,1,0:T(8,128)(2,1)S(1)}, u32[]{:S(2)}, u32[]{:S(2)}) collective-permute-start(bf16[2,2,3,6,512]{4,3,2,1,0:T(8,128)(2,1)S(1)} %get-tuple-element.50), channel_id=1, source_target_pairs={{0,127},{1,120},{2,121},{3,122},{4,123},{5,124},{6,125},{7,126},{8... | collective-permute-start | bytes 221192 | tf_op jit(solution)/shard_map/ppermute | solution.py:342
  60.3 4.2 %all-to-all-done.1 = bf16[8,64,128]{2,1,0:T(8,128)(2,1)S(1)} async-done(((bf16[8,64,128]{2,1,0:T(8,128)(2,1)}), bf16[8,64,128]{2,1,0:T(8,128)(2,1)S(1)}, u32[]{:S(2)}, u32[]{:S(2)}) %all-to-all-start.1) | async-done | bytes 131104 | tf_op jit(solution)/shard_map/all_to_all | solution.py:381
  64.5 0.8 %collective-permute-start.7 = (f32[64,128]{1,0:T(8,128)S(1)}, f32[64,128]{1,0:T(8,128)S(1)}, u32[]{:S(2)}, u32[]{:S(2)}) collective-permute-start(f32[64,128]{1,0:T(8,128)S(1)} %convert_reduce_fusion.share_ref), channel_id=1, source_target_pairs={{0,128},{128,0},{1,129},{129,1},{2,130},{130,2},{3,131},{131,3},{4... | collective-permute-start | bytes 98312 | tf_op jit(solution)/shard_map/ppermute | solution.py:332
  65.3 0.0 collective-permute-done.4.right_ref
  65.3 0.9 %join_outputs.1 = (bf16[1,2,6,24,512]{4,3,2,1,0:T(8,128)(2,1)}, bf16[1,2,6,24,512]{4,3,2,1,0:T(8,128)(2,1)}) custom-call(bf16[2,2,3,18,512]{4,3,2,1,0:T(8,128)(2,1)S(1)} %get-tuple-element.47.own_ref, bf16[2,2,3,6,512]{4,3,2,1,0:T(8,128)(2,1)S(1)} %collective-permute-done.4.right_ref, bf16[2,2,3,18,512]{4,3,2,1,0:T(8,128)(2,1)S(1)} %collective-permute-done.5.lower_ref, ...), custom_call_target="tpu_custom_call" | custom-call | flops 1000 | bytes 1179648 | tf_op jit(solution)/shard_map/join_outputs/pallas_call | solution.py:281
  66.1 2.4 %collective-permute-done.7.other_ref = f32[64,128]{1,0:T(8,128)S(1)} collective-permute-done((f32[64,128]{1,0:T(8,128)S(1)}, f32[64,128]{1,0:T(8,128)S(1)}, u32[]{:S(2)}, u32[]{:S(2)}) %collective-permute-start.7) | collective-permute-done | bytes 32800 | tf_op jit(solution)/shard_map/ppermute | solution.py:332
  68.5 0.6 last_sum.1
  (16 shorter events, 0.1 us)
Async XLA Ops:
  0.6 14.4 %copy-start.5 = (bf16[1,2,6,24,512]{4,3,2,1,0:T(8,128)(2,1)S(1)}, bf16[1,2,6,24,512]{4,3,2,1,0:T(8,128)(2,1)}, u32[]{:S(2)}) copy-start(bf16[1,2,6,24,512]{4,3,2,1,0:T(8,128)(2,1)} %own_u_ref.1) | copy-start | bytes 884740
  0.6 14.4 %copy-start.4 = (bf16[1,2,6,24,512]{4,3,2,1,0:T(8,128)(2,1)S(1)}, bf16[1,2,6,24,512]{4,3,2,1,0:T(8,128)(2,1)}, u32[]{:S(2)}) copy-start(bf16[1,2,6,24,512]{4,3,2,1,0:T(8,128)(2,1)} %own_x_ref.1) | copy-start | bytes 884740
  1.9 9.4 %collective-permute-start.1 = (bf16[2,2,3,6,512]{4,3,2,1,0:T(8,128)(2,1)S(1)}, bf16[2,2,3,6,512]{4,3,2,1,0:T(8,128)(2,1)S(1)}, u32[]{:S(2)}, u32[]{:S(2)}) collective-permute-start(bf16[2,2,3,6,512]{4,3,2,1,0:T(8,128)(2,1)S(1)} %get-tuple-element.31), channel_id=1, source_target_pairs={{0,9},{1,10},{2,11},{3,12},{4,13},{5,14},{6,15},{7,8},{8,17},{9,18... | collective-permute-start | bytes 221192 | tf_op jit(solution)/shard_map/ppermute | solution.py:342
  3.3 7.9 %collective-permute-start.2 = (bf16[2,2,3,6,512]{4,3,2,1,0:T(8,128)(2,1)S(1)}, bf16[2,2,3,6,512]{4,3,2,1,0:T(8,128)(2,1)S(1)}, u32[]{:S(2)}, u32[]{:S(2)}) collective-permute-start(bf16[2,2,3,6,512]{4,3,2,1,0:T(8,128)(2,1)S(1)} %get-tuple-element.32), channel_id=1, source_target_pairs={{0,1},{1,2},{2,3},{3,4},{4,5},{5,6},{6,7},{7,0},{8,9},{9,10},{10,1... | collective-permute-start | bytes 221192 | tf_op jit(solution)/shard_map/ppermute | solution.py:332
  5.3 9.8 %collective-permute-start = (bf16[2,2,3,18,512]{4,3,2,1,0:T(8,128)(2,1)S(1)}, bf16[2,2,3,18,512]{4,3,2,1,0:T(8,128)(2,1)S(1)}, u32[]{:S(2)}, u32[]{:S(2)}) collective-permute-start(bf16[2,2,3,18,512]{4,3,2,1,0:T(8,128)(2,1)S(1)} %get-tuple-element.30), channel_id=1, source_target_pairs={{0,8},{8,16},{16,24},{24,32},{32,40},{40,48},{48,56},{56,64},{64,7... | collective-permute-start | bytes 663560 | tf_op jit(solution)/shard_map/ppermute | solution.py:332
  7.8 1.4 %copy-start = (bf16[512,1536]{1,0:T(8,128)(2,1)S(1)}, bf16[512,1536]{1,0:T(8,128)(2,1)}, u32[]{:S(2)}) copy-start(bf16[512,1536]{1,0:T(8,128)(2,1)} %qkv_ref.3) | copy-start | bytes 4718596
  9.2 1.0 %copy-start.2 = (bf16[512,512]{1,0:T(8,128)(2,1)S(1)}, bf16[512,512]{1,0:T(8,128)(2,1)}, u32[]{:S(2)}) copy-start(bf16[512,512]{1,0:T(8,128)(2,1)} %proj_ref.3) | copy-start | bytes 1572868
  15.0 8.1 %copy-start.1 = (bf16[512,1536]{1,0:T(8,128)(2,1)S(1)}, bf16[512,1536]{1,0:T(8,128)(2,1)}, u32[]{:S(2)}) copy-start(bf16[512,1536]{1,0:T(8,128)(2,1)} %qkv_ref.3) | copy-start | bytes 4718596
  15.0 8.1 %copy-start.3 = (bf16[512,512]{1,0:T(8,128)(2,1)S(1)}, bf16[512,512]{1,0:T(8,128)(2,1)}, u32[]{:S(2)}) copy-start(bf16[512,512]{1,0:T(8,128)(2,1)} %proj_ref.3) | copy-start | bytes 1572868
  22.8 2.9 %collective-permute-start.3 = (bf16[32,2,64,128]{3,2,1,0:T(8,128)(2,1)S(1)}, bf16[32,2,64,128]{3,2,1,0:T(8,128)(2,1)S(1)}, u32[]{:S(2)}, u32[]{:S(2)}) collective-permute-start(bf16[32,2,64,128]{3,2,1,0:T(8,128)(2,1)S(1)} %get-tuple-element.46), channel_id=1, source_target_pairs={{0,8},{8,0},{1,9},{9,1},{2,10},{10,2},{3,11},{11,3},{4,12},{12,4},... | collective-permute-start | bytes 3145736 | tf_op jit(solution)/shard_map/ppermute | solution.py:332
  48.5 16.0 %all-to-all-start.1 = ((bf16[8,64,128]{2,1,0:T(8,128)(2,1)}), bf16[8,64,128]{2,1,0:T(8,128)(2,1)S(1)}, u32[]{:S(2)}, u32[]{:S(2)}) async-start(bf16[8,64,128]{2,1,0:T(8,128)(2,1)} %bitcast.2), calls=%async_computation.1 | async-start | bytes 262144 | tf_op jit(solution)/shard_map/all_to_all | solution.py:381
  56.3 8.9 %collective-permute-start.5 = (bf16[2,2,3,18,512]{4,3,2,1,0:T(8,128)(2,1)S(1)}, bf16[2,2,3,18,512]{4,3,2,1,0:T(8,128)(2,1)S(1)}, u32[]{:S(2)}, u32[]{:S(2)}) collective-permute-start(bf16[2,2,3,18,512]{4,3,2,1,0:T(8,128)(2,1)S(1)} %get-tuple-element.49), channel_id=1, source_target_pairs={{0,120},{8,0},{16,8},{24,16},{32,24},{40,32},{48,40},{56,48},{64,5... | collective-permute-start | bytes 663560 | tf_op jit(solution)/shard_map/ppermute | solution.py:332
  56.3 8.9 %collective-permute-start.4 = (bf16[2,2,3,6,512]{4,3,2,1,0:T(8,128)(2,1)S(1)}, bf16[2,2,3,6,512]{4,3,2,1,0:T(8,128)(2,1)S(1)}, u32[]{:S(2)}, u32[]{:S(2)}) collective-permute-start(bf16[2,2,3,6,512]{4,3,2,1,0:T(8,128)(2,1)S(1)} %get-tuple-element.48), channel_id=1, source_target_pairs={{0,7},{1,0},{2,1},{3,2},{4,3},{5,4},{6,5},{7,6},{8,15},{9,8},{10,9... | collective-permute-start | bytes 221192 | tf_op jit(solution)/shard_map/ppermute | solution.py:332
  56.4 8.9 %collective-permute-start.6 = (bf16[2,2,3,6,512]{4,3,2,1,0:T(8,128)(2,1)S(1)}, bf16[2,2,3,6,512]{4,3,2,1,0:T(8,128)(2,1)S(1)}, u32[]{:S(2)}, u32[]{:S(2)}) collective-permute-start(bf16[2,2,3,6,512]{4,3,2,1,0:T(8,128)(2,1)S(1)} %get-tuple-element.50), channel_id=1, source_target_pairs={{0,127},{1,120},{2,121},{3,122},{4,123},{5,124},{6,125},{7,126},{8... | collective-permute-start | bytes 221192 | tf_op jit(solution)/shard_map/ppermute | solution.py:342
  64.5 4.0 %collective-permute-start.7 = (f32[64,128]{1,0:T(8,128)S(1)}, f32[64,128]{1,0:T(8,128)S(1)}, u32[]{:S(2)}, u32[]{:S(2)}) collective-permute-start(f32[64,128]{1,0:T(8,128)S(1)} %convert_reduce_fusion.share_ref), channel_id=1, source_target_pairs={{0,128},{128,0},{1,129},{129,1},{2,130},{130,2},{3,131},{131,3},{4... | collective-permute-start | bytes 98312 | tf_op jit(solution)/shard_map/ppermute | solution.py:332

commit v4 on v3

--- a/solution.py
+++ b/solution.py
@@ -182,21 +182,51 @@
     store_shares(send_ref, grads)
 
 
-def add_kernel(own_ref, got_ref, sum_ref):
-    sum_ref[...] = (own_ref[...] + got_ref[...].astype(jnp.float32)).astype(jnp.bfloat16)
-
-
-def sum_kernel(parts_ref, sum_ref):
-    total = parts_ref[0].astype(jnp.float32)
-    for part in range(1, parts_ref.shape[0]):
-        total = total + parts_ref[part].astype(jnp.float32)
-    sum_ref[...] = total.astype(sum_ref.dtype)
+def first_kernel(half_ref, got_ref, keep0_ref, send0_ref, keep1_ref, send1_ref):
+    a, d = lax.axis_index("xl"), lax.axis_index("dp")
+
+    def total(*at):
+        return half_ref[at] + got_ref[at].astype(jnp.float32)
+
+    for yh in range(2):
+        keep0_ref[yh] = total(yh, 0, a)
+        send0_ref[yh] = total(yh, 0, 1 - a).astype(jnp.bfloat16)
+        for xl in range(2):
+            for lon in range(8):
+                keep1_ref[yh, xl, lon] = total(yh, 1, xl, lon, d)
+                send1_ref[yh, xl, lon] = total(yh, 1, xl, lon, 1 - d).astype(jnp.bfloat16)
+
+
+def second_kernel(keep0_ref, got0_ref, keep1_ref, got1_ref, own_ref, send0_ref, send1_ref):
+    a, d = lax.axis_index("xl"), lax.axis_index("dp")
+
+    def total0(*at):
+        return keep0_ref[at] + got0_ref[at].astype(jnp.float32)
+
+    def total1(*at):
+        return keep1_ref[at] + got1_ref[at].astype(jnp.float32)
+
+    for yh in range(2):
+        own_ref[1, yh] = total1(yh, a)
+        send1_ref[yh] = total1(yh, 1 - a).astype(jnp.bfloat16)
+        for lon in range(8):
+            own_ref[0, yh, lon] = total0(yh, lon, d)
+            send0_ref[yh, lon] = total0(yh, lon, 1 - d).astype(jnp.bfloat16)
+
+
+def third_kernel(own_ref, got0_ref, got1_ref, sum_ref):
+    for xh, ref in enumerate((got0_ref, got1_ref)):
+        for yh in range(2):
+            sum_ref[yh, xh] = (own_ref[xh, yh] + ref[yh].astype(jnp.float32)).astype(jnp.bfloat16)
 
 
 def last_kernel(share_ref, other_ref, qkv_ref, proj_ref):
-    total = share_ref[...] + other_ref[...]
+    second = lax.axis_index("dp") == 1
+    share, other = share_ref[...], other_ref[...]
+    halves = (jnp.where(second, other, share), jnp.where(second, share, other))
     for tile in range(16):
-        piece = total[tile * 4:tile * 4 + 4, :]
+        row = tile % 8 * 4
+        piece = halves[tile // 8][row:row + 4, :]
         if tile < 12:
             qkv_ref[:, tile * 128:(tile + 1) * 128] = piece
         else:
@@ -323,7 +353,7 @@
     )
 
 
-LAT = ("yh", "x", "core")
+LAT = ("yh", "xh", "xl", "core")
 
 
 def passed_along(value, axis, steps):
@@ -371,14 +401,26 @@
         nkeep, mkeep, gp, u, x, mix, w_qkv, w_proj,
         dtypes=(jnp.float32,) + (jnp.bfloat16,) * 4, any_args=(6, 7), limit=16,
     )
-    (sums,) = call(add_kernel, "add_halves", (send.shape,), (), 1_000_000, half, got, placed=True)
+    low, full = jnp.bfloat16, jnp.float32
+    shape = (2, 2, 2, 8, 2, 32, 128)
+    keep0, send0, keep1, send1 = call(
+        first_kernel, "first_sums", ((2, 8, 2, 32, 128),) * 2 + ((2, 2, 8, 32, 128),) * 2, (), 1_000_000,
+        half.reshape(shape), got.reshape(shape), dtypes=(full, low) * 2, placed=True,
+    )
+    got0, got1 = passed_along(send0, "xl", 1), passed_along(send1, "dp", 1)
+    mine, send0, send1 = call(
+        second_kernel, "second_sums", ((2, 2, 8, 32, 128),) + ((2, 8, 32, 128),) * 2, (), 1_000_000,
+        keep0, got0, keep1, got1, dtypes=(full, low, low), placed=True,
+    )
+    got0, got1 = passed_along(send0, "dp", 1), passed_along(send1, "xl", 1)
+    (sums,) = call(
+        third_kernel, "third_sums", ((2, 2, 8, 32, 128),), (), 1_000_000, mine, got0, got1, placed=True
+    )
     own, left, upper, corner, sums = lax.optimization_barrier((own, left, upper, corner, sums))
-    spread = lax.all_to_all(sums.reshape(8, 512, 128), ("yh", "x"), 0, 0, tiled=True)
+    spread = lax.all_to_all(sums.reshape(32, 32, 128), ("yh", "xh", "lon"), 0, 0, tiled=True)
     corner = diagonal(corner, -1)
     lower = passed_along(upper, LAT, -1)
     right = passed_along(left, "lon", -1)
-    (sums,) = call(sum_kernel, "sum_parts", ((512, 128),), (), 1_000_000, spread, placed=True)
-    spread = lax.all_to_all(sums.reshape(8, 64, 128), "lon", 0, 0, tiled=True)
     share = jnp.sum(spread.astype(jnp.float32), 0)
     other = passed_along(share, "dp", 1)
     grad_qkv, grad_proj = call(
@@ -393,7 +435,7 @@
 
 
 def solution(mesh):
-    mesh = Mesh(mesh.devices.reshape(2, 2, 4, 2, 8), ("dp", "yh", "x", "core", "lon"))
+    mesh = Mesh(mesh.devices.reshape(2, 2, 2, 2, 2, 8), ("dp", *LAT, "lon"))
     tokens = P("dp", None, LAT, "lon", None)
     return jax.shard_map(
         per_device,

time: 69.6 us -> 71.3 us (1.024)
  blocking collectives: 21.8 us -> 0 us
  starting transfers between devices: 17.5 us -> 29.4 us
  waiting for transfers between devices: 11.7 us -> 23 us
    all_to_all x1 -> x0, blocking collectives: 21.8 us -> none  [per_device(): lax.all_to_all(sums.reshape(8, 512, 128), ('yh', 'x'), 0, 0, tiled=True)]
    ppermute x6 -> x10, waiting for transfers between devices: 6.63 us -> 17.1 us  [passed_along(): return lax.ppermute(value, axis, pairs)]
    ppermute x6 -> x10, starting transfers between devices: 4.37 us -> 12.5 us  [passed_along(): return lax.ppermute(value, axis, pairs)]
    all_to_all x1, starting transfers between devices: 7.83 us -> 10.3 us  [per_device(): lax.all_to_all(sums.reshape(32, 32, 128), ('yh', 'xh', 'lon'), 0, 0, tile...]
    ppermute x2, starting transfers between devices: 5.31 us -> 6.54 us  [diagonal(): return lax.ppermute(value, (*LAT, 'lon'), pairs)]
    all_to_all x1, waiting for transfers between devices: 4.18 us -> 5.07 us  [per_device(): lax.all_to_all(sums.reshape(32, 32, 128), ('yh', 'xh', 'lon'), 0, 0, tile...]
    pallas_call x7 -> x8, Pallas kernels: 13.6 us -> 13.6 us  [call(): pl.pallas_call(kernel, out_shape=tuple((make(shape, dtype) for shape, dty...]
  transfers between devices with their start and end apart: 9 -> 13, of which waited for: 5 -> 9; matrix products, arithmetic and copies ran while one was open for 2% -> 2% of each run, Pallas kernels for 5% -> 4%
where the time goes in v4:
time: 71.3 us; the launch traced here: 70.7 us
  starting transfers between devices  29.4 us (41%)
  waiting for transfers between devices  23 us (32%)
  Pallas kernels  13.8 us (19%)
  local copies, waits for them, and re-layouts  2.86 us (4%)
  other arithmetic  0.81 us (1%)
  between operations  0.77 us (1%)
    ppermute x10, waiting for transfers between devices, passed_along(): return lax.ppermute(value, axis, pairs)  17.1 us
    pallas_call x8, Pallas kernels, call(): pl.pallas_call(kernel, out_shape=tuple((make(shape, dtype) for shape, dty...  13.6 us
    ppermute x10, starting transfers between devices, passed_along(): return lax.ppermute(value, axis, pairs)  12.5 us
    all_to_all x1, starting transfers between devices, per_device(): lax.all_to_all(sums.reshape(32, 32, 128), ('yh', 'xh', 'lon'), 0, 0, tile...  10.3 us
    ppermute x2, starting transfers between devices, diagonal(): return lax.ppermute(value, (*LAT, 'lon'), pairs)  6.54 us
    all_to_all x1, waiting for transfers between devices, per_device(): lax.all_to_all(sums.reshape(32, 32, 128), ('yh', 'xh', 'lon'), 0, 0, tile...  5.07 us
    unnamed x12, local copies, waits for them, and re-layouts  2.46 us
  transfers between devices with their start and end apart: 13, of which 9 were waited for; matrix products, arithmetic and copies ran while one was open for 2% of the time, Pallas kernels for 4%

profile of v4, /device:TPU:32, one launch (start us, length us, event | category | flops | bytes accessed | tf_op | source)
XLA Modules:
  0.0 70.7 jit_solution(18068369106596248330)
XLA Ops:
  0.7 1.2 %cut_halos.1 = (bf16[2,2,3,18,512]{4,3,2,1,0:T(8,128)(2,1)S(1)}, bf16[2,2,3,6,512]{4,3,2,1,0:T(8,128)(2,1)S(1)}, bf16[2,2,3,6,512]{4,3,2,1,0:T(8,128)(2,1)S(1)}) custom-call(bf16[1,2,6,24,512]{4,3,2,1,0:T(8,128)(2,1)} %own_x_ref.1, bf16[1,2,6,24,512]{4,3,2,1,0:T(8,128)(2,1)} %own_u_ref.1), custom_call_target="tpu_custom_call" | custom-call | flops 1000 | bytes 737280 | tf_op jit(solution)/shard_map/cut_halos/pallas_call | solution.py:311
  1.9 1.4 %collective-permute-start.1 = (bf16[2,2,3,6,512]{4,3,2,1,0:T(8,128)(2,1)S(1)}, bf16[2,2,3,6,512]{4,3,2,1,0:T(8,128)(2,1)S(1)}, u32[]{:S(2)}, u32[]{:S(2)}) collective-permute-start(bf16[2,2,3,6,512]{4,3,2,1,0:T(8,128)(2,1)S(1)} %get-tuple-element.38), channel_id=1, source_target_pairs={{0,9},{1,10},{2,11},{3,12},{4,13},{5,14},{6,15},{7,8},{8,17},{9,18... | collective-permute-start | bytes 221192 | tf_op jit(solution)/shard_map/ppermute | solution.py:372
  3.3 1.9 %collective-permute-start.2 = (bf16[2,2,3,6,512]{4,3,2,1,0:T(8,128)(2,1)S(1)}, bf16[2,2,3,6,512]{4,3,2,1,0:T(8,128)(2,1)S(1)}, u32[]{:S(2)}, u32[]{:S(2)}) collective-permute-start(bf16[2,2,3,6,512]{4,3,2,1,0:T(8,128)(2,1)S(1)} %get-tuple-element.39), channel_id=1, source_target_pairs={{0,1},{1,2},{2,3},{3,4},{4,5},{5,6},{6,7},{7,0},{8,9},{9,10},{10,1... | collective-permute-start | bytes 221192 | tf_op jit(solution)/shard_map/ppermute | solution.py:362
  5.3 1.3 %collective-permute-start = (bf16[2,2,3,18,512]{4,3,2,1,0:T(8,128)(2,1)S(1)}, bf16[2,2,3,18,512]{4,3,2,1,0:T(8,128)(2,1)S(1)}, u32[]{:S(2)}, u32[]{:S(2)}) collective-permute-start(bf16[2,2,3,18,512]{4,3,2,1,0:T(8,128)(2,1)S(1)} %get-tuple-element.37), channel_id=1, source_target_pairs={{0,8},{8,16},{16,24},{24,32},{32,40},{40,48},{48,56},{56,64},{64,7... | collective-permute-start | bytes 663560 | tf_op jit(solution)/shard_map/ppermute | solution.py:362
  6.6 0.8 %broadcast_add_fusion = s32[6,24]{1,0:T(8,128)S(1)} fusion(s32[6,24]{1,0:T(8,128)} %param.7, s32[6]{0:T(128)S(1)} %and_select_fusion), kind=kLoop, calls=%fused_computation.2 | loop fusion | flops 144 | bytes 1176 | tf_op jit(solution)/shard_map/add | solution.py:389
  7.6 0.1 tile.16.lcol_ref
  7.8 1.4 %copy-done = bf16[512,1536]{1,0:T(8,128)(2,1)S(1)} copy-done((bf16[512,1536]{1,0:T(8,128)(2,1)S(1)}, bf16[512,1536]{1,0:T(8,128)(2,1)}, u32[]{:S(2)}) %copy-start) | copy-done | bytes 1572888
  9.2 1.0 %copy-done.2 = bf16[512,512]{1,0:T(8,128)(2,1)S(1)} copy-done((bf16[512,512]{1,0:T(8,128)(2,1)S(1)}, bf16[512,512]{1,0:T(8,128)(2,1)}, u32[]{:S(2)}) %copy-start.2) | copy-done | bytes 524312
  10.2 0.2 stage_weights.1
  10.4 0.9 %collective-permute-done.1.corner_ref = bf16[2,2,3,6,512]{4,3,2,1,0:T(8,128)(2,1)S(1)} collective-permute-done((bf16[2,2,3,6,512]{4,3,2,1,0:T(8,128)(2,1)S(1)}, bf16[2,2,3,6,512]{4,3,2,1,0:T(8,128)(2,1)S(1)}, u32[]{:S(2)}, u32[]{:S(2)}) %collective-permute-start.1) | collective-permute-done | bytes 73760 | tf_op jit(solution)/shard_map/ppermute | solution.py:372
  11.3 3.8 %collective-permute-done.upper_ref = bf16[2,2,3,18,512]{4,3,2,1,0:T(8,128)(2,1)S(1)} collective-permute-done((bf16[2,2,3,18,512]{4,3,2,1,0:T(8,128)(2,1)S(1)}, bf16[2,2,3,18,512]{4,3,2,1,0:T(8,128)(2,1)S(1)}, u32[]{:S(2)}, u32[]{:S(2)}) %collective-permute-start) | collective-permute-done | bytes 221216 | tf_op jit(solution)/shard_map/ppermute | solution.py:362
  15.0 7.8 %window_attention.1 = (bf16[32,2,64,128]{3,2,1,0:T(8,128)(2,1)S(1)}, bf16[288,1536]{1,0:T(8,128)(2,1)S(1)}, bf16[288,512]{1,0:T(8,128)(2,1)S(1)}, bf16[256,288]{...) custom-call(bf16[1,2,6,24,512]{4,3,2,1,0:T(8,128)(2,1)S(1)} %copy-do, ...), custom_call_target="tpu_custom_call" | custom-call | flops 5000000000 | bytes 6225920 | tf_op jit(solution)/shard_map/window_attention/pallas_call | solution.py:311
  22.8 0.3 collective-permute-start.3
  23.1 2.1 %own_half_and_outputs.1 = (f32[32,2,64,128]{3,2,1,0:T(8,128)S(1)}, bf16[2,2,3,18,512]{4,3,2,1,0:T(8,128)(2,1)S(1)}, bf16[2,2,3,6,512]{4,3,2,1,0:T(8,128)(2,1)S(1...) custom-call(bf16[256,288]{1,0:T(8,128)(2,1)S(1)} %get-tuple-element.42.n_ref, ...), custom_call_target="tpu_custom_call" | custom-call | flops 600000000 | bytes 3276800 | tf_op jit(solution)/shard_map/own_half_and_outputs/pallas_call | solution.py:311
  25.3 0.5 collective-permute-done.3
  25.8 0.2 first_sums.1
  26.0 1.7 %collective-permute-start.5 = (bf16[2,2,8,32,128]{4,3,2,1,0:T(8,128)(2,1)S(1)}, bf16[2,2,8,32,128]{4,3,2,1,0:T(8,128)(2,1)S(1)}, u32[]{:S(2)}, u32[]{:S(2)}) collective-permute-start(bf16[2,2,8,32,128]{4,3,2,1,0:T(8,128)(2,1)S(1)} %get-tuple-element.57), channel_id=1, source_target_pairs={{0,128},{128,0},{1,129},{129,1},{2,130},{130,2},{3,131},{131,3},{4... | collective-permute-start | bytes 786440 | tf_op jit(solution)/shard_map/ppermute | solution.py:362
  27.7 6.7 %collective-permute-done.4.got0_ref = bf16[2,8,2,32,128]{4,3,2,1,0:T(8,128)(2,1)S(1)} collective-permute-done((bf16[2,8,2,32,128]{4,3,2,1,0:T(8,128)(2,1)S(1)}, bf16[2,8,2,32,128]{4,3,2,1,0:T(8,128)(2,1)S(1)}, u32[]{:S(2)}, u32[]{:S(2)}) %collective-permute-start.4) | collective-permute-done | bytes 262176 | tf_op jit(solution)/shard_map/ppermute | solution.py:362
  34.6 1.7 %collective-permute-start.6 = (bf16[2,8,32,128]{3,2,1,0:T(8,128)(2,1)S(1)}, bf16[2,8,32,128]{3,2,1,0:T(8,128)(2,1)S(1)}, u32[]{:S(2)}, u32[]{:S(2)}) collective-permute-start(bf16[2,8,32,128]{3,2,1,0:T(8,128)(2,1)S(1)} %get-tuple-element.59), channel_id=1, source_target_pairs={{0,128},{128,0},{1,129},{129,1},{2,130},{130,2},{3,131},{131,3},{4... | collective-permute-start | bytes 393224 | tf_op jit(solution)/shard_map/ppermute | solution.py:362
  36.2 1.6 %collective-permute-start.7 = (bf16[2,8,32,128]{3,2,1,0:T(8,128)(2,1)S(1)}, bf16[2,8,32,128]{3,2,1,0:T(8,128)(2,1)S(1)}, u32[]{:S(2)}, u32[]{:S(2)}) collective-permute-start(bf16[2,8,32,128]{3,2,1,0:T(8,128)(2,1)S(1)} %get-tuple-element.60), channel_id=1, source_target_pairs={{0,16},{16,0},{1,17},{17,1},{2,18},{18,2},{3,19},{19,3},{4,20},{20... | collective-permute-start | bytes 393224 | tf_op jit(solution)/shard_map/ppermute | solution.py:362
  37.9 1.7 %collective-permute-done.6.got0_ref = bf16[2,8,32,128]{3,2,1,0:T(8,128)(2,1)S(1)} collective-permute-done((bf16[2,8,32,128]{3,2,1,0:T(8,128)(2,1)S(1)}, bf16[2,8,32,128]{3,2,1,0:T(8,128)(2,1)S(1)}, u32[]{:S(2)}, u32[]{:S(2)}) %collective-permute-start.6) | collective-permute-done | bytes 131104 | tf_op jit(solution)/shard_map/ppermute | solution.py:362
  39.6 1.6 %collective-permute-done.7.got1_ref = bf16[2,8,32,128]{3,2,1,0:T(8,128)(2,1)S(1)} collective-permute-done((bf16[2,8,32,128]{3,2,1,0:T(8,128)(2,1)S(1)}, bf16[2,8,32,128]{3,2,1,0:T(8,128)(2,1)S(1)}, u32[]{:S(2)}, u32[]{:S(2)}) %collective-permute-start.7) | collective-permute-done | bytes 131104 | tf_op jit(solution)/shard_map/ppermute | solution.py:362
  41.2 0.7 %third_sums.1 = bf16[2,2,8,32,128]{4,3,2,1,0:T(8,128)(2,1)} custom-call(f32[2,2,8,32,128]{4,3,2,1,0:T(8,128)S(1)} %get-tuple-element.58.own_ref, bf16[2,8,32,128]{3,2,1,0:T(8,128)(2,1)S(1)} %collective-permute-done.6.got0_ref, bf16[2,8,32,128]{3,2,1,0:T(8,128)(2,1)S(1)} %collective-permute-done.7.got1_ref), custom_call_target="tpu_custom_call" | custom-call | flops 1000000 | bytes 524288 | tf_op jit(solution)/shard_map/third_sums/pallas_call | solution.py:311
  41.9 10.3 %all-to-all-start = ((bf16[32,32,128]{2,1,0:T(8,128)(2,1)}), bf16[32,32,128]{2,1,0:T(8,128)(2,1)S(1)}, u32[]{:S(2)}, u32[]{:S(2)}) async-start(bf16[32,32,128]{2,1,0:T(8,128)(2,1)} %bitcast.3), calls=%async_computation | async-start | bytes 524288 | tf_op jit(solution)/shard_map/all_to_all | solution.py:420
  52.3 3.2 %collective-permute-start.9 = (bf16[2,2,3,18,512]{4,3,2,1,0:T(8,128)(2,1)S(1)}, bf16[2,2,3,18,512]{4,3,2,1,0:T(8,128)(2,1)S(1)}, u32[]{:S(2)}, u32[]{:S(2)}) collective-permute-start(bf16[2,2,3,18,512]{4,3,2,1,0:T(8,128)(2,1)S(1)} %get-tuple-element.63), channel_id=1, source_target_pairs={{0,120},{8,0},{16,8},{24,16},{32,24},{40,32},{48,40},{56,48},{64,5... | collective-permute-start | bytes 663560 | tf_op jit(solution)/shard_map/ppermute | solution.py:362
  55.5 0.6 collective-permute-start.8
  56.0 5.1 %collective-permute-start.10 = (bf16[2,2,3,6,512]{4,3,2,1,0:T(8,128)(2,1)S(1)}, bf16[2,2,3,6,512]{4,3,2,1,0:T(8,128)(2,1)S(1)}, u32[]{:S(2)}, u32[]{:S(2)}) collective-permute-start(bf16[2,2,3,6,512]{4,3,2,1,0:T(8,128)(2,1)S(1)} %get-tuple-element.64), channel_id=1, source_target_pairs={{0,127},{1,120},{2,121},{3,122},{4,123},{5,124},{6,125},{7,126},{8... | collective-permute-start | bytes 221192 | tf_op jit(solution)/shard_map/ppermute | solution.py:372
  61.1 5.1 %all-to-all-done = bf16[32,32,128]{2,1,0:T(8,128)(2,1)S(1)} async-done(((bf16[32,32,128]{2,1,0:T(8,128)(2,1)}), bf16[32,32,128]{2,1,0:T(8,128)(2,1)S(1)}, u32[]{:S(2)}, u32[]{:S(2)}) %all-to-all-start) | async-done | bytes 262176 | tf_op jit(solution)/shard_map/all_to_all | solution.py:420
  66.2 0.2 collective-permute-start.11
  66.5 0.9 %join_outputs.1 = (bf16[1,2,6,24,512]{4,3,2,1,0:T(8,128)(2,1)}, bf16[1,2,6,24,512]{4,3,2,1,0:T(8,128)(2,1)}) custom-call(bf16[2,2,3,18,512]{4,3,2,1,0:T(8,128)(2,1)S(1)} %get-tuple-element.61.own_ref, bf16[2,2,3,6,512]{4,3,2,1,0:T(8,128)(2,1)S(1)} %collective-permute-done.8.right_ref, bf16[2,2,3,18,512]{4,3,2,1,0:T(8,128)(2,1)S(1)} %collective-permute-done.9.lower_ref, ...), custom_call_target="tpu_custom_call" | custom-call | flops 1000 | bytes 1179648 | tf_op jit(solution)/shard_map/join_outputs/pallas_call | solution.py:311
  67.3 2.7 %collective-permute-done.11.other_ref = f32[32,128]{1,0:T(8,128)S(1)} collective-permute-done((f32[32,128]{1,0:T(8,128)S(1)}, f32[32,128]{1,0:T(8,128)S(1)}, u32[]{:S(2)}, u32[]{:S(2)}) %collective-permute-start.11) | collective-permute-done | bytes 16416 | tf_op jit(solution)/shard_map/ppermute | solution.py:362
  70.1 0.6 last_sum.1
  (24 shorter events, 0.6 us)
Async XLA Ops:
  0.6 14.4 %copy-start.5 = (bf16[1,2,6,24,512]{4,3,2,1,0:T(8,128)(2,1)S(1)}, bf16[1,2,6,24,512]{4,3,2,1,0:T(8,128)(2,1)}, u32[]{:S(2)}) copy-start(bf16[1,2,6,24,512]{4,3,2,1,0:T(8,128)(2,1)} %own_u_ref.1) | copy-start | bytes 884740
  0.6 14.4 %copy-start.4 = (bf16[1,2,6,24,512]{4,3,2,1,0:T(8,128)(2,1)S(1)}, bf16[1,2,6,24,512]{4,3,2,1,0:T(8,128)(2,1)}, u32[]{:S(2)}) copy-start(bf16[1,2,6,24,512]{4,3,2,1,0:T(8,128)(2,1)} %own_x_ref.1) | copy-start | bytes 884740
  1.9 9.4 %collective-permute-start.1 = (bf16[2,2,3,6,512]{4,3,2,1,0:T(8,128)(2,1)S(1)}, bf16[2,2,3,6,512]{4,3,2,1,0:T(8,128)(2,1)S(1)}, u32[]{:S(2)}, u32[]{:S(2)}) collective-permute-start(bf16[2,2,3,6,512]{4,3,2,1,0:T(8,128)(2,1)S(1)} %get-tuple-element.38), channel_id=1, source_target_pairs={{0,9},{1,10},{2,11},{3,12},{4,13},{5,14},{6,15},{7,8},{8,17},{9,18... | collective-permute-start | bytes 221192 | tf_op jit(solution)/shard_map/ppermute | solution.py:372
  3.3 7.9 %collective-permute-start.2 = (bf16[2,2,3,6,512]{4,3,2,1,0:T(8,128)(2,1)S(1)}, bf16[2,2,3,6,512]{4,3,2,1,0:T(8,128)(2,1)S(1)}, u32[]{:S(2)}, u32[]{:S(2)}) collective-permute-start(bf16[2,2,3,6,512]{4,3,2,1,0:T(8,128)(2,1)S(1)} %get-tuple-element.39), channel_id=1, source_target_pairs={{0,1},{1,2},{2,3},{3,4},{4,5},{5,6},{6,7},{7,0},{8,9},{9,10},{10,1... | collective-permute-start | bytes 221192 | tf_op jit(solution)/shard_map/ppermute | solution.py:362
  5.3 9.8 %collective-permute-start = (bf16[2,2,3,18,512]{4,3,2,1,0:T(8,128)(2,1)S(1)}, bf16[2,2,3,18,512]{4,3,2,1,0:T(8,128)(2,1)S(1)}, u32[]{:S(2)}, u32[]{:S(2)}) collective-permute-start(bf16[2,2,3,18,512]{4,3,2,1,0:T(8,128)(2,1)S(1)} %get-tuple-element.37), channel_id=1, source_target_pairs={{0,8},{8,16},{16,24},{24,32},{32,40},{40,48},{48,56},{56,64},{64,7... | collective-permute-start | bytes 663560 | tf_op jit(solution)/shard_map/ppermute | solution.py:362
  7.8 1.4 %copy-start = (bf16[512,1536]{1,0:T(8,128)(2,1)S(1)}, bf16[512,1536]{1,0:T(8,128)(2,1)}, u32[]{:S(2)}) copy-start(bf16[512,1536]{1,0:T(8,128)(2,1)} %qkv_ref.3) | copy-start | bytes 4718596
  9.2 1.0 %copy-start.2 = (bf16[512,512]{1,0:T(8,128)(2,1)S(1)}, bf16[512,512]{1,0:T(8,128)(2,1)}, u32[]{:S(2)}) copy-start(bf16[512,512]{1,0:T(8,128)(2,1)} %proj_ref.3) | copy-start | bytes 1572868
  15.0 8.1 %copy-start.1 = (bf16[512,1536]{1,0:T(8,128)(2,1)S(1)}, bf16[512,1536]{1,0:T(8,128)(2,1)}, u32[]{:S(2)}) copy-start(bf16[512,1536]{1,0:T(8,128)(2,1)} %qkv_ref.3) | copy-start | bytes 4718596
  15.0 8.1 %copy-start.3 = (bf16[512,512]{1,0:T(8,128)(2,1)S(1)}, bf16[512,512]{1,0:T(8,128)(2,1)}, u32[]{:S(2)}) copy-start(bf16[512,512]{1,0:T(8,128)(2,1)} %proj_ref.3) | copy-start | bytes 1572868
  22.8 2.9 %collective-permute-start.3 = (bf16[32,2,64,128]{3,2,1,0:T(8,128)(2,1)S(1)}, bf16[32,2,64,128]{3,2,1,0:T(8,128)(2,1)S(1)}, u32[]{:S(2)}, u32[]{:S(2)}) collective-permute-start(bf16[32,2,64,128]{3,2,1,0:T(8,128)(2,1)S(1)} %get-tuple-element.53), channel_id=1, source_target_pairs={{0,8},{8,0},{1,9},{9,1},{2,10},{10,2},{3,11},{11,3},{4,12},{12,4},... | collective-permute-start | bytes 3145736 | tf_op jit(solution)/shard_map/ppermute | solution.py:362
  25.9 8.4 %collective-permute-start.4 = (bf16[2,8,2,32,128]{4,3,2,1,0:T(8,128)(2,1)S(1)}, bf16[2,8,2,32,128]{4,3,2,1,0:T(8,128)(2,1)S(1)}, u32[]{:S(2)}, u32[]{:S(2)}) collective-permute-start(bf16[2,8,2,32,128]{4,3,2,1,0:T(8,128)(2,1)S(1)} %get-tuple-element.55), channel_id=1, source_target_pairs={{0,16},{16,0},{1,17},{17,1},{2,18},{18,2},{3,19},{19,3},{4,20},{20... | collective-permute-start | bytes 786440 | tf_op jit(solution)/shard_map/ppermute | solution.py:362
  26.0 8.4 %collective-permute-start.5 = (bf16[2,2,8,32,128]{4,3,2,1,0:T(8,128)(2,1)S(1)}, bf16[2,2,8,32,128]{4,3,2,1,0:T(8,128)(2,1)S(1)}, u32[]{:S(2)}, u32[]{:S(2)}) collective-permute-start(bf16[2,2,8,32,128]{4,3,2,1,0:T(8,128)(2,1)S(1)} %get-tuple-element.57), channel_id=1, source_target_pairs={{0,128},{128,0},{1,129},{129,1},{2,130},{130,2},{3,131},{131,3},{4... | collective-permute-start | bytes 786440 | tf_op jit(solution)/shard_map/ppermute | solution.py:362
  34.6 5.1 %collective-permute-start.6 = (bf16[2,8,32,128]{3,2,1,0:T(8,128)(2,1)S(1)}, bf16[2,8,32,128]{3,2,1,0:T(8,128)(2,1)S(1)}, u32[]{:S(2)}, u32[]{:S(2)}) collective-permute-start(bf16[2,8,32,128]{3,2,1,0:T(8,128)(2,1)S(1)} %get-tuple-element.59), channel_id=1, source_target_pairs={{0,128},{128,0},{1,129},{129,1},{2,130},{130,2},{3,131},{131,3},{4... | collective-permute-start | bytes 393224 | tf_op jit(solution)/shard_map/ppermute | solution.py:362
  36.2 5.0 %collective-permute-start.7 = (bf16[2,8,32,128]{3,2,1,0:T(8,128)(2,1)S(1)}, bf16[2,8,32,128]{3,2,1,0:T(8,128)(2,1)S(1)}, u32[]{:S(2)}, u32[]{:S(2)}) collective-permute-start(bf16[2,8,32,128]{3,2,1,0:T(8,128)(2,1)S(1)} %get-tuple-element.60), channel_id=1, source_target_pairs={{0,16},{16,0},{1,17},{17,1},{2,18},{18,2},{3,19},{19,3},{4,20},{20... | collective-permute-start | bytes 393224 | tf_op jit(solution)/shard_map/ppermute | solution.py:362
  41.9 24.2 %all-to-all-start = ((bf16[32,32,128]{2,1,0:T(8,128)(2,1)}), bf16[32,32,128]{2,1,0:T(8,128)(2,1)S(1)}, u32[]{:S(2)}, u32[]{:S(2)}) async-start(bf16[32,32,128]{2,1,0:T(8,128)(2,1)} %bitcast.3), calls=%async_computation | async-start | bytes 524288 | tf_op jit(solution)/shard_map/all_to_all | solution.py:420
  52.3 14.2 %collective-permute-start.9 = (bf16[2,2,3,18,512]{4,3,2,1,0:T(8,128)(2,1)S(1)}, bf16[2,2,3,18,512]{4,3,2,1,0:T(8,128)(2,1)S(1)}, u32[]{:S(2)}, u32[]{:S(2)}) collective-permute-start(bf16[2,2,3,18,512]{4,3,2,1,0:T(8,128)(2,1)S(1)} %get-tuple-element.63), channel_id=1, source_target_pairs={{0,120},{8,0},{16,8},{24,16},{32,24},{40,32},{48,40},{56,48},{64,5... | collective-permute-start | bytes 663560 | tf_op jit(solution)/shard_map/ppermute | solution.py:362
  55.5 11.0 %collective-permute-start.8 = (bf16[2,2,3,6,512]{4,3,2,1,0:T(8,128)(2,1)S(1)}, bf16[2,2,3,6,512]{4,3,2,1,0:T(8,128)(2,1)S(1)}, u32[]{:S(2)}, u32[]{:S(2)}) collective-permute-start(bf16[2,2,3,6,512]{4,3,2,1,0:T(8,128)(2,1)S(1)} %get-tuple-element.62), channel_id=1, source_target_pairs={{0,7},{1,0},{2,1},{3,2},{4,3},{5,4},{6,5},{7,6},{8,15},{9,8},{10,9... | collective-permute-start | bytes 221192 | tf_op jit(solution)/shard_map/ppermute | solution.py:362
  56.0 10.5 %collective-permute-start.10 = (bf16[2,2,3,6,512]{4,3,2,1,0:T(8,128)(2,1)S(1)}, bf16[2,2,3,6,512]{4,3,2,1,0:T(8,128)(2,1)S(1)}, u32[]{:S(2)}, u32[]{:S(2)}) collective-permute-start(bf16[2,2,3,6,512]{4,3,2,1,0:T(8,128)(2,1)S(1)} %get-tuple-element.64), channel_id=1, source_target_pairs={{0,127},{1,120},{2,121},{3,122},{4,123},{5,124},{6,125},{7,126},{8... | collective-permute-start | bytes 221192 | tf_op jit(solution)/shard_map/ppermute | solution.py:372
  66.2 3.8 %collective-permute-start.11 = (f32[32,128]{1,0:T(8,128)S(1)}, f32[32,128]{1,0:T(8,128)S(1)}, u32[]{:S(2)}, u32[]{:S(2)}) collective-permute-start(f32[32,128]{1,0:T(8,128)S(1)} %convert_reduce_fusion.share_ref), channel_id=1, source_target_pairs={{0,128},{128,0},{1,129},{129,1},{2,130},{130,2},{3,131},{131,3},{4... | collective-permute-start | bytes 49160 | tf_op jit(solution)/shard_map/ppermute | solution.py:362

commit v5 on v3

--- a/solution.py
+++ b/solution.py
@@ -186,15 +186,21 @@
     sum_ref[...] = (own_ref[...] + got_ref[...].astype(jnp.float32)).astype(jnp.bfloat16)
 
 
+def added(parts_ref):
+    total = parts_ref[0].astype(jnp.float32)
+    for at in range(1, parts_ref.shape[0]):
+        total = total + parts_ref[at].astype(jnp.float32)
+    return total
+
+
 def sum_kernel(parts_ref, sum_ref):
-    total = parts_ref[0].astype(jnp.float32)
-    for part in range(1, parts_ref.shape[0]):
-        total = total + parts_ref[part].astype(jnp.float32)
-    sum_ref[...] = total.astype(sum_ref.dtype)
-
-
-def last_kernel(share_ref, other_ref, qkv_ref, proj_ref):
-    total = share_ref[...] + other_ref[...]
+    total = added(parts_ref).astype(jnp.bfloat16)
+    sum_ref[0] = total
+    sum_ref[1] = total
+
+
+def last_kernel(parts_ref, qkv_ref, proj_ref):
+    total = added(parts_ref)
     for tile in range(16):
         piece = total[tile * 4:tile * 4 + 4, :]
         if tile < 12:
@@ -377,12 +383,10 @@
     corner = diagonal(corner, -1)
     lower = passed_along(upper, LAT, -1)
     right = passed_along(left, "lon", -1)
-    (sums,) = call(sum_kernel, "sum_parts", ((512, 128),), (), 1_000_000, spread, placed=True)
-    spread = lax.all_to_all(sums.reshape(8, 64, 128), "lon", 0, 0, tiled=True)
-    share = jnp.sum(spread.astype(jnp.float32), 0)
-    other = passed_along(share, "dp", 1)
+    (sums,) = call(sum_kernel, "sum_parts", ((2, 512, 128),), (), 1_000_000, spread, placed=True)
+    spread = lax.all_to_all(sums.reshape(16, 64, 128), ("dp", "lon"), 0, 0, tiled=True)
     grad_qkv, grad_proj = call(
-        last_kernel, "last_sum", ((4, 3 * D), (4, D)), (), 1000, share, other,
+        last_kernel, "last_sum", ((4, 3 * D), (4, D)), (), 1000, spread,
         dtypes=(jnp.float32,) * 2, limit=4,
     )
     output, grad_inputs = call(

time: 69.6 us -> 70.4 us (1.011)
  the two profiles are of different devices: /device:TPU:32 before, /device:TPU:1 now
where the time goes in v5:
time: 70.4 us; the launch traced here: 70 us
  starting transfers between devices  24.4 us (35%)
  blocking collectives  19.7 us (28%)
  Pallas kernels  13.8 us (20%)
  waiting for transfers between devices  7.76 us (11%)
  local copies, waits for them, and re-layouts  2.86 us (4%)
  other arithmetic  0.76 us (1%)
  between operations  0.74 us (1%)
    all_to_all x1, blocking collectives, per_device(): lax.all_to_all(sums.reshape(8, 512, 128), ('yh', 'x'), 0, 0, tiled=True)  19.7 us
    pallas_call x7, Pallas kernels, call(): pl.pallas_call(kernel, out_shape=tuple((make(shape, dtype) for shape, dty...  13.7 us
    ppermute x5, starting transfers between devices, passed_along(): return lax.ppermute(value, axis, pairs)  11.5 us
    all_to_all x1, starting transfers between devices, per_device(): lax.all_to_all(sums.reshape(16, 64, 128), ('dp', 'lon'), 0, 0, tiled=True)  7.46 us
    ppermute x2, starting transfers between devices, diagonal(): return lax.ppermute(value, (*LAT, 'lon'), pairs)  5.46 us
    ppermute x2, waiting for transfers between devices, diagonal(): return lax.ppermute(value, (*LAT, 'lon'), pairs)  4.53 us
    ppermute x5, waiting for transfers between devices, passed_along(): return lax.ppermute(value, axis, pairs)  3.22 us
    unnamed x12, local copies, waits for them, and re-layouts  2.47 us
  transfers between devices with their start and end apart: 8, of which 5 were waited for; matrix products, arithmetic and copies ran while one was open for 2% of the time, Pallas kernels for 4%

profile of v5, /device:TPU:1, one launch (start us, length us, event | category | flops | bytes accessed | tf_op | source)
XLA Modules:
  0.0 70.0 jit_solution(16248241958033131079)
XLA Ops:
  0.7 1.2 %cut_halos.1 = (bf16[2,2,3,18,512]{4,3,2,1,0:T(8,128)(2,1)S(1)}, bf16[2,2,3,6,512]{4,3,2,1,0:T(8,128)(2,1)S(1)}, bf16[2,2,3,6,512]{4,3,2,1,0:T(8,128)(2,1)S(1)}) custom-call(bf16[1,2,6,24,512]{4,3,2,1,0:T(8,128)(2,1)} %own_x_ref.1, bf16[1,2,6,24,512]{4,3,2,1,0:T(8,128)(2,1)} %own_u_ref.1), custom_call_target="tpu_custom_call" | custom-call | flops 1000 | bytes 737280 | tf_op jit(solution)/shard_map/cut_halos/pallas_call | solution.py:287
  1.9 4.0 %collective-permute-start.1 = (bf16[2,2,3,6,512]{4,3,2,1,0:T(8,128)(2,1)S(1)}, bf16[2,2,3,6,512]{4,3,2,1,0:T(8,128)(2,1)S(1)}, u32[]{:S(2)}, u32[]{:S(2)}) collective-permute-start(bf16[2,2,3,6,512]{4,3,2,1,0:T(8,128)(2,1)S(1)} %get-tuple-element.31), channel_id=1, source_target_pairs={{0,9},{1,10},{2,11},{3,12},{4,13},{5,14},{6,15},{7,8},{8,17},{9,18... | collective-permute-start | bytes 221192 | tf_op jit(solution)/shard_map/ppermute | solution.py:348
  5.9 1.6 %collective-permute-start.2 = (bf16[2,2,3,6,512]{4,3,2,1,0:T(8,128)(2,1)S(1)}, bf16[2,2,3,6,512]{4,3,2,1,0:T(8,128)(2,1)S(1)}, u32[]{:S(2)}, u32[]{:S(2)}) collective-permute-start(bf16[2,2,3,6,512]{4,3,2,1,0:T(8,128)(2,1)S(1)} %get-tuple-element.32), channel_id=1, source_target_pairs={{0,1},{1,2},{2,3},{3,4},{4,5},{5,6},{6,7},{7,0},{8,9},{9,10},{10,1... | collective-permute-start | bytes 221192 | tf_op jit(solution)/shard_map/ppermute | solution.py:338
  7.6 0.3 collective-permute-start
  7.9 0.8 %broadcast_add_fusion = s32[6,24]{1,0:T(8,128)S(1)} fusion(s32[6,24]{1,0:T(8,128)} %param.7, s32[6]{0:T(128)S(1)} %and_select_fusion), kind=kLoop, calls=%fused_computation.1 | loop fusion | flops 144 | bytes 1176 | tf_op jit(solution)/shard_map/add | solution.py:365
  8.6 0.1 reshape.31
  8.7 0.1 tile.12
  8.8 0.1 tile.14.lrow_ref
  8.9 0.1 tile.16.lcol_ref
  9.0 0.0 copy-start
  9.0 1.4 %copy-done = bf16[512,1536]{1,0:T(8,128)(2,1)S(1)} copy-done((bf16[512,1536]{1,0:T(8,128)(2,1)S(1)}, bf16[512,1536]{1,0:T(8,128)(2,1)}, u32[]{:S(2)}) %copy-start) | copy-done | bytes 1572888
  10.4 1.0 %copy-done.2 = bf16[512,512]{1,0:T(8,128)(2,1)S(1)} copy-done((bf16[512,512]{1,0:T(8,128)(2,1)S(1)}, bf16[512,512]{1,0:T(8,128)(2,1)}, u32[]{:S(2)}) %copy-start.2) | copy-done | bytes 524312
  11.5 0.2 stage_weights.1
  11.7 0.6 collective-permute-done.1.corner_ref
  12.3 0.7 %collective-permute-done.2.left_ref = bf16[2,2,3,6,512]{4,3,2,1,0:T(8,128)(2,1)S(1)} collective-permute-done((bf16[2,2,3,6,512]{4,3,2,1,0:T(8,128)(2,1)S(1)}, bf16[2,2,3,6,512]{4,3,2,1,0:T(8,128)(2,1)S(1)}, u32[]{:S(2)}, u32[]{:S(2)}) %collective-permute-start.2) | collective-permute-done | bytes 73760 | tf_op jit(solution)/shard_map/ppermute | solution.py:338
  13.0 0.0 copy-start.1
  13.0 0.0 copy-start.3
  13.1 7.8 %window_attention.1 = (bf16[32,2,64,128]{3,2,1,0:T(8,128)(2,1)S(1)}, bf16[288,1536]{1,0:T(8,128)(2,1)S(1)}, bf16[288,512]{1,0:T(8,128)(2,1)S(1)}, bf16[256,288]{...) custom-call(bf16[1,2,6,24,512]{4,3,2,1,0:T(8,128)(2,1)S(1)} %copy-do, ...), custom_call_target="tpu_custom_call" | custom-call | flops 5000000000 | bytes 6225920 | tf_op jit(solution)/shard_map/window_attention/pallas_call | solution.py:287
  20.8 4.8 %collective-permute-start.3 = (bf16[32,2,64,128]{3,2,1,0:T(8,128)(2,1)S(1)}, bf16[32,2,64,128]{3,2,1,0:T(8,128)(2,1)S(1)}, u32[]{:S(2)}, u32[]{:S(2)}) collective-permute-start(bf16[32,2,64,128]{3,2,1,0:T(8,128)(2,1)S(1)} %get-tuple-element.46), channel_id=1, source_target_pairs={{0,8},{8,0},{1,9},{9,1},{2,10},{10,2},{3,11},{11,3},{4,12},{12,4},... | collective-permute-start | bytes 3145736 | tf_op jit(solution)/shard_map/ppermute | solution.py:338
  25.7 2.1 %own_half_and_outputs.1 = (f32[32,2,64,128]{3,2,1,0:T(8,128)S(1)}, bf16[2,2,3,18,512]{4,3,2,1,0:T(8,128)(2,1)S(1)}, bf16[2,2,3,6,512]{4,3,2,1,0:T(8,128)(2,1)S(1...) custom-call(bf16[256,288]{1,0:T(8,128)(2,1)S(1)} %get-tuple-element.35.n_ref, ...), custom_call_target="tpu_custom_call" | custom-call | flops 600000000 | bytes 3276800 | tf_op jit(solution)/shard_map/own_half_and_outputs/pallas_call | solution.py:287
  27.8 0.1 collective-permute-done.3.got_ref
  27.9 0.2 add_halves.1
  28.1 19.7 %all_to_all.10.parts_ref = bf16[8,512,128]{2,1,0:T(8,128)(2,1)S(1)} all-to-all(bf16[8,512,128]{2,1,0:T(8,128)(2,1)S(1)} %bitcast.5), channel_id=1, replica_groups=mesh['dp'=2,'yh'=2,'x'=4,'core'=2,'lon'=8] {'yh','x'}, dimensions={0} | all-to-all | bytes 2097152 | tf_op jit(solution)/shard_map/all_to_all | solution.py:382
  47.8 0.8 %sum_parts.1 = bf16[2,512,128]{2,1,0:T(8,128)(2,1)} custom-call(bf16[8,512,128]{2,1,0:T(8,128)(2,1)S(1)} %all_to_all.10.parts_ref), custom_call_target="tpu_custom_call" | custom-call | flops 1000000 | bytes 524288 | tf_op jit(solution)/shard_map/sum_parts/pallas_call | solution.py:287
  48.7 7.5 %all-to-all-start.1 = ((bf16[16,64,128]{2,1,0:T(8,128)(2,1)}), bf16[16,64,128]{2,1,0:T(8,128)(2,1)S(1)}, u32[]{:S(2)}, u32[]{:S(2)}) async-start(bf16[16,64,128]{2,1,0:T(8,128)(2,1)} %bitcast.2), calls=%async_computation.1 | async-start | bytes 524288 | tf_op jit(solution)/shard_map/all_to_all | solution.py:387
  56.1 1.9 %collective-permute-start.5 = (bf16[2,2,3,18,512]{4,3,2,1,0:T(8,128)(2,1)S(1)}, bf16[2,2,3,18,512]{4,3,2,1,0:T(8,128)(2,1)S(1)}, u32[]{:S(2)}, u32[]{:S(2)}) collective-permute-start(bf16[2,2,3,18,512]{4,3,2,1,0:T(8,128)(2,1)S(1)} %get-tuple-element.49), channel_id=1, source_target_pairs={{0,120},{8,0},{16,8},{24,16},{32,24},{40,32},{48,40},{56,48},{64,5... | collective-permute-start | bytes 663560 | tf_op jit(solution)/shard_map/ppermute | solution.py:338
  58.1 2.8 %collective-permute-start.4 = (bf16[2,2,3,6,512]{4,3,2,1,0:T(8,128)(2,1)S(1)}, bf16[2,2,3,6,512]{4,3,2,1,0:T(8,128)(2,1)S(1)}, u32[]{:S(2)}, u32[]{:S(2)}) collective-permute-start(bf16[2,2,3,6,512]{4,3,2,1,0:T(8,128)(2,1)S(1)} %get-tuple-element.48), channel_id=1, source_target_pairs={{0,7},{1,0},{2,1},{3,2},{4,3},{5,4},{6,5},{7,6},{8,15},{9,8},{10,9... | collective-permute-start | bytes 221192 | tf_op jit(solution)/shard_map/ppermute | solution.py:338
  60.9 1.4 %collective-permute-start.6 = (bf16[2,2,3,6,512]{4,3,2,1,0:T(8,128)(2,1)S(1)}, bf16[2,2,3,6,512]{4,3,2,1,0:T(8,128)(2,1)S(1)}, u32[]{:S(2)}, u32[]{:S(2)}) collective-permute-start(bf16[2,2,3,6,512]{4,3,2,1,0:T(8,128)(2,1)S(1)} %get-tuple-element.50), channel_id=1, source_target_pairs={{0,127},{1,120},{2,121},{3,122},{4,123},{5,124},{6,125},{7,126},{8... | collective-permute-start | bytes 221192 | tf_op jit(solution)/shard_map/ppermute | solution.py:348
  62.3 2.3 %collective-permute-done.4.right_ref = bf16[2,2,3,6,512]{4,3,2,1,0:T(8,128)(2,1)S(1)} collective-permute-done((bf16[2,2,3,6,512]{4,3,2,1,0:T(8,128)(2,1)S(1)}, bf16[2,2,3,6,512]{4,3,2,1,0:T(8,128)(2,1)S(1)}, u32[]{:S(2)}, u32[]{:S(2)}) %collective-permute-start.4) | collective-permute-done | bytes 73760 | tf_op jit(solution)/shard_map/ppermute | solution.py:338
  64.6 3.9 %collective-permute-done.6.corner_ref = bf16[2,2,3,6,512]{4,3,2,1,0:T(8,128)(2,1)S(1)} collective-permute-done((bf16[2,2,3,6,512]{4,3,2,1,0:T(8,128)(2,1)S(1)}, bf16[2,2,3,6,512]{4,3,2,1,0:T(8,128)(2,1)S(1)}, u32[]{:S(2)}, u32[]{:S(2)}) %collective-permute-start.6) | collective-permute-done | bytes 73760 | tf_op jit(solution)/shard_map/ppermute | solution.py:348
  68.5 0.8 %join_outputs.1 = (bf16[1,2,6,24,512]{4,3,2,1,0:T(8,128)(2,1)}, bf16[1,2,6,24,512]{4,3,2,1,0:T(8,128)(2,1)}) custom-call(bf16[2,2,3,18,512]{4,3,2,1,0:T(8,128)(2,1)S(1)} %get-tuple-element.47.own_ref, bf16[2,2,3,6,512]{4,3,2,1,0:T(8,128)(2,1)S(1)} %collective-permute-done.4.right_ref, bf16[2,2,3,18,512]{4,3,2,1,0:T(8,128)(2,1)S(1)} %collective-permute-done.5.lower_ref, ...), custom_call_target="tpu_custom_call" | custom-call | flops 1000 | bytes 1179648 | tf_op jit(solution)/shard_map/join_outputs/pallas_call | solution.py:287
  69.4 0.6 last_sum.1
  (13 shorter events, 0.0 us)
Async XLA Ops:
  0.6 12.4 %copy-start.5 = (bf16[1,2,6,24,512]{4,3,2,1,0:T(8,128)(2,1)S(1)}, bf16[1,2,6,24,512]{4,3,2,1,0:T(8,128)(2,1)}, u32[]{:S(2)}) copy-start(bf16[1,2,6,24,512]{4,3,2,1,0:T(8,128)(2,1)} %own_u_ref.1) | copy-start | bytes 884740
  0.6 12.4 %copy-start.4 = (bf16[1,2,6,24,512]{4,3,2,1,0:T(8,128)(2,1)S(1)}, bf16[1,2,6,24,512]{4,3,2,1,0:T(8,128)(2,1)}, u32[]{:S(2)}) copy-start(bf16[1,2,6,24,512]{4,3,2,1,0:T(8,128)(2,1)} %own_x_ref.1) | copy-start | bytes 884740
  1.9 10.4 %collective-permute-start.1 = (bf16[2,2,3,6,512]{4,3,2,1,0:T(8,128)(2,1)S(1)}, bf16[2,2,3,6,512]{4,3,2,1,0:T(8,128)(2,1)S(1)}, u32[]{:S(2)}, u32[]{:S(2)}) collective-permute-start(bf16[2,2,3,6,512]{4,3,2,1,0:T(8,128)(2,1)S(1)} %get-tuple-element.31), channel_id=1, source_target_pairs={{0,9},{1,10},{2,11},{3,12},{4,13},{5,14},{6,15},{7,8},{8,17},{9,18... | collective-permute-start | bytes 221192 | tf_op jit(solution)/shard_map/ppermute | solution.py:348
  5.9 7.1 %collective-permute-start.2 = (bf16[2,2,3,6,512]{4,3,2,1,0:T(8,128)(2,1)S(1)}, bf16[2,2,3,6,512]{4,3,2,1,0:T(8,128)(2,1)S(1)}, u32[]{:S(2)}, u32[]{:S(2)}) collective-permute-start(bf16[2,2,3,6,512]{4,3,2,1,0:T(8,128)(2,1)S(1)} %get-tuple-element.32), channel_id=1, source_target_pairs={{0,1},{1,2},{2,3},{3,4},{4,5},{5,6},{6,7},{7,0},{8,9},{9,10},{10,1... | collective-permute-start | bytes 221192 | tf_op jit(solution)/shard_map/ppermute | solution.py:338
  7.6 5.4 %collective-permute-start = (bf16[2,2,3,18,512]{4,3,2,1,0:T(8,128)(2,1)S(1)}, bf16[2,2,3,18,512]{4,3,2,1,0:T(8,128)(2,1)S(1)}, u32[]{:S(2)}, u32[]{:S(2)}) collective-permute-start(bf16[2,2,3,18,512]{4,3,2,1,0:T(8,128)(2,1)S(1)} %get-tuple-element.30), channel_id=1, source_target_pairs={{0,8},{8,16},{16,24},{24,32},{32,40},{40,48},{48,56},{56,64},{64,7... | collective-permute-start | bytes 663560 | tf_op jit(solution)/shard_map/ppermute | solution.py:338
  9.0 1.4 %copy-start = (bf16[512,1536]{1,0:T(8,128)(2,1)S(1)}, bf16[512,1536]{1,0:T(8,128)(2,1)}, u32[]{:S(2)}) copy-start(bf16[512,1536]{1,0:T(8,128)(2,1)} %qkv_ref.3) | copy-start | bytes 4718596
  10.4 1.0 %copy-start.2 = (bf16[512,512]{1,0:T(8,128)(2,1)S(1)}, bf16[512,512]{1,0:T(8,128)(2,1)}, u32[]{:S(2)}) copy-start(bf16[512,512]{1,0:T(8,128)(2,1)} %proj_ref.3) | copy-start | bytes 1572868
  13.0 12.6 %copy-start.1 = (bf16[512,1536]{1,0:T(8,128)(2,1)S(1)}, bf16[512,1536]{1,0:T(8,128)(2,1)}, u32[]{:S(2)}) copy-start(bf16[512,1536]{1,0:T(8,128)(2,1)} %qkv_ref.3) | copy-start | bytes 4718596
  13.0 12.6 %copy-start.3 = (bf16[512,512]{1,0:T(8,128)(2,1)S(1)}, bf16[512,512]{1,0:T(8,128)(2,1)}, u32[]{:S(2)}) copy-start(bf16[512,512]{1,0:T(8,128)(2,1)} %proj_ref.3) | copy-start | bytes 1572868
  20.8 7.1 %collective-permute-start.3 = (bf16[32,2,64,128]{3,2,1,0:T(8,128)(2,1)S(1)}, bf16[32,2,64,128]{3,2,1,0:T(8,128)(2,1)S(1)}, u32[]{:S(2)}, u32[]{:S(2)}) collective-permute-start(bf16[32,2,64,128]{3,2,1,0:T(8,128)(2,1)S(1)} %get-tuple-element.46), channel_id=1, source_target_pairs={{0,8},{8,0},{1,9},{9,1},{2,10},{10,2},{3,11},{11,3},{4,12},{12,4},... | collective-permute-start | bytes 3145736 | tf_op jit(solution)/shard_map/ppermute | solution.py:338
  48.7 20.7 %all-to-all-start.1 = ((bf16[16,64,128]{2,1,0:T(8,128)(2,1)}), bf16[16,64,128]{2,1,0:T(8,128)(2,1)S(1)}, u32[]{:S(2)}, u32[]{:S(2)}) async-start(bf16[16,64,128]{2,1,0:T(8,128)(2,1)} %bitcast.2), calls=%async_computation.1 | async-start | bytes 524288 | tf_op jit(solution)/shard_map/all_to_all | solution.py:387
  56.1 12.4 %collective-permute-start.5 = (bf16[2,2,3,18,512]{4,3,2,1,0:T(8,128)(2,1)S(1)}, bf16[2,2,3,18,512]{4,3,2,1,0:T(8,128)(2,1)S(1)}, u32[]{:S(2)}, u32[]{:S(2)}) collective-permute-start(bf16[2,2,3,18,512]{4,3,2,1,0:T(8,128)(2,1)S(1)} %get-tuple-element.49), channel_id=1, source_target_pairs={{0,120},{8,0},{16,8},{24,16},{32,24},{40,32},{48,40},{56,48},{64,5... | collective-permute-start | bytes 663560 | tf_op jit(solution)/shard_map/ppermute | solution.py:338
  58.1 6.6 %collective-permute-start.4 = (bf16[2,2,3,6,512]{4,3,2,1,0:T(8,128)(2,1)S(1)}, bf16[2,2,3,6,512]{4,3,2,1,0:T(8,128)(2,1)S(1)}, u32[]{:S(2)}, u32[]{:S(2)}) collective-permute-start(bf16[2,2,3,6,512]{4,3,2,1,0:T(8,128)(2,1)S(1)} %get-tuple-element.48), channel_id=1, source_target_pairs={{0,7},{1,0},{2,1},{3,2},{4,3},{5,4},{6,5},{7,6},{8,15},{9,8},{10,9... | collective-permute-start | bytes 221192 | tf_op jit(solution)/shard_map/ppermute | solution.py:338
  60.9 7.7 %collective-permute-start.6 = (bf16[2,2,3,6,512]{4,3,2,1,0:T(8,128)(2,1)S(1)}, bf16[2,2,3,6,512]{4,3,2,1,0:T(8,128)(2,1)S(1)}, u32[]{:S(2)}, u32[]{:S(2)}) collective-permute-start(bf16[2,2,3,6,512]{4,3,2,1,0:T(8,128)(2,1)S(1)} %get-tuple-element.50), channel_id=1, source_target_pairs={{0,127},{1,120},{2,121},{3,122},{4,123},{5,124},{6,125},{7,126},{8... | collective-permute-start | bytes 221192 | tf_op jit(solution)/shard_map/ppermute | solution.py:348

commit v6 on v5

--- a/solution.py
+++ b/solution.py
@@ -53,16 +53,24 @@
                     upper_ref[at, level, row - SLAT] = tokens[:-SLON].astype(jnp.bfloat16)
 
 
-def join_kernel(own_ref, right_ref, lower_ref, corner_ref, out_ref, gin_ref):
+def joined(body, side):
+    both = jnp.concatenate([body.astype(jnp.float32), side.astype(jnp.float32)], axis=0)
+    return both.astype(jnp.bfloat16)
+
+
+def rows_kernel(own_ref, right_ref, rows_ref):
+    for at in range(2):
+        for level in range(LEV):
+            for row in range(SLAT):
+                rows_ref[at, level, row] = joined(own_ref[at, level, row], right_ref[at, level, row])
+
+
+def join_kernel(own_ref, right_ref, lower_ref, out_ref, gin_ref):
     for at, ref in enumerate((out_ref, gin_ref)):
         for level in range(LEV):
-            for row in range(WLAT):
-                if row < SLAT:
-                    body, side = own_ref[at, level, row], right_ref[at, level, row]
-                else:
-                    body, side = lower_ref[at, level, row - SLAT], corner_ref[at, level, row - SLAT]
-                both = jnp.concatenate([body.astype(jnp.float32), side.astype(jnp.float32)], axis=0)
-                ref[0, level, row] = both.astype(jnp.bfloat16)
+            for row in range(SLAT):
+                ref[0, level, row] = joined(own_ref[at, level, SLAT + row], right_ref[at, level, SLAT + row])
+                ref[0, level, SLAT + row] = lower_ref[at, level, row]
 
 
 def assemble(target_ref, at, own_ref, upper_ref, corner_ref, left_ref):
@@ -237,23 +245,18 @@
 
 
 def part(value, at, refs):
-    own_ref, left_ref, upper_ref, corner_ref = refs
+    own_ref, left_ref = refs
     for level in range(LEV):
         for row in range(WLAT):
             base = (level * WLAT + row) * WLON
             tokens = jnp.concatenate([value[base:base + WLON], value[WT + base:WT + base + WLON]], axis=0)
-            side, body = tokens[:SLON].astype(jnp.bfloat16), tokens[SLON:].astype(jnp.bfloat16)
-            if row < SLAT:
-                corner_ref[at, level, row] = side
-                upper_ref[at, level, row] = body
-            else:
-                left_ref[at, level, row - SLAT] = side
-                own_ref[at, level, row - SLAT] = body
+            left_ref[at, level, row] = tokens[:SLON].astype(jnp.bfloat16)
+            own_ref[at, level, row] = tokens[SLON:].astype(jnp.bfloat16)
 
 
 def rest_kernel(
     n_ref, m_ref, gp_ref, u_ref, x_ref, mix_ref, qkv_ref, proj_ref,
-    half_ref, own_ref, left_ref, upper_ref, corner_ref,
+    half_ref, own_ref, left_ref,
     wqkv_ref, wproj_ref, sems,
 ):
     copies = [
@@ -264,7 +267,7 @@
         copy.start()
     grads = jnp.concatenate([dot(n_ref[...], gp_ref[...]), dot(m_ref[...], u_ref[...])], axis=1)
     store_shares(half_ref, grads)
-    refs = (own_ref, left_ref, upper_ref, corner_ref)
+    refs = (own_ref, left_ref)
     x = x_ref[...].astype(jnp.float32)
     copies[0].wait()
     part(x + dot(mix_ref[...], wproj_ref[...]), 0, refs)
@@ -371,27 +374,27 @@
         inputs, cotangent, upper, corner, left, lrow, lcol, *staged(w_qkv, w_proj)
     )
     got = passed_along(send, "core", 1)
-    half, own, left, upper, corner = call(
-        rest_kernel, "own_half_and_outputs", (send.shape, body, side, body, side),
+    half, own, left = call(
+        rest_kernel, "own_half_and_outputs",
+        (send.shape, (2, *inputs.shape[1:3], body[3], D), (2, *inputs.shape[1:3], SLON, D)),
         ((w_qkv.shape, jnp.bfloat16), (w_proj.shape, jnp.bfloat16), ((2,), None)), 600_000_000,
         nkeep, mkeep, gp, u, x, mix, w_qkv, w_proj,
-        dtypes=(jnp.float32,) + (jnp.bfloat16,) * 4, any_args=(6, 7), limit=16,
+        dtypes=(jnp.float32,) + (jnp.bfloat16,) * 2, any_args=(6, 7), limit=16,
     )
     (sums,) = call(add_kernel, "add_halves", (send.shape,), (), 1_000_000, half, got, placed=True)
-    own, left, upper, corner, sums = lax.optimization_barrier((own, left, upper, corner, sums))
+    right = passed_along(left, "lon", -1)
     spread = lax.all_to_all(sums.reshape(8, 512, 128), ("yh", "x"), 0, 0, tiled=True)
-    corner = diagonal(corner, -1)
-    lower = passed_along(upper, LAT, -1)
-    right = passed_along(left, "lon", -1)
+    spread, right = lax.optimization_barrier((spread, right))
     (sums,) = call(sum_kernel, "sum_parts", ((2, 512, 128),), (), 1_000_000, spread, placed=True)
     spread = lax.all_to_all(sums.reshape(16, 64, 128), ("dp", "lon"), 0, 0, tiled=True)
     grad_qkv, grad_proj = call(
         last_kernel, "last_sum", ((4, 3 * D), (4, D)), (), 1000, spread,
         dtypes=(jnp.float32,) * 2, limit=4,
     )
+    (rows,) = call(rows_kernel, "halo_rows", ((2, LEV, SLAT, *inputs.shape[3:]),), (), 1000, own, right, limit=8)
+    lower = passed_along(rows, LAT, -1)
     output, grad_inputs = call(
-        join_kernel, "join_outputs", (inputs.shape, inputs.shape), (), 1000,
-        own, right, lower, corner, limit=8,
+        join_kernel, "join_outputs", (inputs.shape, inputs.shape), (), 1000, own, right, lower, limit=8
     )
     return (output, grad_inputs, grad_qkv, grad_proj)
 

time: 70.4 us -> 68.9 us (0.979)
  the two profiles are of different devices: /device:TPU:1 before, /device:TPU:32 now
where the time goes in v6:
time: 68.9 us; the launch traced here: 68.5 us
  waiting for transfers between devices  31 us (45%)
  starting transfers between devices  18.3 us (27%)
  Pallas kernels  14.8 us (21%)
  local copies, waits for them, and re-layouts  2.86 us (4%)
  other arithmetic  0.76 us (1%)
  between operations  0.74 us (1%)
    ppermute x5, waiting for transfers between devices, passed_along(): return lax.ppermute(value, axis, pairs)  16.5 us
    pallas_call x8, Pallas kernels, call(): pl.pallas_call(kernel, out_shape=tuple((make(shape, dtype) for shape, dty...  14.7 us
    all_to_all x1, waiting for transfers between devices, per_device(): lax.all_to_all(sums.reshape(8, 512, 128), ('yh', 'x'), 0, 0, tiled=True)  9.45 us
    all_to_all x1, starting transfers between devices, per_device(): lax.all_to_all(sums.reshape(16, 64, 128), ('dp', 'lon'), 0, 0, tiled=True)  8.17 us
    all_to_all x1, starting transfers between devices, per_device(): lax.all_to_all(sums.reshape(8, 512, 128), ('yh', 'x'), 0, 0, tiled=True)  4.46 us
    ppermute x5, starting transfers between devices, passed_along(): return lax.ppermute(value, axis, pairs)  4.26 us
    all_to_all x1, waiting for transfers between devices, per_device(): lax.all_to_all(sums.reshape(16, 64, 128), ('dp', 'lon'), 0, 0, tiled=True)  4.13 us
    unnamed x12, local copies, waits for them, and re-layouts  2.46 us
  transfers between devices with their start and end apart: 8, of which 7 were waited for; matrix products, arithmetic and copies ran while one was open for 2% of the time, Pallas kernels for 5%

profile of v6, /device:TPU:32, one launch (start us, length us, event | category | flops | bytes accessed | tf_op | source)
XLA Modules:
  0.0 68.5 jit_solution(2319075315001867419)
XLA Ops:
  0.7 1.2 %cut_halos.1 = (bf16[2,2,3,18,512]{4,3,2,1,0:T(8,128)(2,1)S(1)}, bf16[2,2,3,6,512]{4,3,2,1,0:T(8,128)(2,1)S(1)}, bf16[2,2,3,6,512]{4,3,2,1,0:T(8,128)(2,1)S(1)}) custom-call(bf16[1,2,6,24,512]{4,3,2,1,0:T(8,128)(2,1)} %own_x_ref.1, bf16[1,2,6,24,512]{4,3,2,1,0:T(8,128)(2,1)} %own_u_ref.1), custom_call_target="tpu_custom_call" | custom-call | flops 1000 | bytes 737280 | tf_op jit(solution)/shard_map/cut_halos/pallas_call | solution.py:290
  1.9 1.4 %collective-permute-start.1 = (bf16[2,2,3,6,512]{4,3,2,1,0:T(8,128)(2,1)S(1)}, bf16[2,2,3,6,512]{4,3,2,1,0:T(8,128)(2,1)S(1)}, u32[]{:S(2)}, u32[]{:S(2)}) collective-permute-start(bf16[2,2,3,6,512]{4,3,2,1,0:T(8,128)(2,1)S(1)} %get-tuple-element.26), channel_id=1, source_target_pairs={{0,9},{1,10},{2,11},{3,12},{4,13},{5,14},{6,15},{7,8},{8,17},{9,18... | collective-permute-start | bytes 221192 | tf_op jit(solution)/shard_map/ppermute | solution.py:351
  3.3 1.9 %collective-permute-start.2 = (bf16[2,2,3,6,512]{4,3,2,1,0:T(8,128)(2,1)S(1)}, bf16[2,2,3,6,512]{4,3,2,1,0:T(8,128)(2,1)S(1)}, u32[]{:S(2)}, u32[]{:S(2)}) collective-permute-start(bf16[2,2,3,6,512]{4,3,2,1,0:T(8,128)(2,1)S(1)} %get-tuple-element.27), channel_id=1, source_target_pairs={{0,1},{1,2},{2,3},{3,4},{4,5},{5,6},{6,7},{7,0},{8,9},{9,10},{10,1... | collective-permute-start | bytes 221192 | tf_op jit(solution)/shard_map/ppermute | solution.py:341
  5.3 1.3 %collective-permute-start = (bf16[2,2,3,18,512]{4,3,2,1,0:T(8,128)(2,1)S(1)}, bf16[2,2,3,18,512]{4,3,2,1,0:T(8,128)(2,1)S(1)}, u32[]{:S(2)}, u32[]{:S(2)}) collective-permute-start(bf16[2,2,3,18,512]{4,3,2,1,0:T(8,128)(2,1)S(1)} %get-tuple-element.25), channel_id=1, source_target_pairs={{0,8},{8,16},{16,24},{24,32},{32,40},{40,48},{48,56},{56,64},{64,7... | collective-permute-start | bytes 663560 | tf_op jit(solution)/shard_map/ppermute | solution.py:341
  6.6 0.8 %broadcast_add_fusion = s32[6,24]{1,0:T(8,128)S(1)} fusion(s32[6,24]{1,0:T(8,128)} %param.7, s32[6]{0:T(128)S(1)} %and_select_fusion), kind=kLoop, calls=%fused_computation.1 | loop fusion | flops 144 | bytes 1176 | tf_op jit(solution)/shard_map/add | solution.py:368
  7.3 0.1 reshape.31
  7.4 0.1 tile.12
  7.5 0.1 tile.14.lrow_ref
  7.6 0.1 tile.16.lcol_ref
  7.8 0.0 copy-start
  7.8 1.4 %copy-done = bf16[512,1536]{1,0:T(8,128)(2,1)S(1)} copy-done((bf16[512,1536]{1,0:T(8,128)(2,1)S(1)}, bf16[512,1536]{1,0:T(8,128)(2,1)}, u32[]{:S(2)}) %copy-start) | copy-done | bytes 1572888
  9.2 1.0 %copy-done.2 = bf16[512,512]{1,0:T(8,128)(2,1)S(1)} copy-done((bf16[512,512]{1,0:T(8,128)(2,1)S(1)}, bf16[512,512]{1,0:T(8,128)(2,1)}, u32[]{:S(2)}) %copy-start.2) | copy-done | bytes 524312
  10.2 0.2 stage_weights.1
  10.4 0.9 %collective-permute-done.1.corner_ref = bf16[2,2,3,6,512]{4,3,2,1,0:T(8,128)(2,1)S(1)} collective-permute-done((bf16[2,2,3,6,512]{4,3,2,1,0:T(8,128)(2,1)S(1)}, bf16[2,2,3,6,512]{4,3,2,1,0:T(8,128)(2,1)S(1)}, u32[]{:S(2)}, u32[]{:S(2)}) %collective-permute-start.1) | collective-permute-done | bytes 73760 | tf_op jit(solution)/shard_map/ppermute | solution.py:351
  11.3 0.0 collective-permute-done.2.left_ref
  11.3 3.8 %collective-permute-done.upper_ref = bf16[2,2,3,18,512]{4,3,2,1,0:T(8,128)(2,1)S(1)} collective-permute-done((bf16[2,2,3,18,512]{4,3,2,1,0:T(8,128)(2,1)S(1)}, bf16[2,2,3,18,512]{4,3,2,1,0:T(8,128)(2,1)S(1)}, u32[]{:S(2)}, u32[]{:S(2)}) %collective-permute-start) | collective-permute-done | bytes 221216 | tf_op jit(solution)/shard_map/ppermute | solution.py:341
  15.0 7.8 %window_attention.1 = (bf16[32,2,64,128]{3,2,1,0:T(8,128)(2,1)S(1)}, bf16[288,1536]{1,0:T(8,128)(2,1)S(1)}, bf16[288,512]{1,0:T(8,128)(2,1)S(1)}, bf16[256,288]{...) custom-call(bf16[1,2,6,24,512]{4,3,2,1,0:T(8,128)(2,1)S(1)} %copy-do, ...), custom_call_target="tpu_custom_call" | custom-call | flops 5000000000 | bytes 6225920 | tf_op jit(solution)/shard_map/window_attention/pallas_call | solution.py:290
  22.8 0.3 collective-permute-start.3
  23.1 2.1 %own_half_and_outputs.1 = (f32[32,2,64,128]{3,2,1,0:T(8,128)S(1)}, bf16[2,2,6,18,512]{4,3,2,1,0:T(8,128)(2,1)S(1)}, bf16[2,2,6,6,512]{4,3,2,1,0:T(8,128)(2,1)S(1)}) custom-call(bf16[256,288]{1,0:T(8,128)(2,1)S(1)} %get-tuple-element.30.n_ref, bf16[256,288]{1,0:T(8,128)(2,1)S(1)} %get-tuple-element.31.m_ref, bf16[288,1536]{1,0:T(8,128)(2,1)S(1)} %get-tuple-element.32.gp_ref, ...), custom_call_target="tpu_custom_call" | custom-call | flops 600000000 | bytes 3276800 | tf_op jit(solution)/shard_map/own_half_and_outputs/pallas_call | solution.py:290
  25.3 0.5 collective-permute-done.3.got_ref
  25.8 1.2 %add_halves.1 = bf16[32,2,64,128]{3,2,1,0:T(8,128)(2,1)} custom-call(f32[32,2,64,128]{3,2,1,0:T(8,128)S(1)} %get-tuple-element.37.own_ref, bf16[32,2,64,128]{3,2,1,0:T(8,128)(2,1)S(1)} %collective-permute-done.3.got_ref), custom_call_target="tpu_custom_call" | custom-call | flops 1000000 | bytes 2097152 | tf_op jit(solution)/shard_map/add_halves/pallas_call | solution.py:290
  26.9 4.5 %all-to-all-start = ((bf16[8,512,128]{2,1,0:T(8,128)(2,1)}), bf16[8,512,128]{2,1,0:T(8,128)(2,1)S(1)}, u32[]{:S(2)}, u32[]{:S(2)}) async-start(bf16[8,512,128]{2,1,0:T(8,128)(2,1)} %bitcast.1), calls=%async_computation | async-start | bytes 2097152 | tf_op jit(solution)/shard_map/all_to_all | solution.py:386
  31.4 0.4 collective-permute-start.4
  31.7 7.7 %collective-permute-done.4.right_ref = bf16[2,2,6,6,512]{4,3,2,1,0:T(8,128)(2,1)S(1)} collective-permute-done((bf16[2,2,6,6,512]{4,3,2,1,0:T(8,128)(2,1)S(1)}, bf16[2,2,6,6,512]{4,3,2,1,0:T(8,128)(2,1)S(1)}, u32[]{:S(2)}, u32[]{:S(2)}) %collective-permute-start.4) | collective-permute-done | bytes 147488 | tf_op jit(solution)/shard_map/ppermute | solution.py:341
  39.4 9.5 %all-to-all-done.parts_ref = bf16[8,512,128]{2,1,0:T(8,128)(2,1)S(1)} async-done(((bf16[8,512,128]{2,1,0:T(8,128)(2,1)}), bf16[8,512,128]{2,1,0:T(8,128)(2,1)S(1)}, u32[]{:S(2)}, u32[]{:S(2)}) %all-to-all-start) | async-done | bytes 1048608 | tf_op jit(solution)/shard_map/all_to_all | solution.py:386
  48.9 0.8 %sum_parts.1 = bf16[2,512,128]{2,1,0:T(8,128)(2,1)} custom-call(bf16[8,512,128]{2,1,0:T(8,128)(2,1)S(1)} %all-to-all-done.parts_ref), custom_call_target="tpu_custom_call" | custom-call | flops 1000000 | bytes 524288 | tf_op jit(solution)/shard_map/sum_parts/pallas_call | solution.py:290
  49.7 8.2 %all-to-all-start.1 = ((bf16[16,64,128]{2,1,0:T(8,128)(2,1)}), bf16[16,64,128]{2,1,0:T(8,128)(2,1)S(1)}, u32[]{:S(2)}, u32[]{:S(2)}) async-start(bf16[16,64,128]{2,1,0:T(8,128)(2,1)} %bitcast.2), calls=%async_computation.1 | async-start | bytes 524288 | tf_op jit(solution)/shard_map/all_to_all | solution.py:389
  57.9 0.4 collective-permute-start.5
  58.3 4.6 %collective-permute-done.5.lower_ref = bf16[2,2,3,24,512]{4,3,2,1,0:T(8,128)(2,1)S(1)} collective-permute-done((bf16[2,2,3,24,512]{4,3,2,1,0:T(8,128)(2,1)S(1)}, bf16[2,2,3,24,512]{4,3,2,1,0:T(8,128)(2,1)S(1)}, u32[]{:S(2)}, u32[]{:S(2)}) %collective-permute-start.5) | collective-permute-done | bytes 294944 | tf_op jit(solution)/shard_map/ppermute | solution.py:341
  62.9 0.9 %join_outputs.1 = (bf16[1,2,6,24,512]{4,3,2,1,0:T(8,128)(2,1)}, bf16[1,2,6,24,512]{4,3,2,1,0:T(8,128)(2,1)}) custom-call(bf16[2,2,6,18,512]{4,3,2,1,0:T(8,128)(2,1)S(1)} %get-tuple-element.36.own_ref, bf16[2,2,6,6,512]{4,3,2,1,0:T(8,128)(2,1)S(1)} %collective-permute-done.4.right_ref, bf16[2,2,3,24,512]{4,3,2,1,0:T(8,128)(2,1)S(1)} %collective-permute-done.5.lower_ref), custom_call_target="tpu_custom_call" | custom-call | flops 1000 | bytes 1179648 | tf_op jit(solution)/shard_map/join_outputs/pallas_call | solution.py:290
  63.7 4.1 %all-to-all-done.1.parts_ref = bf16[16,64,128]{2,1,0:T(8,128)(2,1)S(1)} async-done(((bf16[16,64,128]{2,1,0:T(8,128)(2,1)}), bf16[16,64,128]{2,1,0:T(8,128)(2,1)S(1)}, u32[]{:S(2)}, u32[]{:S(2)}) %all-to-all-start.1) | async-done | bytes 262176 | tf_op jit(solution)/shard_map/all_to_all | solution.py:389
  67.9 0.6 last_sum.1
  (13 shorter events, 0.1 us)
Async XLA Ops:
  0.6 14.4 %copy-start.5 = (bf16[1,2,6,24,512]{4,3,2,1,0:T(8,128)(2,1)S(1)}, bf16[1,2,6,24,512]{4,3,2,1,0:T(8,128)(2,1)}, u32[]{:S(2)}) copy-start(bf16[1,2,6,24,512]{4,3,2,1,0:T(8,128)(2,1)} %own_u_ref.1) | copy-start | bytes 884740
  0.6 14.4 %copy-start.4 = (bf16[1,2,6,24,512]{4,3,2,1,0:T(8,128)(2,1)S(1)}, bf16[1,2,6,24,512]{4,3,2,1,0:T(8,128)(2,1)}, u32[]{:S(2)}) copy-start(bf16[1,2,6,24,512]{4,3,2,1,0:T(8,128)(2,1)} %own_x_ref.1) | copy-start | bytes 884740
  1.9 9.4 %collective-permute-start.1 = (bf16[2,2,3,6,512]{4,3,2,1,0:T(8,128)(2,1)S(1)}, bf16[2,2,3,6,512]{4,3,2,1,0:T(8,128)(2,1)S(1)}, u32[]{:S(2)}, u32[]{:S(2)}) collective-permute-start(bf16[2,2,3,6,512]{4,3,2,1,0:T(8,128)(2,1)S(1)} %get-tuple-element.26), channel_id=1, source_target_pairs={{0,9},{1,10},{2,11},{3,12},{4,13},{5,14},{6,15},{7,8},{8,17},{9,18... | collective-permute-start | bytes 221192 | tf_op jit(solution)/shard_map/ppermute | solution.py:351
  3.3 7.9 %collective-permute-start.2 = (bf16[2,2,3,6,512]{4,3,2,1,0:T(8,128)(2,1)S(1)}, bf16[2,2,3,6,512]{4,3,2,1,0:T(8,128)(2,1)S(1)}, u32[]{:S(2)}, u32[]{:S(2)}) collective-permute-start(bf16[2,2,3,6,512]{4,3,2,1,0:T(8,128)(2,1)S(1)} %get-tuple-element.27), channel_id=1, source_target_pairs={{0,1},{1,2},{2,3},{3,4},{4,5},{5,6},{6,7},{7,0},{8,9},{9,10},{10,1... | collective-permute-start | bytes 221192 | tf_op jit(solution)/shard_map/ppermute | solution.py:341
  5.3 9.8 %collective-permute-start = (bf16[2,2,3,18,512]{4,3,2,1,0:T(8,128)(2,1)S(1)}, bf16[2,2,3,18,512]{4,3,2,1,0:T(8,128)(2,1)S(1)}, u32[]{:S(2)}, u32[]{:S(2)}) collective-permute-start(bf16[2,2,3,18,512]{4,3,2,1,0:T(8,128)(2,1)S(1)} %get-tuple-element.25), channel_id=1, source_target_pairs={{0,8},{8,16},{16,24},{24,32},{32,40},{40,48},{48,56},{56,64},{64,7... | collective-permute-start | bytes 663560 | tf_op jit(solution)/shard_map/ppermute | solution.py:341
  7.8 1.4 %copy-start = (bf16[512,1536]{1,0:T(8,128)(2,1)S(1)}, bf16[512,1536]{1,0:T(8,128)(2,1)}, u32[]{:S(2)}) copy-start(bf16[512,1536]{1,0:T(8,128)(2,1)} %qkv_ref.3) | copy-start | bytes 4718596
  9.2 1.0 %copy-start.2 = (bf16[512,512]{1,0:T(8,128)(2,1)S(1)}, bf16[512,512]{1,0:T(8,128)(2,1)}, u32[]{:S(2)}) copy-start(bf16[512,512]{1,0:T(8,128)(2,1)} %proj_ref.3) | copy-start | bytes 1572868
  15.0 8.1 %copy-start.1 = (bf16[512,1536]{1,0:T(8,128)(2,1)S(1)}, bf16[512,1536]{1,0:T(8,128)(2,1)}, u32[]{:S(2)}) copy-start(bf16[512,1536]{1,0:T(8,128)(2,1)} %qkv_ref.3) | copy-start | bytes 4718596
  15.0 8.1 %copy-start.3 = (bf16[512,512]{1,0:T(8,128)(2,1)S(1)}, bf16[512,512]{1,0:T(8,128)(2,1)}, u32[]{:S(2)}) copy-start(bf16[512,512]{1,0:T(8,128)(2,1)} %proj_ref.3) | copy-start | bytes 1572868
  22.8 2.9 %collective-permute-start.3 = (bf16[32,2,64,128]{3,2,1,0:T(8,128)(2,1)S(1)}, bf16[32,2,64,128]{3,2,1,0:T(8,128)(2,1)S(1)}, u32[]{:S(2)}, u32[]{:S(2)}) collective-permute-start(bf16[32,2,64,128]{3,2,1,0:T(8,128)(2,1)S(1)} %get-tuple-element.38), channel_id=1, source_target_pairs={{0,8},{8,0},{1,9},{9,1},{2,10},{10,2},{3,11},{11,3},{4,12},{12,4},... | collective-permute-start | bytes 3145736 | tf_op jit(solution)/shard_map/ppermute | solution.py:341
  26.9 22.0 %all-to-all-start = ((bf16[8,512,128]{2,1,0:T(8,128)(2,1)}), bf16[8,512,128]{2,1,0:T(8,128)(2,1)S(1)}, u32[]{:S(2)}, u32[]{:S(2)}) async-start(bf16[8,512,128]{2,1,0:T(8,128)(2,1)} %bitcast.1), calls=%async_computation | async-start | bytes 2097152 | tf_op jit(solution)/shard_map/all_to_all | solution.py:386
  31.4 8.1 %collective-permute-start.4 = (bf16[2,2,6,6,512]{4,3,2,1,0:T(8,128)(2,1)S(1)}, bf16[2,2,6,6,512]{4,3,2,1,0:T(8,128)(2,1)S(1)}, u32[]{:S(2)}, u32[]{:S(2)}) collective-permute-start(bf16[2,2,6,6,512]{4,3,2,1,0:T(8,128)(2,1)S(1)} %get-tuple-element.39), channel_id=1, source_target_pairs={{0,7},{1,0},{2,1},{3,2},{4,3},{5,4},{6,5},{7,6},{8,15},{9,8},{10,9... | collective-permute-start | bytes 442376 | tf_op jit(solution)/shard_map/ppermute | solution.py:341
  49.7 18.2 %all-to-all-start.1 = ((bf16[16,64,128]{2,1,0:T(8,128)(2,1)}), bf16[16,64,128]{2,1,0:T(8,128)(2,1)S(1)}, u32[]{:S(2)}, u32[]{:S(2)}) async-start(bf16[16,64,128]{2,1,0:T(8,128)(2,1)} %bitcast.2), calls=%async_computation.1 | async-start | bytes 524288 | tf_op jit(solution)/shard_map/all_to_all | solution.py:389
  57.9 5.0 %collective-permute-start.5 = (bf16[2,2,3,24,512]{4,3,2,1,0:T(8,128)(2,1)S(1)}, bf16[2,2,3,24,512]{4,3,2,1,0:T(8,128)(2,1)S(1)}, u32[]{:S(2)}, u32[]{:S(2)}) collective-permute-start(bf16[2,2,3,24,512]{4,3,2,1,0:T(8,128)(2,1)S(1)} %halo_rows.1), channel_id=1, source_target_pairs={{0,120},{8,0},{16,8},{24,16},{32,24},{40,32},{48,40},{56,48},{64,5... | collective-permute-start | bytes 884744 | tf_op jit(solution)/shard_map/ppermute | solution.py:341

commit v7 on v6

--- a/solution.py
+++ b/solution.py
@@ -18,8 +18,11 @@
 SLAT = 3
 SLON = 6
 WT = LEV * WLAT * WLON
-PER = 4
+PER = 8
 LANES = PER * HD
+MAIN = 128
+REST = WT - MAIN
+WIDE = PER * WT
 UNITS = D // LANES
 FACTOR = 1.0 / math.sqrt(HD)
 LOG2E = 1.4426950408889634
@@ -115,7 +118,7 @@
 def attention_kernel(
     own_x_ref, own_u_ref, upper_ref, corner_ref, left_ref, lrow_ref, lcol_ref, wqkv_ref, wproj_ref,
     send_ref, gp_ref, mix_ref, nkeep_ref, mkeep_ref, x_ref, u_ref,
-    full_ref, proj_ref, gm_ref, nt_ref, mt_ref, mixt_ref, al_ref, gl_ref, s_ref, da_ref,
+    full_ref, proj_ref, gm_ref, nt_ref, mt_ref, al_ref, gl_ref, s_ref, da_ref, qs_ref, gs_ref,
 ):
     windows = x_ref.shape[0] // WT
     core = lax.axis_index("core")
@@ -140,48 +143,54 @@
     lane = lax.broadcasted_iota(jnp.int32, (1, LANES), 1) // HD
     masks = [(lane == h).astype(jnp.float32) for h in range(PER)]
     low_masks = [m.astype(jnp.bfloat16) for m in masks]
-
-    def stacked(array):
-        return jnp.concatenate([array * m for m in low_masks], axis=0)
-
-    def unstacked(array):
-        total = array[:WT] * masks[0]
+    tiles = [slice(t * MAIN, (t + 1) * MAIN) for t in range(PER + 1)]
+
+    def stack(target_ref, array):
+        for h in range(PER):
+            target_ref[tiles[h], :] = array[:MAIN] * low_masks[h]
+            rest = PER * MAIN + h * REST
+            target_ref[rest:rest + REST, :] = array[MAIN:] * low_masks[h]
+
+    def mix(target_ref, rows, cols, left, weights_ref):
+        turned = left.T
+        for pair in range(PER // 2):
+            both = slice(pair * 2 * MAIN, (pair + 1) * 2 * MAIN)
+            mixed = dot(turned[pair * 2 * HD:(pair + 1) * 2 * HD, :], weights_ref[:, both])
+            s_ref[pair * 2 * HD:pair * 2 * HD + HD, :MAIN] = mixed[:HD, :MAIN]
+            s_ref[pair * 2 * HD + HD:(pair + 1) * 2 * HD, :MAIN] = mixed[HD:, MAIN:]
+        rest = dot(weights_ref[:, tiles[PER]].T, left)
+        total = rest[:REST] * masks[0]
         for h in range(1, PER):
-            total = total + array[h * WT:(h + 1) * WT] * masks[h]
-        return total.astype(jnp.bfloat16)
+            total = total + rest[h * REST:(h + 1) * REST] * masks[h]
+        target_ref[rows.start:rows.start + MAIN, cols] = s_ref[:LANES, :MAIN].T.astype(jnp.bfloat16)
+        target_ref[rows.start + MAIN:rows.stop, cols] = total.astype(jnp.bfloat16)
 
     for w in range(windows):
         rows = slice(w * WT, (w + 1) * WT)
-        allowed = lcol_ref[rows, :] == lrow_ref[w:w + 1, :]
+        labels = lcol_ref[rows, :]
+        allowed = [labels == lrow_ref[w:w + 1, tiles[at]] for at in range(2)]
         for g in range(UNITS):
             q_cols, k_cols, v_cols = (
                 slice(part * D + g * LANES, part * D + (g + 1) * LANES) for part in range(3)
             )
-            q = proj_ref[rows, q_cols]
             k = proj_ref[rows, k_cols]
             v = proj_ref[rows, v_cols]
-            gm = gm_ref[rows, q_cols]
-            s_ref[...] = dot(stacked(k), q, NT)
-            da_ref[...] = dot(stacked(v), gm, NT)
-            vt = v.T
-            kt = k.T
-            for h in range(PER):
-                part = slice(h * WT, (h + 1) * WT)
-                s = jnp.where(allowed, s_ref[part, :], jnp.float32(-1e30))
+            stack(qs_ref, proj_ref[rows, q_cols])
+            stack(gs_ref, gm_ref[rows, q_cols])
+            s_ref[:WT, :] = dot(k, qs_ref[...], NT)
+            da_ref[...] = dot(v, gs_ref[...], NT)
+            for t in range(PER + 1):
+                s = jnp.where(allowed[t // PER], s_ref[:WT, tiles[t]], jnp.float32(-1e30))
                 e = jnp.exp2((s - jnp.max(s, 0, keepdims=True)) * jnp.float32(FACTOR * LOG2E))
                 a = e * (1.0 / jnp.sum(e, 0, keepdims=True))
-                al = a.astype(jnp.bfloat16)
-                al_ref[part, :] = al
-                ga = da_ref[part, :] * a
-                gl = ((ga - a * jnp.sum(ga, 0, keepdims=True)) * jnp.float32(FACTOR)).astype(jnp.bfloat16)
-                gl_ref[part, :] = gl
-                chan = slice(g * LANES + h * HD, g * LANES + (h + 1) * HD)
-                mixt_ref[chan, :] = dot(vt[h * HD:(h + 1) * HD, :], al)
-                s_ref[h * HD:(h + 1) * HD, :] = dot(kt[h * HD:(h + 1) * HD, :], gl)
-            gp_ref[rows, q_cols] = s_ref[:LANES, :].T.astype(jnp.bfloat16)
-            gp_ref[rows, k_cols] = unstacked(dot(gl_ref[...], q))
-            gp_ref[rows, v_cols] = unstacked(dot(al_ref[...], gm))
-        mix_ref[rows, :] = mixt_ref[...].T.astype(jnp.bfloat16)
+                al_ref[:, tiles[t]] = a.astype(jnp.bfloat16)
+                ga = da_ref[:, tiles[t]] * a
+                gl = (ga - a * jnp.sum(ga, 0, keepdims=True)) * jnp.float32(FACTOR)
+                gl_ref[:, tiles[t]] = gl.astype(jnp.bfloat16)
+            gp_ref[rows, k_cols] = dot(gl_ref[...], qs_ref[...]).astype(jnp.bfloat16)
+            gp_ref[rows, v_cols] = dot(al_ref[...], gs_ref[...]).astype(jnp.bfloat16)
+            mix(mix_ref, rows, q_cols, v, al_ref)
+            mix(gp_ref, rows, q_cols, k, gl_ref)
 
     place(mt_ref, mix_ref[...].T)
     nkeep_ref[...] = nt_ref[:half, :]
@@ -320,11 +329,12 @@
             ((tokens, D), low),
             ((D, tokens), low),
             ((D, tokens), low),
-            ((D, WT), full),
-            ((PER * WT, WT), low),
-            ((PER * WT, WT), low),
-            ((PER * WT, WT), full),
-            ((PER * WT, WT), full),
+            ((WT, WIDE), low),
+            ((WT, WIDE), low),
+            ((LANES, WIDE), full),
+            ((WT, WIDE), full),
+            ((WIDE, LANES), low),
+            ((WIDE, LANES), low),
         ),
         5_000_000_000,
         x, u, upper, corner, left, lrow, lcol, w_qkv, w_proj,
@@ -368,8 +378,9 @@
     groups = mask_ids + 4 * wrapped[:, None]
     windows = groups.shape[1] // WLON
     labels = groups.reshape(WLAT, windows, WLON).transpose(1, 0, 2).reshape(windows, WLAT * WLON)
-    lrow = jnp.tile(labels, (1, LEV))
-    lcol = lrow.reshape(windows * WT, 1)
+    labels = jnp.tile(labels, (1, LEV))
+    lcol = labels.reshape(windows * WT, 1)
+    lrow = jnp.concatenate([labels[:, :MAIN], jnp.tile(labels[:, MAIN:], (1, PER))], axis=1)
     send, gp, mix, nkeep, mkeep, x, u = attention(
         inputs, cotangent, upper, corner, left, lrow, lcol, *staged(w_qkv, w_proj)
     )

time: 68.9 us -> 66 us (0.958)
  Pallas kernels: 14.8 us -> 12.2 us
    pallas_call x8, Pallas kernels: 14.7 us -> 12 us  [call(): pl.pallas_call(kernel, out_shape=tuple((make(shape, dtype) for shape, dty...]
where the time goes in v7:
time: 66 us; the launch traced here: 65.7 us
  waiting for transfers between devices  30.9 us (47%)
  starting transfers between devices  18.2 us (28%)
  Pallas kernels  12.2 us (18%)
  local copies, waits for them, and re-layouts  2.95 us (4%)
  other arithmetic  0.76 us (1%)
  between operations  0.75 us (1%)
    ppermute x5, waiting for transfers between devices, passed_along(): return lax.ppermute(value, axis, pairs)  16.5 us
    pallas_call x8, Pallas kernels, call(): pl.pallas_call(kernel, out_shape=tuple((make(shape, dtype) for shape, dty...  12 us
    all_to_all x1, waiting for transfers between devices, per_device(): lax.all_to_all(sums.reshape(8, 512, 128), ('yh', 'x'), 0, 0, tiled=True)  9.45 us
    all_to_all x1, starting transfers between devices, per_device(): lax.all_to_all(sums.reshape(16, 64, 128), ('dp', 'lon'), 0, 0, tiled=True)  8.17 us
    all_to_all x1, starting transfers between devices, per_device(): lax.all_to_all(sums.reshape(8, 512, 128), ('yh', 'x'), 0, 0, tiled=True)  4.47 us
    all_to_all x1, waiting for transfers between devices, per_device(): lax.all_to_all(sums.reshape(16, 64, 128), ('dp', 'lon'), 0, 0, tiled=True)  4.13 us
    ppermute x5, starting transfers between devices, passed_along(): return lax.ppermute(value, axis, pairs)  4.08 us
    unnamed x12, local copies, waits for them, and re-layouts  2.47 us
  transfers between devices with their start and end apart: 8, of which 7 were waited for; matrix products, arithmetic and copies ran while one was open for 2% of the time, Pallas kernels for 5%

profile of v7, /device:TPU:32, one launch (start us, length us, event | category | flops | bytes accessed | tf_op | source)
XLA Modules:
  0.0 65.7 jit_solution(15352716835720049474)
XLA Ops:
  0.7 1.2 %cut_halos.1 = (bf16[2,2,3,18,512]{4,3,2,1,0:T(8,128)(2,1)S(1)}, bf16[2,2,3,6,512]{4,3,2,1,0:T(8,128)(2,1)S(1)}, bf16[2,2,3,6,512]{4,3,2,1,0:T(8,128)(2,1)S(1)}) custom-call(bf16[1,2,6,24,512]{4,3,2,1,0:T(8,128)(2,1)} %own_x_ref.1, bf16[1,2,6,24,512]{4,3,2,1,0:T(8,128)(2,1)} %own_u_ref.1), custom_call_target="tpu_custom_call" | custom-call | flops 1000 | bytes 737280 | tf_op jit(solution)/shard_map/cut_halos/pallas_call | solution.py:299
  1.9 1.4 %collective-permute-start.1 = (bf16[2,2,3,6,512]{4,3,2,1,0:T(8,128)(2,1)S(1)}, bf16[2,2,3,6,512]{4,3,2,1,0:T(8,128)(2,1)S(1)}, u32[]{:S(2)}, u32[]{:S(2)}) collective-permute-start(bf16[2,2,3,6,512]{4,3,2,1,0:T(8,128)(2,1)S(1)} %get-tuple-element.26), channel_id=1, source_target_pairs={{0,9},{1,10},{2,11},{3,12},{4,13},{5,14},{6,15},{7,8},{8,17},{9,18... | collective-permute-start | bytes 221192 | tf_op jit(solution)/shard_map/ppermute | solution.py:361
  3.3 1.9 %collective-permute-start.2 = (bf16[2,2,3,6,512]{4,3,2,1,0:T(8,128)(2,1)S(1)}, bf16[2,2,3,6,512]{4,3,2,1,0:T(8,128)(2,1)S(1)}, u32[]{:S(2)}, u32[]{:S(2)}) collective-permute-start(bf16[2,2,3,6,512]{4,3,2,1,0:T(8,128)(2,1)S(1)} %get-tuple-element.27), channel_id=1, source_target_pairs={{0,1},{1,2},{2,3},{3,4},{4,5},{5,6},{6,7},{7,0},{8,9},{9,10},{10,1... | collective-permute-start | bytes 221192 | tf_op jit(solution)/shard_map/ppermute | solution.py:351
  5.3 1.3 %collective-permute-start = (bf16[2,2,3,18,512]{4,3,2,1,0:T(8,128)(2,1)S(1)}, bf16[2,2,3,18,512]{4,3,2,1,0:T(8,128)(2,1)S(1)}, u32[]{:S(2)}, u32[]{:S(2)}) collective-permute-start(bf16[2,2,3,18,512]{4,3,2,1,0:T(8,128)(2,1)S(1)} %get-tuple-element.25), channel_id=1, source_target_pairs={{0,8},{8,16},{16,24},{24,32},{32,40},{40,48},{48,56},{56,64},{64,7... | collective-permute-start | bytes 663560 | tf_op jit(solution)/shard_map/ppermute | solution.py:351
  6.6 0.8 %broadcast_add_fusion = s32[6,24]{1,0:T(8,128)S(1)} fusion(s32[6,24]{1,0:T(8,128)} %param.7, s32[6]{0:T(128)S(1)} %and_select_fusion), kind=kLoop, calls=%fused_computation.2 | loop fusion | flops 144 | bytes 1176 | tf_op jit(solution)/shard_map/add | solution.py:378
  7.3 0.1 reshape.35
  7.4 0.1 tile.21
  7.5 0.1 tile.23
  7.6 0.1 tile.27.lcol_ref
  7.8 0.1 tile.25
  7.9 1.4 %copy-done = bf16[512,1536]{1,0:T(8,128)(2,1)S(1)} copy-done((bf16[512,1536]{1,0:T(8,128)(2,1)S(1)}, bf16[512,1536]{1,0:T(8,128)(2,1)}, u32[]{:S(2)}) %copy-start) | copy-done | bytes 1572888
  9.3 1.0 %copy-done.2 = bf16[512,512]{1,0:T(8,128)(2,1)S(1)} copy-done((bf16[512,512]{1,0:T(8,128)(2,1)S(1)}, bf16[512,512]{1,0:T(8,128)(2,1)}, u32[]{:S(2)}) %copy-start.2) | copy-done | bytes 524312
  10.3 0.2 stage_weights.1
  10.5 0.8 %collective-permute-done.1.corner_ref = bf16[2,2,3,6,512]{4,3,2,1,0:T(8,128)(2,1)S(1)} collective-permute-done((bf16[2,2,3,6,512]{4,3,2,1,0:T(8,128)(2,1)S(1)}, bf16[2,2,3,6,512]{4,3,2,1,0:T(8,128)(2,1)S(1)}, u32[]{:S(2)}, u32[]{:S(2)}) %collective-permute-start.1) | collective-permute-done | bytes 73760 | tf_op jit(solution)/shard_map/ppermute | solution.py:361
  11.3 0.0 collective-permute-done.2.left_ref
  11.3 3.8 %collective-permute-done.upper_ref = bf16[2,2,3,18,512]{4,3,2,1,0:T(8,128)(2,1)S(1)} collective-permute-done((bf16[2,2,3,18,512]{4,3,2,1,0:T(8,128)(2,1)S(1)}, bf16[2,2,3,18,512]{4,3,2,1,0:T(8,128)(2,1)S(1)}, u32[]{:S(2)}, u32[]{:S(2)}) %collective-permute-start) | collective-permute-done | bytes 221216 | tf_op jit(solution)/shard_map/ppermute | solution.py:351
  15.0 5.1 %window_attention.1 = (bf16[32,2,64,128]{3,2,1,0:T(8,128)(2,1)S(1)}, bf16[288,1536]{1,0:T(8,128)(2,1)S(1)}, bf16[288,512]{1,0:T(8,128)(2,1)S(1)}, bf16[256,288]{...) custom-call(bf16[1,2,6,24,512]{4,3,2,1,0:T(8,128)(2,1)S(1)} %copy-do, ...), custom_call_target="tpu_custom_call" | custom-call | flops 5000000000 | bytes 6225920 | tf_op jit(solution)/shard_map/window_attention/pallas_call | solution.py:299
  20.1 0.1 collective-permute-start.3
  20.3 2.1 %own_half_and_outputs.1 = (f32[32,2,64,128]{3,2,1,0:T(8,128)S(1)}, bf16[2,2,6,18,512]{4,3,2,1,0:T(8,128)(2,1)S(1)}, bf16[2,2,6,6,512]{4,3,2,1,0:T(8,128)(2,1)S(1)}) custom-call(bf16[256,288]{1,0:T(8,128)(2,1)S(1)} %get-tuple-element.30.n_ref, bf16[256,288]{1,0:T(8,128)(2,1)S(1)} %get-tuple-element.31.m_ref, bf16[288,1536]{1,0:T(8,128)(2,1)S(1)} %get-tuple-element.32.gp_ref, ...), custom_call_target="tpu_custom_call" | custom-call | flops 600000000 | bytes 3276800 | tf_op jit(solution)/shard_map/own_half_and_outputs/pallas_call | solution.py:299
  22.4 0.5 collective-permute-done.3.got_ref
  22.9 1.2 %add_halves.1 = bf16[32,2,64,128]{3,2,1,0:T(8,128)(2,1)} custom-call(f32[32,2,64,128]{3,2,1,0:T(8,128)S(1)} %get-tuple-element.37.own_ref, bf16[32,2,64,128]{3,2,1,0:T(8,128)(2,1)S(1)} %collective-permute-done.3.got_ref), custom_call_target="tpu_custom_call" | custom-call | flops 1000000 | bytes 2097152 | tf_op jit(solution)/shard_map/add_halves/pallas_call | solution.py:299
  24.0 4.5 %all-to-all-start = ((bf16[8,512,128]{2,1,0:T(8,128)(2,1)}), bf16[8,512,128]{2,1,0:T(8,128)(2,1)S(1)}, u32[]{:S(2)}, u32[]{:S(2)}) async-start(bf16[8,512,128]{2,1,0:T(8,128)(2,1)} %bitcast.1), calls=%async_computation | async-start | bytes 2097152 | tf_op jit(solution)/shard_map/all_to_all | solution.py:397
  28.5 0.4 collective-permute-start.4
  28.9 7.7 %collective-permute-done.4.right_ref = bf16[2,2,6,6,512]{4,3,2,1,0:T(8,128)(2,1)S(1)} collective-permute-done((bf16[2,2,6,6,512]{4,3,2,1,0:T(8,128)(2,1)S(1)}, bf16[2,2,6,6,512]{4,3,2,1,0:T(8,128)(2,1)S(1)}, u32[]{:S(2)}, u32[]{:S(2)}) %collective-permute-start.4) | collective-permute-done | bytes 147488 | tf_op jit(solution)/shard_map/ppermute | solution.py:351
  36.6 9.5 %all-to-all-done.parts_ref = bf16[8,512,128]{2,1,0:T(8,128)(2,1)S(1)} async-done(((bf16[8,512,128]{2,1,0:T(8,128)(2,1)}), bf16[8,512,128]{2,1,0:T(8,128)(2,1)S(1)}, u32[]{:S(2)}, u32[]{:S(2)}) %all-to-all-start) | async-done | bytes 1048608 | tf_op jit(solution)/shard_map/all_to_all | solution.py:397
  46.0 0.8 %sum_parts.1 = bf16[2,512,128]{2,1,0:T(8,128)(2,1)} custom-call(bf16[8,512,128]{2,1,0:T(8,128)(2,1)S(1)} %all-to-all-done.parts_ref), custom_call_target="tpu_custom_call" | custom-call | flops 1000000 | bytes 524288 | tf_op jit(solution)/shard_map/sum_parts/pallas_call | solution.py:299
  46.9 8.2 %all-to-all-start.1 = ((bf16[16,64,128]{2,1,0:T(8,128)(2,1)}), bf16[16,64,128]{2,1,0:T(8,128)(2,1)S(1)}, u32[]{:S(2)}, u32[]{:S(2)}) async-start(bf16[16,64,128]{2,1,0:T(8,128)(2,1)} %bitcast.2), calls=%async_computation.1 | async-start | bytes 524288 | tf_op jit(solution)/shard_map/all_to_all | solution.py:400
  55.1 0.4 collective-permute-start.5
  55.5 4.6 %collective-permute-done.5.lower_ref = bf16[2,2,3,24,512]{4,3,2,1,0:T(8,128)(2,1)S(1)} collective-permute-done((bf16[2,2,3,24,512]{4,3,2,1,0:T(8,128)(2,1)S(1)}, bf16[2,2,3,24,512]{4,3,2,1,0:T(8,128)(2,1)S(1)}, u32[]{:S(2)}, u32[]{:S(2)}) %collective-permute-start.5) | collective-permute-done | bytes 294944 | tf_op jit(solution)/shard_map/ppermute | solution.py:351
  60.0 0.9 %join_outputs.1 = (bf16[1,2,6,24,512]{4,3,2,1,0:T(8,128)(2,1)}, bf16[1,2,6,24,512]{4,3,2,1,0:T(8,128)(2,1)}) custom-call(bf16[2,2,6,18,512]{4,3,2,1,0:T(8,128)(2,1)S(1)} %get-tuple-element.36.own_ref, bf16[2,2,6,6,512]{4,3,2,1,0:T(8,128)(2,1)S(1)} %collective-permute-done.4.right_ref, bf16[2,2,3,24,512]{4,3,2,1,0:T(8,128)(2,1)S(1)} %collective-permute-done.5.lower_ref), custom_call_target="tpu_custom_call" | custom-call | flops 1000 | bytes 1179648 | tf_op jit(solution)/shard_map/join_outputs/pallas_call | solution.py:299
  60.9 4.1 %all-to-all-done.1.parts_ref = bf16[16,64,128]{2,1,0:T(8,128)(2,1)S(1)} async-done(((bf16[16,64,128]{2,1,0:T(8,128)(2,1)}), bf16[16,64,128]{2,1,0:T(8,128)(2,1)S(1)}, u32[]{:S(2)}, u32[]{:S(2)}) %all-to-all-start.1) | async-done | bytes 262176 | tf_op jit(solution)/shard_map/all_to_all | solution.py:400
  65.0 0.6 last_sum.1
  (18 shorter events, 0.1 us)
Async XLA Ops:
  0.6 14.4 %copy-start.5 = (bf16[1,2,6,24,512]{4,3,2,1,0:T(8,128)(2,1)S(1)}, bf16[1,2,6,24,512]{4,3,2,1,0:T(8,128)(2,1)}, u32[]{:S(2)}) copy-start(bf16[1,2,6,24,512]{4,3,2,1,0:T(8,128)(2,1)} %own_u_ref.1) | copy-start | bytes 884740
  0.6 14.4 %copy-start.4 = (bf16[1,2,6,24,512]{4,3,2,1,0:T(8,128)(2,1)S(1)}, bf16[1,2,6,24,512]{4,3,2,1,0:T(8,128)(2,1)}, u32[]{:S(2)}) copy-start(bf16[1,2,6,24,512]{4,3,2,1,0:T(8,128)(2,1)} %own_x_ref.1) | copy-start | bytes 884740
  1.9 9.4 %collective-permute-start.1 = (bf16[2,2,3,6,512]{4,3,2,1,0:T(8,128)(2,1)S(1)}, bf16[2,2,3,6,512]{4,3,2,1,0:T(8,128)(2,1)S(1)}, u32[]{:S(2)}, u32[]{:S(2)}) collective-permute-start(bf16[2,2,3,6,512]{4,3,2,1,0:T(8,128)(2,1)S(1)} %get-tuple-element.26), channel_id=1, source_target_pairs={{0,9},{1,10},{2,11},{3,12},{4,13},{5,14},{6,15},{7,8},{8,17},{9,18... | collective-permute-start | bytes 221192 | tf_op jit(solution)/shard_map/ppermute | solution.py:361
  3.3 7.9 %collective-permute-start.2 = (bf16[2,2,3,6,512]{4,3,2,1,0:T(8,128)(2,1)S(1)}, bf16[2,2,3,6,512]{4,3,2,1,0:T(8,128)(2,1)S(1)}, u32[]{:S(2)}, u32[]{:S(2)}) collective-permute-start(bf16[2,2,3,6,512]{4,3,2,1,0:T(8,128)(2,1)S(1)} %get-tuple-element.27), channel_id=1, source_target_pairs={{0,1},{1,2},{2,3},{3,4},{4,5},{5,6},{6,7},{7,0},{8,9},{9,10},{10,1... | collective-permute-start | bytes 221192 | tf_op jit(solution)/shard_map/ppermute | solution.py:351
  5.3 9.8 %collective-permute-start = (bf16[2,2,3,18,512]{4,3,2,1,0:T(8,128)(2,1)S(1)}, bf16[2,2,3,18,512]{4,3,2,1,0:T(8,128)(2,1)S(1)}, u32[]{:S(2)}, u32[]{:S(2)}) collective-permute-start(bf16[2,2,3,18,512]{4,3,2,1,0:T(8,128)(2,1)S(1)} %get-tuple-element.25), channel_id=1, source_target_pairs={{0,8},{8,16},{16,24},{24,32},{32,40},{40,48},{48,56},{56,64},{64,7... | collective-permute-start | bytes 663560 | tf_op jit(solution)/shard_map/ppermute | solution.py:351
  7.9 1.4 %copy-start = (bf16[512,1536]{1,0:T(8,128)(2,1)S(1)}, bf16[512,1536]{1,0:T(8,128)(2,1)}, u32[]{:S(2)}) copy-start(bf16[512,1536]{1,0:T(8,128)(2,1)} %qkv_ref.3) | copy-start | bytes 4718596
  9.3 1.0 %copy-start.2 = (bf16[512,512]{1,0:T(8,128)(2,1)S(1)}, bf16[512,512]{1,0:T(8,128)(2,1)}, u32[]{:S(2)}) copy-start(bf16[512,512]{1,0:T(8,128)(2,1)} %proj_ref.3) | copy-start | bytes 1572868
  15.0 5.2 %copy-start.1 = (bf16[512,1536]{1,0:T(8,128)(2,1)S(1)}, bf16[512,1536]{1,0:T(8,128)(2,1)}, u32[]{:S(2)}) copy-start(bf16[512,1536]{1,0:T(8,128)(2,1)} %qkv_ref.3) | copy-start | bytes 4718596
  15.0 5.2 %copy-start.3 = (bf16[512,512]{1,0:T(8,128)(2,1)S(1)}, bf16[512,512]{1,0:T(8,128)(2,1)}, u32[]{:S(2)}) copy-start(bf16[512,512]{1,0:T(8,128)(2,1)} %proj_ref.3) | copy-start | bytes 1572868
  20.1 2.7 %collective-permute-start.3 = (bf16[32,2,64,128]{3,2,1,0:T(8,128)(2,1)S(1)}, bf16[32,2,64,128]{3,2,1,0:T(8,128)(2,1)S(1)}, u32[]{:S(2)}, u32[]{:S(2)}) collective-permute-start(bf16[32,2,64,128]{3,2,1,0:T(8,128)(2,1)S(1)} %get-tuple-element.38), channel_id=1, source_target_pairs={{0,8},{8,0},{1,9},{9,1},{2,10},{10,2},{3,11},{11,3},{4,12},{12,4},... | collective-permute-start | bytes 3145736 | tf_op jit(solution)/shard_map/ppermute | solution.py:351
  24.0 22.0 %all-to-all-start = ((bf16[8,512,128]{2,1,0:T(8,128)(2,1)}), bf16[8,512,128]{2,1,0:T(8,128)(2,1)S(1)}, u32[]{:S(2)}, u32[]{:S(2)}) async-start(bf16[8,512,128]{2,1,0:T(8,128)(2,1)} %bitcast.1), calls=%async_computation | async-start | bytes 2097152 | tf_op jit(solution)/shard_map/all_to_all | solution.py:397
  28.5 8.1 %collective-permute-start.4 = (bf16[2,2,6,6,512]{4,3,2,1,0:T(8,128)(2,1)S(1)}, bf16[2,2,6,6,512]{4,3,2,1,0:T(8,128)(2,1)S(1)}, u32[]{:S(2)}, u32[]{:S(2)}) collective-permute-start(bf16[2,2,6,6,512]{4,3,2,1,0:T(8,128)(2,1)S(1)} %get-tuple-element.39), channel_id=1, source_target_pairs={{0,7},{1,0},{2,1},{3,2},{4,3},{5,4},{6,5},{7,6},{8,15},{9,8},{10,9... | collective-permute-start | bytes 442376 | tf_op jit(solution)/shard_map/ppermute | solution.py:351
  46.9 18.2 %all-to-all-start.1 = ((bf16[16,64,128]{2,1,0:T(8,128)(2,1)}), bf16[16,64,128]{2,1,0:T(8,128)(2,1)S(1)}, u32[]{:S(2)}, u32[]{:S(2)}) async-start(bf16[16,64,128]{2,1,0:T(8,128)(2,1)} %bitcast.2), calls=%async_computation.1 | async-start | bytes 524288 | tf_op jit(solution)/shard_map/all_to_all | solution.py:400
  55.1 5.0 %collective-permute-start.5 = (bf16[2,2,3,24,512]{4,3,2,1,0:T(8,128)(2,1)S(1)}, bf16[2,2,3,24,512]{4,3,2,1,0:T(8,128)(2,1)S(1)}, u32[]{:S(2)}, u32[]{:S(2)}) collective-permute-start(bf16[2,2,3,24,512]{4,3,2,1,0:T(8,128)(2,1)S(1)} %halo_rows.1), channel_id=1, source_target_pairs={{0,120},{8,0},{16,8},{24,16},{32,24},{40,32},{48,40},{56,48},{64,5... | collective-permute-start | bytes 884744 | tf_op jit(solution)/shard_map/ppermute | solution.py:351

commit v8 on v7

--- a/solution.py
+++ b/solution.py
@@ -199,27 +199,51 @@
     store_shares(send_ref, grads)
 
 
-def add_kernel(own_ref, got_ref, sum_ref):
-    sum_ref[...] = (own_ref[...] + got_ref[...].astype(jnp.float32)).astype(jnp.bfloat16)
-
-
-def added(parts_ref):
-    total = parts_ref[0].astype(jnp.float32)
-    for at in range(1, parts_ref.shape[0]):
-        total = total + parts_ref[at].astype(jnp.float32)
-    return total
-
-
-def sum_kernel(parts_ref, sum_ref):
-    total = added(parts_ref).astype(jnp.bfloat16)
-    sum_ref[0] = total
-    sum_ref[1] = total
-
-
-def last_kernel(parts_ref, qkv_ref, proj_ref):
-    total = added(parts_ref)
+def first_kernel(half_ref, got_ref, keep0_ref, send0_ref, keep1_ref, send1_ref):
+    a, d = lax.axis_index("xl"), lax.axis_index("dp")
+
+    def total(*at):
+        return half_ref[at] + got_ref[at].astype(jnp.float32)
+
+    for yh in range(2):
+        keep0_ref[yh] = total(yh, 0, a)
+        send0_ref[yh] = total(yh, 0, 1 - a).astype(jnp.bfloat16)
+        for xl in range(2):
+            for lon in range(8):
+                keep1_ref[yh, xl, lon] = total(yh, 1, xl, lon, d)
+                send1_ref[yh, xl, lon] = total(yh, 1, xl, lon, 1 - d).astype(jnp.bfloat16)
+
+
+def second_kernel(keep0_ref, got0_ref, keep1_ref, got1_ref, own_ref, send0_ref, send1_ref):
+    a, d = lax.axis_index("xl"), lax.axis_index("dp")
+
+    def total0(*at):
+        return keep0_ref[at] + got0_ref[at].astype(jnp.float32)
+
+    def total1(*at):
+        return keep1_ref[at] + got1_ref[at].astype(jnp.float32)
+
+    for yh in range(2):
+        own_ref[1, yh] = total1(yh, a)
+        send1_ref[yh] = total1(yh, 1 - a).astype(jnp.bfloat16)
+        for lon in range(8):
+            own_ref[0, yh, lon] = total0(yh, lon, d)
+            send0_ref[yh, lon] = total0(yh, lon, 1 - d).astype(jnp.bfloat16)
+
+
+def third_kernel(own_ref, got0_ref, got1_ref, sum_ref):
+    for xh, ref in enumerate((got0_ref, got1_ref)):
+        for yh in range(2):
+            sum_ref[yh, xh] = (own_ref[xh, yh] + ref[yh].astype(jnp.float32)).astype(jnp.bfloat16)
+
+
+def last_kernel(share_ref, other_ref, qkv_ref, proj_ref):
+    second = lax.axis_index("dp") == 1
+    share, other = share_ref[...], other_ref[...]
+    halves = (jnp.where(second, other, share), jnp.where(second, share, other))
     for tile in range(16):
-        piece = total[tile * 4:tile * 4 + 4, :]
+        row = tile % 8 * 4
+        piece = halves[tile // 8][row:row + 4, :]
         if tile < 12:
             qkv_ref[:, tile * 128:(tile + 1) * 128] = piece
         else:
@@ -342,7 +366,7 @@
     )
 
 
-LAT = ("yh", "x", "core")
+LAT = ("yh", "xh", "xl", "core")
 
 
 def passed_along(value, axis, steps):
@@ -392,14 +416,28 @@
         nkeep, mkeep, gp, u, x, mix, w_qkv, w_proj,
         dtypes=(jnp.float32,) + (jnp.bfloat16,) * 2, any_args=(6, 7), limit=16,
     )
-    (sums,) = call(add_kernel, "add_halves", (send.shape,), (), 1_000_000, half, got, placed=True)
+    low, full = jnp.bfloat16, jnp.float32
+    shape = (2, 2, 2, 8, 2, 32, 128)
+    keep0, send0, keep1, send1 = call(
+        first_kernel, "first_sums", ((2, 8, 2, 32, 128),) * 2 + ((2, 2, 8, 32, 128),) * 2, (), 1_000_000,
+        half.reshape(shape), got.reshape(shape), dtypes=(full, low) * 2,
+    )
+    got0, got1 = passed_along(send0, "xl", 1), passed_along(send1, "dp", 1)
     right = passed_along(left, "lon", -1)
-    spread = lax.all_to_all(sums.reshape(8, 512, 128), ("yh", "x"), 0, 0, tiled=True)
-    spread, right = lax.optimization_barrier((spread, right))
-    (sums,) = call(sum_kernel, "sum_parts", ((2, 512, 128),), (), 1_000_000, spread, placed=True)
-    spread = lax.all_to_all(sums.reshape(16, 64, 128), ("dp", "lon"), 0, 0, tiled=True)
+    got0, got1, right = lax.optimization_barrier((got0, got1, right))
+    mine, send0, send1 = call(
+        second_kernel, "second_sums", ((2, 2, 8, 32, 128),) + ((2, 8, 32, 128),) * 2, (), 1_000_000,
+        keep0, got0, keep1, got1, dtypes=(full, low, low),
+    )
+    got0, got1 = passed_along(send0, "dp", 1), passed_along(send1, "xl", 1)
+    (sums,) = call(
+        third_kernel, "third_sums", ((2, 2, 8, 32, 128),), (), 1_000_000, mine, got0, got1
+    )
+    spread = lax.all_to_all(sums.reshape(32, 32, 128), ("yh", "xh", "lon"), 0, 0, tiled=True)
+    share = jnp.sum(spread.astype(jnp.float32), 0)
+    other = passed_along(share, "dp", 1)
     grad_qkv, grad_proj = call(
-        last_kernel, "last_sum", ((4, 3 * D), (4, D)), (), 1000, spread,
+        last_kernel, "last_sum", ((4, 3 * D), (4, D)), (), 1000, share, other,
         dtypes=(jnp.float32,) * 2, limit=4,
     )
     (rows,) = call(rows_kernel, "halo_rows", ((2, LEV, SLAT, *inputs.shape[3:]),), (), 1000, own, right, limit=8)
@@ -411,7 +449,7 @@
 
 
 def solution(mesh):
-    mesh = Mesh(mesh.devices.reshape(2, 2, 4, 2, 8), ("dp", "yh", "x", "core", "lon"))
+    mesh = Mesh(mesh.devices.reshape(2, 2, 2, 2, 2, 8), ("dp", *LAT, "lon"))
     tokens = P("dp", None, LAT, "lon", None)
     return jax.shard_map(
         per_device,

time: 66 us -> 68 us (1.030)
  starting transfers between devices: 18.2 us -> 23.6 us
  waiting for transfers between devices: 30.9 us -> 27.8 us
  Pallas kernels: 12.2 us -> 11.2 us
    ppermute x5 -> x10, starting transfers between devices: 4.08 us -> 12 us  [passed_along(): return lax.ppermute(value, axis, pairs)]
    all_to_all x2 -> x1, waiting for transfers between devices: 13.6 us -> 9.78 us  [per_device(): lax.all_to_all(sums.reshape(32, 32, 128), ('yh', 'xh', 'lon'), 0, 0, tile...]
    all_to_all x2 -> x1, starting transfers between devices: 12.6 us -> 10.2 us  [per_device(): lax.all_to_all(sums.reshape(32, 32, 128), ('yh', 'xh', 'lon'), 0, 0, tile...]
    pallas_call x8 -> x9, Pallas kernels: 12 us -> 11 us  [call(): pl.pallas_call(kernel, out_shape=tuple((make(shape, dtype) for shape, dty...]
    ppermute x5 -> x10, waiting for transfers between devices: 16.5 us -> 17.2 us  [passed_along(): return lax.ppermute(value, axis, pairs)]
  transfers between devices with their start and end apart: 8 -> 12, of which waited for: 7 -> 8; matrix products, arithmetic and copies ran while one was open for 2% -> 2% of each run, Pallas kernels for 5% -> 5%
where the time goes in v8:
time: 68 us; the launch traced here: 67.1 us
  waiting for transfers between devices  27.8 us (41%)
  starting transfers between devices  23.6 us (35%)
  Pallas kernels  11.2 us (16%)
  local copies, waits for them, and re-layouts  2.95 us (4%)
  other arithmetic  0.81 us (1%)
  between operations  0.78 us (1%)
    ppermute x10, waiting for transfers between devices, passed_along(): return lax.ppermute(value, axis, pairs)  17.2 us
    ppermute x10, starting transfers between devices, passed_along(): return lax.ppermute(value, axis, pairs)  12 us
    pallas_call x9, Pallas kernels, call(): pl.pallas_call(kernel, out_shape=tuple((make(shape, dtype) for shape, dty...  11 us
    all_to_all x1, starting transfers between devices, per_device(): lax.all_to_all(sums.reshape(32, 32, 128), ('yh', 'xh', 'lon'), 0, 0, tile...  10.2 us
    all_to_all x1, waiting for transfers between devices, per_device(): lax.all_to_all(sums.reshape(32, 32, 128), ('yh', 'xh', 'lon'), 0, 0, tile...  9.78 us
    unnamed x12, local copies, waits for them, and re-layouts  2.47 us
    ppermute x1, starting transfers between devices, diagonal(): return lax.ppermute(value, (*LAT, 'lon'), pairs)  1.43 us
  transfers between devices with their start and end apart: 12, of which 8 were waited for; matrix products, arithmetic and copies ran while one was open for 2% of the time, Pallas kernels for 5%

profile of v8, /device:TPU:32, one launch (start us, length us, event | category | flops | bytes accessed | tf_op | source)
XLA Modules:
  0.0 67.1 jit_solution(17523785132818153842)
XLA Ops:
  0.7 1.2 %cut_halos.1 = (bf16[2,2,3,18,512]{4,3,2,1,0:T(8,128)(2,1)S(1)}, bf16[2,2,3,6,512]{4,3,2,1,0:T(8,128)(2,1)S(1)}, bf16[2,2,3,6,512]{4,3,2,1,0:T(8,128)(2,1)S(1)}) custom-call(bf16[1,2,6,24,512]{4,3,2,1,0:T(8,128)(2,1)} %own_x_ref.1, bf16[1,2,6,24,512]{4,3,2,1,0:T(8,128)(2,1)} %own_u_ref.1), custom_call_target="tpu_custom_call" | custom-call | flops 1000 | bytes 737280 | tf_op jit(solution)/shard_map/cut_halos/pallas_call | solution.py:323
  1.9 1.4 %collective-permute-start.1 = (bf16[2,2,3,6,512]{4,3,2,1,0:T(8,128)(2,1)S(1)}, bf16[2,2,3,6,512]{4,3,2,1,0:T(8,128)(2,1)S(1)}, u32[]{:S(2)}, u32[]{:S(2)}) collective-permute-start(bf16[2,2,3,6,512]{4,3,2,1,0:T(8,128)(2,1)S(1)} %get-tuple-element.34), channel_id=1, source_target_pairs={{0,9},{1,10},{2,11},{3,12},{4,13},{5,14},{6,15},{7,8},{8,17},{9,18... | collective-permute-start | bytes 221192 | tf_op jit(solution)/shard_map/ppermute | solution.py:385
  3.3 1.9 %collective-permute-start.2 = (bf16[2,2,3,6,512]{4,3,2,1,0:T(8,128)(2,1)S(1)}, bf16[2,2,3,6,512]{4,3,2,1,0:T(8,128)(2,1)S(1)}, u32[]{:S(2)}, u32[]{:S(2)}) collective-permute-start(bf16[2,2,3,6,512]{4,3,2,1,0:T(8,128)(2,1)S(1)} %get-tuple-element.35), channel_id=1, source_target_pairs={{0,1},{1,2},{2,3},{3,4},{4,5},{5,6},{6,7},{7,0},{8,9},{9,10},{10,1... | collective-permute-start | bytes 221192 | tf_op jit(solution)/shard_map/ppermute | solution.py:375
  5.3 1.3 %collective-permute-start = (bf16[2,2,3,18,512]{4,3,2,1,0:T(8,128)(2,1)S(1)}, bf16[2,2,3,18,512]{4,3,2,1,0:T(8,128)(2,1)S(1)}, u32[]{:S(2)}, u32[]{:S(2)}) collective-permute-start(bf16[2,2,3,18,512]{4,3,2,1,0:T(8,128)(2,1)S(1)} %get-tuple-element.33), channel_id=1, source_target_pairs={{0,8},{8,16},{16,24},{24,32},{32,40},{40,48},{48,56},{56,64},{64,7... | collective-permute-start | bytes 663560 | tf_op jit(solution)/shard_map/ppermute | solution.py:375
  6.6 0.8 %broadcast_add_fusion = s32[6,24]{1,0:T(8,128)S(1)} fusion(s32[6,24]{1,0:T(8,128)} %param.7, s32[6]{0:T(128)S(1)} %and_select_fusion), kind=kLoop, calls=%fused_computation.3 | loop fusion | flops 144 | bytes 1176 | tf_op jit(solution)/shard_map/add | solution.py:402
  7.6 0.1 tile.27.lcol_ref
  7.9 1.4 %copy-done = bf16[512,1536]{1,0:T(8,128)(2,1)S(1)} copy-done((bf16[512,1536]{1,0:T(8,128)(2,1)S(1)}, bf16[512,1536]{1,0:T(8,128)(2,1)}, u32[]{:S(2)}) %copy-start) | copy-done | bytes 1572888
  9.3 1.0 %copy-done.2 = bf16[512,512]{1,0:T(8,128)(2,1)S(1)} copy-done((bf16[512,512]{1,0:T(8,128)(2,1)S(1)}, bf16[512,512]{1,0:T(8,128)(2,1)}, u32[]{:S(2)}) %copy-start.2) | copy-done | bytes 524312
  10.3 0.2 stage_weights.1
  10.5 0.8 %collective-permute-done.1.corner_ref = bf16[2,2,3,6,512]{4,3,2,1,0:T(8,128)(2,1)S(1)} collective-permute-done((bf16[2,2,3,6,512]{4,3,2,1,0:T(8,128)(2,1)S(1)}, bf16[2,2,3,6,512]{4,3,2,1,0:T(8,128)(2,1)S(1)}, u32[]{:S(2)}, u32[]{:S(2)}) %collective-permute-start.1) | collective-permute-done | bytes 73760 | tf_op jit(solution)/shard_map/ppermute | solution.py:385
  11.3 3.8 %collective-permute-done.upper_ref = bf16[2,2,3,18,512]{4,3,2,1,0:T(8,128)(2,1)S(1)} collective-permute-done((bf16[2,2,3,18,512]{4,3,2,1,0:T(8,128)(2,1)S(1)}, bf16[2,2,3,18,512]{4,3,2,1,0:T(8,128)(2,1)S(1)}, u32[]{:S(2)}, u32[]{:S(2)}) %collective-permute-start) | collective-permute-done | bytes 221216 | tf_op jit(solution)/shard_map/ppermute | solution.py:375
  15.0 5.1 %window_attention.1 = (bf16[32,2,64,128]{3,2,1,0:T(8,128)(2,1)S(1)}, bf16[288,1536]{1,0:T(8,128)(2,1)S(1)}, bf16[288,512]{1,0:T(8,128)(2,1)S(1)}, bf16[256,288]{...) custom-call(bf16[1,2,6,24,512]{4,3,2,1,0:T(8,128)(2,1)S(1)} %copy-do, ...), custom_call_target="tpu_custom_call" | custom-call | flops 5000000000 | bytes 6225920 | tf_op jit(solution)/shard_map/window_attention/pallas_call | solution.py:323
  20.1 0.1 collective-permute-start.3
  20.3 2.1 %own_half_and_outputs.1 = (f32[32,2,64,128]{3,2,1,0:T(8,128)S(1)}, bf16[2,2,6,18,512]{4,3,2,1,0:T(8,128)(2,1)S(1)}, bf16[2,2,6,6,512]{4,3,2,1,0:T(8,128)(2,1)S(1)}) custom-call(bf16[256,288]{1,0:T(8,128)(2,1)S(1)} %get-tuple-element.38.n_ref, bf16[256,288]{1,0:T(8,128)(2,1)S(1)} %get-tuple-element.39.m_ref, bf16[288,1536]{1,0:T(8,128)(2,1)S(1)} %get-tuple-element.40.gp_ref, ...), custom_call_target="tpu_custom_call" | custom-call | flops 600000000 | bytes 3276800 | tf_op jit(solution)/shard_map/own_half_and_outputs/pallas_call | solution.py:323
  22.4 0.5 collective-permute-done.3
  22.9 0.2 first_sums.1
  23.1 0.1 collective-permute-start.4
  23.2 1.7 %collective-permute-start.5 = (bf16[2,2,8,32,128]{4,3,2,1,0:T(8,128)(2,1)S(1)}, bf16[2,2,8,32,128]{4,3,2,1,0:T(8,128)(2,1)S(1)}, u32[]{:S(2)}, u32[]{:S(2)}) collective-permute-start(bf16[2,2,8,32,128]{4,3,2,1,0:T(8,128)(2,1)S(1)} %get-tuple-element.48), channel_id=1, source_target_pairs={{0,128},{128,0},{1,129},{129,1},{2,130},{130,2},{3,131},{131,3},{4... | collective-permute-start | bytes 786440 | tf_op jit(solution)/shard_map/ppermute | solution.py:375
  24.8 1.2 %collective-permute-start.6 = (bf16[2,2,6,6,512]{4,3,2,1,0:T(8,128)(2,1)S(1)}, bf16[2,2,6,6,512]{4,3,2,1,0:T(8,128)(2,1)S(1)}, u32[]{:S(2)}, u32[]{:S(2)}) collective-permute-start(bf16[2,2,6,6,512]{4,3,2,1,0:T(8,128)(2,1)S(1)} %get-tuple-element.49), channel_id=1, source_target_pairs={{0,7},{1,0},{2,1},{3,2},{4,3},{5,4},{6,5},{7,6},{8,15},{9,8},{10,9... | collective-permute-start | bytes 442376 | tf_op jit(solution)/shard_map/ppermute | solution.py:375
  26.0 6.9 %collective-permute-done.6.right_ref = bf16[2,2,6,6,512]{4,3,2,1,0:T(8,128)(2,1)S(1)} collective-permute-done((bf16[2,2,6,6,512]{4,3,2,1,0:T(8,128)(2,1)S(1)}, bf16[2,2,6,6,512]{4,3,2,1,0:T(8,128)(2,1)S(1)}, u32[]{:S(2)}, u32[]{:S(2)}) %collective-permute-start.6) | collective-permute-done | bytes 147488 | tf_op jit(solution)/shard_map/ppermute | solution.py:375
  33.0 0.7 %collective-permute-start.8 = (bf16[2,8,32,128]{3,2,1,0:T(8,128)(2,1)S(1)}, bf16[2,8,32,128]{3,2,1,0:T(8,128)(2,1)S(1)}, u32[]{:S(2)}, u32[]{:S(2)}) collective-permute-start(bf16[2,8,32,128]{3,2,1,0:T(8,128)(2,1)S(1)} %get-tuple-element.58), channel_id=1, source_target_pairs={{0,128},{128,0},{1,129},{129,1},{2,130},{130,2},{3,131},{131,3},{4... | collective-permute-start | bytes 393224 | tf_op jit(solution)/shard_map/ppermute | solution.py:375
  33.7 1.6 %collective-permute-start.9 = (bf16[2,8,32,128]{3,2,1,0:T(8,128)(2,1)S(1)}, bf16[2,8,32,128]{3,2,1,0:T(8,128)(2,1)S(1)}, u32[]{:S(2)}, u32[]{:S(2)}) collective-permute-start(bf16[2,8,32,128]{3,2,1,0:T(8,128)(2,1)S(1)} %get-tuple-element.59), channel_id=1, source_target_pairs={{0,16},{16,0},{1,17},{17,1},{2,18},{18,2},{3,19},{19,3},{4,20},{20... | collective-permute-start | bytes 393224 | tf_op jit(solution)/shard_map/ppermute | solution.py:375
  35.3 2.9 %collective-permute-done.8.got0_ref = bf16[2,8,32,128]{3,2,1,0:T(8,128)(2,1)S(1)} collective-permute-done((bf16[2,8,32,128]{3,2,1,0:T(8,128)(2,1)S(1)}, bf16[2,8,32,128]{3,2,1,0:T(8,128)(2,1)S(1)}, u32[]{:S(2)}, u32[]{:S(2)}) %collective-permute-start.8) | collective-permute-done | bytes 131104 | tf_op jit(solution)/shard_map/ppermute | solution.py:375
  38.2 0.4 collective-permute-done.9.got1_ref
  38.7 0.7 %third_sums.1 = bf16[2,2,8,32,128]{4,3,2,1,0:T(8,128)(2,1)} custom-call(f32[2,2,8,32,128]{4,3,2,1,0:T(8,128)S(1)} %get-tuple-element.57.own_ref, bf16[2,8,32,128]{3,2,1,0:T(8,128)(2,1)S(1)} %collective-permute-done.8.got0_ref, bf16[2,8,32,128]{3,2,1,0:T(8,128)(2,1)S(1)} %collective-permute-done.9.got1_ref), custom_call_target="tpu_custom_call" | custom-call | flops 1000000 | bytes 524288 | tf_op jit(solution)/shard_map/third_sums/pallas_call | solution.py:323
  39.4 10.2 %all-to-all-start = ((bf16[32,32,128]{2,1,0:T(8,128)(2,1)}), bf16[32,32,128]{2,1,0:T(8,128)(2,1)S(1)}, u32[]{:S(2)}, u32[]{:S(2)}) async-start(bf16[32,32,128]{2,1,0:T(8,128)(2,1)} %bitcast.3), calls=%async_computation | async-start | bytes 524288 | tf_op jit(solution)/shard_map/all_to_all | solution.py:436
  49.6 3.2 %collective-permute-start.7 = (bf16[2,2,3,24,512]{4,3,2,1,0:T(8,128)(2,1)S(1)}, bf16[2,2,3,24,512]{4,3,2,1,0:T(8,128)(2,1)S(1)}, u32[]{:S(2)}, u32[]{:S(2)}) collective-permute-start(bf16[2,2,3,24,512]{4,3,2,1,0:T(8,128)(2,1)S(1)} %halo_rows.1), channel_id=1, source_target_pairs={{0,120},{8,0},{16,8},{24,16},{32,24},{40,32},{48,40},{56,48},{64,5... | collective-permute-start | bytes 884744 | tf_op jit(solution)/shard_map/ppermute | solution.py:375
  52.8 9.8 %all-to-all-done = bf16[32,32,128]{2,1,0:T(8,128)(2,1)S(1)} async-done(((bf16[32,32,128]{2,1,0:T(8,128)(2,1)}), bf16[32,32,128]{2,1,0:T(8,128)(2,1)S(1)}, u32[]{:S(2)}, u32[]{:S(2)}) %all-to-all-start) | async-done | bytes 262176 | tf_op jit(solution)/shard_map/all_to_all | solution.py:436
  62.6 0.2 collective-permute-start.10
  62.9 0.9 %join_outputs.1 = (bf16[1,2,6,24,512]{4,3,2,1,0:T(8,128)(2,1)}, bf16[1,2,6,24,512]{4,3,2,1,0:T(8,128)(2,1)}) custom-call(bf16[2,2,6,18,512]{4,3,2,1,0:T(8,128)(2,1)S(1)} %get-tuple-element.44.own_ref, bf16[2,2,6,6,512]{4,3,2,1,0:T(8,128)(2,1)S(1)} %collective-permute-done.6.right_ref, bf16[2,2,3,24,512]{4,3,2,1,0:T(8,128)(2,1)S(1)} %collective-permute-done.7.lower_ref), custom_call_target="tpu_custom_call" | custom-call | flops 1000 | bytes 1179648 | tf_op jit(solution)/shard_map/join_outputs/pallas_call | solution.py:323
  63.7 2.7 %collective-permute-done.10.other_ref = f32[32,128]{1,0:T(8,128)S(1)} collective-permute-done((f32[32,128]{1,0:T(8,128)S(1)}, f32[32,128]{1,0:T(8,128)S(1)}, u32[]{:S(2)}, u32[]{:S(2)}) %collective-permute-start.10) | collective-permute-done | bytes 16416 | tf_op jit(solution)/shard_map/ppermute | solution.py:375
  66.5 0.6 last_sum.1
  (28 shorter events, 0.6 us)
Async XLA Ops:
  0.6 14.4 %copy-start.5 = (bf16[1,2,6,24,512]{4,3,2,1,0:T(8,128)(2,1)S(1)}, bf16[1,2,6,24,512]{4,3,2,1,0:T(8,128)(2,1)}, u32[]{:S(2)}) copy-start(bf16[1,2,6,24,512]{4,3,2,1,0:T(8,128)(2,1)} %own_u_ref.1) | copy-start | bytes 884740
  0.6 14.4 %copy-start.4 = (bf16[1,2,6,24,512]{4,3,2,1,0:T(8,128)(2,1)S(1)}, bf16[1,2,6,24,512]{4,3,2,1,0:T(8,128)(2,1)}, u32[]{:S(2)}) copy-start(bf16[1,2,6,24,512]{4,3,2,1,0:T(8,128)(2,1)} %own_x_ref.1) | copy-start | bytes 884740
  1.9 9.4 %collective-permute-start.1 = (bf16[2,2,3,6,512]{4,3,2,1,0:T(8,128)(2,1)S(1)}, bf16[2,2,3,6,512]{4,3,2,1,0:T(8,128)(2,1)S(1)}, u32[]{:S(2)}, u32[]{:S(2)}) collective-permute-start(bf16[2,2,3,6,512]{4,3,2,1,0:T(8,128)(2,1)S(1)} %get-tuple-element.34), channel_id=1, source_target_pairs={{0,9},{1,10},{2,11},{3,12},{4,13},{5,14},{6,15},{7,8},{8,17},{9,18... | collective-permute-start | bytes 221192 | tf_op jit(solution)/shard_map/ppermute | solution.py:385
  3.3 7.9 %collective-permute-start.2 = (bf16[2,2,3,6,512]{4,3,2,1,0:T(8,128)(2,1)S(1)}, bf16[2,2,3,6,512]{4,3,2,1,0:T(8,128)(2,1)S(1)}, u32[]{:S(2)}, u32[]{:S(2)}) collective-permute-start(bf16[2,2,3,6,512]{4,3,2,1,0:T(8,128)(2,1)S(1)} %get-tuple-element.35), channel_id=1, source_target_pairs={{0,1},{1,2},{2,3},{3,4},{4,5},{5,6},{6,7},{7,0},{8,9},{9,10},{10,1... | collective-permute-start | bytes 221192 | tf_op jit(solution)/shard_map/ppermute | solution.py:375
  5.3 9.8 %collective-permute-start = (bf16[2,2,3,18,512]{4,3,2,1,0:T(8,128)(2,1)S(1)}, bf16[2,2,3,18,512]{4,3,2,1,0:T(8,128)(2,1)S(1)}, u32[]{:S(2)}, u32[]{:S(2)}) collective-permute-start(bf16[2,2,3,18,512]{4,3,2,1,0:T(8,128)(2,1)S(1)} %get-tuple-element.33), channel_id=1, source_target_pairs={{0,8},{8,16},{16,24},{24,32},{32,40},{40,48},{48,56},{56,64},{64,7... | collective-permute-start | bytes 663560 | tf_op jit(solution)/shard_map/ppermute | solution.py:375
  7.9 1.4 %copy-start = (bf16[512,1536]{1,0:T(8,128)(2,1)S(1)}, bf16[512,1536]{1,0:T(8,128)(2,1)}, u32[]{:S(2)}) copy-start(bf16[512,1536]{1,0:T(8,128)(2,1)} %qkv_ref.3) | copy-start | bytes 4718596
  9.3 1.0 %copy-start.2 = (bf16[512,512]{1,0:T(8,128)(2,1)S(1)}, bf16[512,512]{1,0:T(8,128)(2,1)}, u32[]{:S(2)}) copy-start(bf16[512,512]{1,0:T(8,128)(2,1)} %proj_ref.3) | copy-start | bytes 1572868
  15.0 5.2 %copy-start.1 = (bf16[512,1536]{1,0:T(8,128)(2,1)S(1)}, bf16[512,1536]{1,0:T(8,128)(2,1)}, u32[]{:S(2)}) copy-start(bf16[512,1536]{1,0:T(8,128)(2,1)} %qkv_ref.3) | copy-start | bytes 4718596
  15.0 5.2 %copy-start.3 = (bf16[512,512]{1,0:T(8,128)(2,1)S(1)}, bf16[512,512]{1,0:T(8,128)(2,1)}, u32[]{:S(2)}) copy-start(bf16[512,512]{1,0:T(8,128)(2,1)} %proj_ref.3) | copy-start | bytes 1572868
  20.1 2.7 %collective-permute-start.3 = (bf16[32,2,64,128]{3,2,1,0:T(8,128)(2,1)S(1)}, bf16[32,2,64,128]{3,2,1,0:T(8,128)(2,1)S(1)}, u32[]{:S(2)}, u32[]{:S(2)}) collective-permute-start(bf16[32,2,64,128]{3,2,1,0:T(8,128)(2,1)S(1)} %get-tuple-element.46), channel_id=1, source_target_pairs={{0,8},{8,0},{1,9},{9,1},{2,10},{10,2},{3,11},{11,3},{4,12},{12,4},... | collective-permute-start | bytes 3145736 | tf_op jit(solution)/shard_map/ppermute | solution.py:375
  23.1 9.8 %collective-permute-start.4 = (bf16[2,8,2,32,128]{4,3,2,1,0:T(8,128)(2,1)S(1)}, bf16[2,8,2,32,128]{4,3,2,1,0:T(8,128)(2,1)S(1)}, u32[]{:S(2)}, u32[]{:S(2)}) collective-permute-start(bf16[2,8,2,32,128]{4,3,2,1,0:T(8,128)(2,1)S(1)} %get-tuple-element.47), channel_id=1, source_target_pairs={{0,16},{16,0},{1,17},{17,1},{2,18},{18,2},{3,19},{19,3},{4,20},{20... | collective-permute-start | bytes 786440 | tf_op jit(solution)/shard_map/ppermute | solution.py:375
  23.2 9.7 %collective-permute-start.5 = (bf16[2,2,8,32,128]{4,3,2,1,0:T(8,128)(2,1)S(1)}, bf16[2,2,8,32,128]{4,3,2,1,0:T(8,128)(2,1)S(1)}, u32[]{:S(2)}, u32[]{:S(2)}) collective-permute-start(bf16[2,2,8,32,128]{4,3,2,1,0:T(8,128)(2,1)S(1)} %get-tuple-element.48), channel_id=1, source_target_pairs={{0,128},{128,0},{1,129},{129,1},{2,130},{130,2},{3,131},{131,3},{4... | collective-permute-start | bytes 786440 | tf_op jit(solution)/shard_map/ppermute | solution.py:375
  24.8 8.1 %collective-permute-start.6 = (bf16[2,2,6,6,512]{4,3,2,1,0:T(8,128)(2,1)S(1)}, bf16[2,2,6,6,512]{4,3,2,1,0:T(8,128)(2,1)S(1)}, u32[]{:S(2)}, u32[]{:S(2)}) collective-permute-start(bf16[2,2,6,6,512]{4,3,2,1,0:T(8,128)(2,1)S(1)} %get-tuple-element.49), channel_id=1, source_target_pairs={{0,7},{1,0},{2,1},{3,2},{4,3},{5,4},{6,5},{7,6},{8,15},{9,8},{10,9... | collective-permute-start | bytes 442376 | tf_op jit(solution)/shard_map/ppermute | solution.py:375
  33.0 5.2 %collective-permute-start.8 = (bf16[2,8,32,128]{3,2,1,0:T(8,128)(2,1)S(1)}, bf16[2,8,32,128]{3,2,1,0:T(8,128)(2,1)S(1)}, u32[]{:S(2)}, u32[]{:S(2)}) collective-permute-start(bf16[2,8,32,128]{3,2,1,0:T(8,128)(2,1)S(1)} %get-tuple-element.58), channel_id=1, source_target_pairs={{0,128},{128,0},{1,129},{129,1},{2,130},{130,2},{3,131},{131,3},{4... | collective-permute-start | bytes 393224 | tf_op jit(solution)/shard_map/ppermute | solution.py:375
  33.7 5.0 %collective-permute-start.9 = (bf16[2,8,32,128]{3,2,1,0:T(8,128)(2,1)S(1)}, bf16[2,8,32,128]{3,2,1,0:T(8,128)(2,1)S(1)}, u32[]{:S(2)}, u32[]{:S(2)}) collective-permute-start(bf16[2,8,32,128]{3,2,1,0:T(8,128)(2,1)S(1)} %get-tuple-element.59), channel_id=1, source_target_pairs={{0,16},{16,0},{1,17},{17,1},{2,18},{18,2},{3,19},{19,3},{4,20},{20... | collective-permute-start | bytes 393224 | tf_op jit(solution)/shard_map/ppermute | solution.py:375
  39.4 23.2 %all-to-all-start = ((bf16[32,32,128]{2,1,0:T(8,128)(2,1)}), bf16[32,32,128]{2,1,0:T(8,128)(2,1)S(1)}, u32[]{:S(2)}, u32[]{:S(2)}) async-start(bf16[32,32,128]{2,1,0:T(8,128)(2,1)} %bitcast.3), calls=%async_computation | async-start | bytes 524288 | tf_op jit(solution)/shard_map/all_to_all | solution.py:436
  49.6 13.2 %collective-permute-start.7 = (bf16[2,2,3,24,512]{4,3,2,1,0:T(8,128)(2,1)S(1)}, bf16[2,2,3,24,512]{4,3,2,1,0:T(8,128)(2,1)S(1)}, u32[]{:S(2)}, u32[]{:S(2)}) collective-permute-start(bf16[2,2,3,24,512]{4,3,2,1,0:T(8,128)(2,1)S(1)} %halo_rows.1), channel_id=1, source_target_pairs={{0,120},{8,0},{16,8},{24,16},{32,24},{40,32},{48,40},{56,48},{64,5... | collective-permute-start | bytes 884744 | tf_op jit(solution)/shard_map/ppermute | solution.py:375
  62.6 3.8 %collective-permute-start.10 = (f32[32,128]{1,0:T(8,128)S(1)}, f32[32,128]{1,0:T(8,128)S(1)}, u32[]{:S(2)}, u32[]{:S(2)}) collective-permute-start(f32[32,128]{1,0:T(8,128)S(1)} %convert_reduce_fusion.share_ref), channel_id=1, source_target_pairs={{0,128},{128,0},{1,129},{129,1},{2,130},{130,2},{3,131},{131,3},{4... | collective-permute-start | bytes 49160 | tf_op jit(solution)/shard_map/ppermute | solution.py:375

commit v9 on v7

--- a/solution.py
+++ b/solution.py
@@ -116,7 +116,7 @@
 
 
 def attention_kernel(
-    own_x_ref, own_u_ref, upper_ref, corner_ref, left_ref, lrow_ref, lcol_ref, wqkv_ref, wproj_ref,
+    own_x_ref, own_u_ref, left_ref, corner_ref, upper_ref, lrow_ref, lcol_ref, wqkv_ref, wproj_ref,
     send_ref, gp_ref, mix_ref, nkeep_ref, mkeep_ref, x_ref, u_ref,
     full_ref, proj_ref, gm_ref, nt_ref, mt_ref, al_ref, gl_ref, s_ref, da_ref, qs_ref, gs_ref,
 ):
@@ -337,7 +337,7 @@
             ((WIDE, LANES), low),
         ),
         5_000_000_000,
-        x, u, upper, corner, left, lrow, lcol, w_qkv, w_proj,
+        x, u, left, corner, upper, lrow, lcol, w_qkv, w_proj,
         limit=20,
     )
 
@@ -370,9 +370,9 @@
         *(pltpu.with_memory_space_constraint(array, pltpu.HBM) for array in (inputs, cotangent)),
         limit=8, any_args=(0, 1),
     )
+    left = passed_along(left, "lon", 1)
+    corner = diagonal(corner, 1)
     upper = passed_along(upper, LAT, 1)
-    corner = diagonal(corner, 1)
-    left = passed_along(left, "lon", 1)
     first_band = lax.axis_index(LAT) == 0
     wrapped = jnp.logical_and(first_band, jnp.arange(WLAT) < SLAT).astype(jnp.int32)
     groups = mask_ids + 4 * wrapped[:, None]

time: 66 us -> 66 us (level)
    ppermute x5, waiting for transfers between devices: 16.5 us -> 14.3 us  [passed_along(): return lax.ppermute(value, axis, pairs)]
    ppermute x1, waiting for transfers between devices: 0.78 us -> 2.73 us  [diagonal(): return lax.ppermute(value, (*LAT, 'lon'), pairs)]
    ppermute x5, starting transfers between devices: 4.08 us -> 4.91 us  [passed_along(): return lax.ppermute(value, axis, pairs)]
where the time goes in v9:
time: 66 us; the launch traced here: 65.7 us
  waiting for transfers between devices  31.2 us (47%)
  starting transfers between devices  17.8 us (27%)
  Pallas kernels  12.1 us (18%)
  local copies, waits for them, and re-layouts  2.95 us (4%)
  other arithmetic  0.76 us (1%)
  between operations  0.76 us (1%)
    ppermute x5, waiting for transfers between devices, passed_along(): return lax.ppermute(value, axis, pairs)  14.3 us
    pallas_call x8, Pallas kernels, call(): pl.pallas_call(kernel, out_shape=tuple((make(shape, dtype) for shape, dty...  12 us
    all_to_all x1, waiting for transfers between devices, per_device(): lax.all_to_all(sums.reshape(8, 512, 128), ('yh', 'x'), 0, 0, tiled=True)  10.1 us
    all_to_all x1, starting transfers between devices, per_device(): lax.all_to_all(sums.reshape(16, 64, 128), ('dp', 'lon'), 0, 0, tiled=True)  7.56 us
    ppermute x5, starting transfers between devices, passed_along(): return lax.ppermute(value, axis, pairs)  4.91 us
    all_to_all x1, starting transfers between devices, per_device(): lax.all_to_all(sums.reshape(8, 512, 128), ('yh', 'x'), 0, 0, tiled=True)  4.26 us
    all_to_all x1, waiting for transfers between devices, per_device(): lax.all_to_all(sums.reshape(16, 64, 128), ('dp', 'lon'), 0, 0, tiled=True)  4.14 us
    ppermute x1, waiting for transfers between devices, diagonal(): return lax.ppermute(value, (*LAT, 'lon'), pairs)  2.73 us
  transfers between devices with their start and end apart: 8, of which 7 were waited for; matrix products, arithmetic and copies ran while one was open for 2% of the time, Pallas kernels for 5%

profile of v9, /device:TPU:32, one launch (start us, length us, event | category | flops | bytes accessed | tf_op | source)
XLA Modules:
  0.0 65.7 jit_solution(1737049697017972653)
XLA Ops:
  0.7 1.2 %cut_halos.1 = (bf16[2,2,3,18,512]{4,3,2,1,0:T(8,128)(2,1)S(1)}, bf16[2,2,3,6,512]{4,3,2,1,0:T(8,128)(2,1)S(1)}, bf16[2,2,3,6,512]{4,3,2,1,0:T(8,128)(2,1)S(1)}) custom-call(bf16[1,2,6,24,512]{4,3,2,1,0:T(8,128)(2,1)} %own_x_ref.1, bf16[1,2,6,24,512]{4,3,2,1,0:T(8,128)(2,1)} %own_u_ref.1), custom_call_target="tpu_custom_call" | custom-call | flops 1000 | bytes 737280 | tf_op jit(solution)/shard_map/cut_halos/pallas_call | solution.py:299
  1.9 2.0 %collective-permute-start = (bf16[2,2,3,6,512]{4,3,2,1,0:T(8,128)(2,1)S(1)}, bf16[2,2,3,6,512]{4,3,2,1,0:T(8,128)(2,1)S(1)}, u32[]{:S(2)}, u32[]{:S(2)}) collective-permute-start(bf16[2,2,3,6,512]{4,3,2,1,0:T(8,128)(2,1)S(1)} %get-tuple-element.25), channel_id=1, source_target_pairs={{0,1},{1,2},{2,3},{3,4},{4,5},{5,6},{6,7},{7,0},{8,9},{9,10},{10,1... | collective-permute-start | bytes 221192 | tf_op jit(solution)/shard_map/ppermute | solution.py:351
  3.9 1.1 %collective-permute-start.1 = (bf16[2,2,3,6,512]{4,3,2,1,0:T(8,128)(2,1)S(1)}, bf16[2,2,3,6,512]{4,3,2,1,0:T(8,128)(2,1)S(1)}, u32[]{:S(2)}, u32[]{:S(2)}) collective-permute-start(bf16[2,2,3,6,512]{4,3,2,1,0:T(8,128)(2,1)S(1)} %get-tuple-element.26), channel_id=1, source_target_pairs={{0,9},{1,10},{2,11},{3,12},{4,13},{5,14},{6,15},{7,8},{8,17},{9,18... | collective-permute-start | bytes 221192 | tf_op jit(solution)/shard_map/ppermute | solution.py:361
  5.0 1.9 %collective-permute-start.2 = (bf16[2,2,3,18,512]{4,3,2,1,0:T(8,128)(2,1)S(1)}, bf16[2,2,3,18,512]{4,3,2,1,0:T(8,128)(2,1)S(1)}, u32[]{:S(2)}, u32[]{:S(2)}) collective-permute-start(bf16[2,2,3,18,512]{4,3,2,1,0:T(8,128)(2,1)S(1)} %get-tuple-element.27), channel_id=1, source_target_pairs={{0,8},{8,16},{16,24},{24,32},{32,40},{40,48},{48,56},{56,64},{64,7... | collective-permute-start | bytes 663560 | tf_op jit(solution)/shard_map/ppermute | solution.py:351
  6.9 0.8 %broadcast_add_fusion = s32[6,24]{1,0:T(8,128)S(1)} fusion(s32[6,24]{1,0:T(8,128)} %param.7, s32[6]{0:T(128)S(1)} %and_select_fusion), kind=kLoop, calls=%fused_computation.2 | loop fusion | flops 144 | bytes 1176 | tf_op jit(solution)/shard_map/add | solution.py:378
  7.6 0.1 reshape.35
  7.7 0.1 tile.21
  7.8 0.1 tile.23
  7.9 0.1 tile.27.lcol_ref
  8.1 0.1 tile.25
  8.1 1.4 %copy-done = bf16[512,1536]{1,0:T(8,128)(2,1)S(1)} copy-done((bf16[512,1536]{1,0:T(8,128)(2,1)S(1)}, bf16[512,1536]{1,0:T(8,128)(2,1)}, u32[]{:S(2)}) %copy-start) | copy-done | bytes 1572888
  9.5 1.0 %copy-done.2 = bf16[512,512]{1,0:T(8,128)(2,1)S(1)} copy-done((bf16[512,512]{1,0:T(8,128)(2,1)S(1)}, bf16[512,512]{1,0:T(8,128)(2,1)}, u32[]{:S(2)}) %copy-start.2) | copy-done | bytes 524312
  10.6 0.2 stage_weights.1
  10.8 0.0 collective-permute-done.left_ref
  10.8 2.7 %collective-permute-done.1.corner_ref = bf16[2,2,3,6,512]{4,3,2,1,0:T(8,128)(2,1)S(1)} collective-permute-done((bf16[2,2,3,6,512]{4,3,2,1,0:T(8,128)(2,1)S(1)}, bf16[2,2,3,6,512]{4,3,2,1,0:T(8,128)(2,1)S(1)}, u32[]{:S(2)}, u32[]{:S(2)}) %collective-permute-start.1) | collective-permute-done | bytes 73760 | tf_op jit(solution)/shard_map/ppermute | solution.py:361
  13.5 2.3 %collective-permute-done.2.upper_ref = bf16[2,2,3,18,512]{4,3,2,1,0:T(8,128)(2,1)S(1)} collective-permute-done((bf16[2,2,3,18,512]{4,3,2,1,0:T(8,128)(2,1)S(1)}, bf16[2,2,3,18,512]{4,3,2,1,0:T(8,128)(2,1)S(1)}, u32[]{:S(2)}, u32[]{:S(2)}) %collective-permute-start.2) | collective-permute-done | bytes 221216 | tf_op jit(solution)/shard_map/ppermute | solution.py:351
  15.9 5.1 %window_attention.1 = (bf16[32,2,64,128]{3,2,1,0:T(8,128)(2,1)S(1)}, bf16[288,1536]{1,0:T(8,128)(2,1)S(1)}, bf16[288,512]{1,0:T(8,128)(2,1)S(1)}, bf16[256,288]{...) custom-call(bf16[1,2,6,24,512]{4,3,2,1,0:T(8,128)(2,1)S(1)} %copy-do, ...), custom_call_target="tpu_custom_call" | custom-call | flops 5000000000 | bytes 6225920 | tf_op jit(solution)/shard_map/window_attention/pallas_call | solution.py:299
  21.0 0.1 collective-permute-start.3
  21.1 2.1 %own_half_and_outputs.1 = (f32[32,2,64,128]{3,2,1,0:T(8,128)S(1)}, bf16[2,2,6,18,512]{4,3,2,1,0:T(8,128)(2,1)S(1)}, bf16[2,2,6,6,512]{4,3,2,1,0:T(8,128)(2,1)S(1)}) custom-call(bf16[256,288]{1,0:T(8,128)(2,1)S(1)} %get-tuple-element.30.n_ref, bf16[256,288]{1,0:T(8,128)(2,1)S(1)} %get-tuple-element.31.m_ref, bf16[288,1536]{1,0:T(8,128)(2,1)S(1)} %get-tuple-element.32.gp_ref, ...), custom_call_target="tpu_custom_call" | custom-call | flops 600000000 | bytes 3276800 | tf_op jit(solution)/shard_map/own_half_and_outputs/pallas_call | solution.py:299
  23.2 0.5 collective-permute-done.3.got_ref
  23.7 1.2 %add_halves.1 = bf16[32,2,64,128]{3,2,1,0:T(8,128)(2,1)} custom-call(f32[32,2,64,128]{3,2,1,0:T(8,128)S(1)} %get-tuple-element.37.own_ref, bf16[32,2,64,128]{3,2,1,0:T(8,128)(2,1)S(1)} %collective-permute-done.3.got_ref), custom_call_target="tpu_custom_call" | custom-call | flops 1000000 | bytes 2097152 | tf_op jit(solution)/shard_map/add_halves/pallas_call | solution.py:299
  24.9 4.3 %all-to-all-start = ((bf16[8,512,128]{2,1,0:T(8,128)(2,1)}), bf16[8,512,128]{2,1,0:T(8,128)(2,1)S(1)}, u32[]{:S(2)}, u32[]{:S(2)}) async-start(bf16[8,512,128]{2,1,0:T(8,128)(2,1)} %bitcast.1), calls=%async_computation | async-start | bytes 2097152 | tf_op jit(solution)/shard_map/all_to_all | solution.py:397
  29.1 0.6 collective-permute-start.4
  29.7 6.9 %collective-permute-done.4.right_ref = bf16[2,2,6,6,512]{4,3,2,1,0:T(8,128)(2,1)S(1)} collective-permute-done((bf16[2,2,6,6,512]{4,3,2,1,0:T(8,128)(2,1)S(1)}, bf16[2,2,6,6,512]{4,3,2,1,0:T(8,128)(2,1)S(1)}, u32[]{:S(2)}, u32[]{:S(2)}) %collective-permute-start.4) | collective-permute-done | bytes 147488 | tf_op jit(solution)/shard_map/ppermute | solution.py:351
  36.6 10.1 %all-to-all-done.parts_ref = bf16[8,512,128]{2,1,0:T(8,128)(2,1)S(1)} async-done(((bf16[8,512,128]{2,1,0:T(8,128)(2,1)}), bf16[8,512,128]{2,1,0:T(8,128)(2,1)S(1)}, u32[]{:S(2)}, u32[]{:S(2)}) %all-to-all-start) | async-done | bytes 1048608 | tf_op jit(solution)/shard_map/all_to_all | solution.py:397
  46.6 0.8 %sum_parts.1 = bf16[2,512,128]{2,1,0:T(8,128)(2,1)} custom-call(bf16[8,512,128]{2,1,0:T(8,128)(2,1)S(1)} %all-to-all-done.parts_ref), custom_call_target="tpu_custom_call" | custom-call | flops 1000000 | bytes 524288 | tf_op jit(solution)/shard_map/sum_parts/pallas_call | solution.py:299
  47.5 7.6 %all-to-all-start.1 = ((bf16[16,64,128]{2,1,0:T(8,128)(2,1)}), bf16[16,64,128]{2,1,0:T(8,128)(2,1)S(1)}, u32[]{:S(2)}, u32[]{:S(2)}) async-start(bf16[16,64,128]{2,1,0:T(8,128)(2,1)} %bitcast.2), calls=%async_computation.1 | async-start | bytes 524288 | tf_op jit(solution)/shard_map/all_to_all | solution.py:400
  55.1 0.4 collective-permute-start.5
  55.4 4.6 %collective-permute-done.5.lower_ref = bf16[2,2,3,24,512]{4,3,2,1,0:T(8,128)(2,1)S(1)} collective-permute-done((bf16[2,2,3,24,512]{4,3,2,1,0:T(8,128)(2,1)S(1)}, bf16[2,2,3,24,512]{4,3,2,1,0:T(8,128)(2,1)S(1)}, u32[]{:S(2)}, u32[]{:S(2)}) %collective-permute-start.5) | collective-permute-done | bytes 294944 | tf_op jit(solution)/shard_map/ppermute | solution.py:351
  60.0 0.9 %join_outputs.1 = (bf16[1,2,6,24,512]{4,3,2,1,0:T(8,128)(2,1)}, bf16[1,2,6,24,512]{4,3,2,1,0:T(8,128)(2,1)}) custom-call(bf16[2,2,6,18,512]{4,3,2,1,0:T(8,128)(2,1)S(1)} %get-tuple-element.36.own_ref, bf16[2,2,6,6,512]{4,3,2,1,0:T(8,128)(2,1)S(1)} %collective-permute-done.4.right_ref, bf16[2,2,3,24,512]{4,3,2,1,0:T(8,128)(2,1)S(1)} %collective-permute-done.5.lower_ref), custom_call_target="tpu_custom_call" | custom-call | flops 1000 | bytes 1179648 | tf_op jit(solution)/shard_map/join_outputs/pallas_call | solution.py:299
  60.9 4.1 %all-to-all-done.1.parts_ref = bf16[16,64,128]{2,1,0:T(8,128)(2,1)S(1)} async-done(((bf16[16,64,128]{2,1,0:T(8,128)(2,1)}), bf16[16,64,128]{2,1,0:T(8,128)(2,1)S(1)}, u32[]{:S(2)}, u32[]{:S(2)}) %all-to-all-start.1) | async-done | bytes 262176 | tf_op jit(solution)/shard_map/all_to_all | solution.py:400
  65.0 0.6 last_sum.1
  (18 shorter events, 0.1 us)
Async XLA Ops:
  0.6 15.2 %copy-start.5 = (bf16[1,2,6,24,512]{4,3,2,1,0:T(8,128)(2,1)S(1)}, bf16[1,2,6,24,512]{4,3,2,1,0:T(8,128)(2,1)}, u32[]{:S(2)}) copy-start(bf16[1,2,6,24,512]{4,3,2,1,0:T(8,128)(2,1)} %own_u_ref.1) | copy-start | bytes 884740
  0.6 15.2 %copy-start.4 = (bf16[1,2,6,24,512]{4,3,2,1,0:T(8,128)(2,1)S(1)}, bf16[1,2,6,24,512]{4,3,2,1,0:T(8,128)(2,1)}, u32[]{:S(2)}) copy-start(bf16[1,2,6,24,512]{4,3,2,1,0:T(8,128)(2,1)} %own_x_ref.1) | copy-start | bytes 884740
  1.9 8.9 %collective-permute-start = (bf16[2,2,3,6,512]{4,3,2,1,0:T(8,128)(2,1)S(1)}, bf16[2,2,3,6,512]{4,3,2,1,0:T(8,128)(2,1)S(1)}, u32[]{:S(2)}, u32[]{:S(2)}) collective-permute-start(bf16[2,2,3,6,512]{4,3,2,1,0:T(8,128)(2,1)S(1)} %get-tuple-element.25), channel_id=1, source_target_pairs={{0,1},{1,2},{2,3},{3,4},{4,5},{5,6},{6,7},{7,0},{8,9},{9,10},{10,1... | collective-permute-start | bytes 221192 | tf_op jit(solution)/shard_map/ppermute | solution.py:351
  3.9 9.6 %collective-permute-start.1 = (bf16[2,2,3,6,512]{4,3,2,1,0:T(8,128)(2,1)S(1)}, bf16[2,2,3,6,512]{4,3,2,1,0:T(8,128)(2,1)S(1)}, u32[]{:S(2)}, u32[]{:S(2)}) collective-permute-start(bf16[2,2,3,6,512]{4,3,2,1,0:T(8,128)(2,1)S(1)} %get-tuple-element.26), channel_id=1, source_target_pairs={{0,9},{1,10},{2,11},{3,12},{4,13},{5,14},{6,15},{7,8},{8,17},{9,18... | collective-permute-start | bytes 221192 | tf_op jit(solution)/shard_map/ppermute | solution.py:361
  5.0 10.9 %collective-permute-start.2 = (bf16[2,2,3,18,512]{4,3,2,1,0:T(8,128)(2,1)S(1)}, bf16[2,2,3,18,512]{4,3,2,1,0:T(8,128)(2,1)S(1)}, u32[]{:S(2)}, u32[]{:S(2)}) collective-permute-start(bf16[2,2,3,18,512]{4,3,2,1,0:T(8,128)(2,1)S(1)} %get-tuple-element.27), channel_id=1, source_target_pairs={{0,8},{8,16},{16,24},{24,32},{32,40},{40,48},{48,56},{56,64},{64,7... | collective-permute-start | bytes 663560 | tf_op jit(solution)/shard_map/ppermute | solution.py:351
  8.1 1.4 %copy-start = (bf16[512,1536]{1,0:T(8,128)(2,1)S(1)}, bf16[512,1536]{1,0:T(8,128)(2,1)}, u32[]{:S(2)}) copy-start(bf16[512,1536]{1,0:T(8,128)(2,1)} %qkv_ref.3) | copy-start | bytes 4718596
  9.5 1.0 %copy-start.2 = (bf16[512,512]{1,0:T(8,128)(2,1)S(1)}, bf16[512,512]{1,0:T(8,128)(2,1)}, u32[]{:S(2)}) copy-start(bf16[512,512]{1,0:T(8,128)(2,1)} %proj_ref.3) | copy-start | bytes 1572868
  15.9 5.2 %copy-start.1 = (bf16[512,1536]{1,0:T(8,128)(2,1)S(1)}, bf16[512,1536]{1,0:T(8,128)(2,1)}, u32[]{:S(2)}) copy-start(bf16[512,1536]{1,0:T(8,128)(2,1)} %qkv_ref.3) | copy-start | bytes 4718596
  15.9 5.2 %copy-start.3 = (bf16[512,512]{1,0:T(8,128)(2,1)S(1)}, bf16[512,512]{1,0:T(8,128)(2,1)}, u32[]{:S(2)}) copy-start(bf16[512,512]{1,0:T(8,128)(2,1)} %proj_ref.3) | copy-start | bytes 1572868
  21.0 2.7 %collective-permute-start.3 = (bf16[32,2,64,128]{3,2,1,0:T(8,128)(2,1)S(1)}, bf16[32,2,64,128]{3,2,1,0:T(8,128)(2,1)S(1)}, u32[]{:S(2)}, u32[]{:S(2)}) collective-permute-start(bf16[32,2,64,128]{3,2,1,0:T(8,128)(2,1)S(1)} %get-tuple-element.38), channel_id=1, source_target_pairs={{0,8},{8,0},{1,9},{9,1},{2,10},{10,2},{3,11},{11,3},{4,12},{12,4},... | collective-permute-start | bytes 3145736 | tf_op jit(solution)/shard_map/ppermute | solution.py:351
  24.9 21.8 %all-to-all-start = ((bf16[8,512,128]{2,1,0:T(8,128)(2,1)}), bf16[8,512,128]{2,1,0:T(8,128)(2,1)S(1)}, u32[]{:S(2)}, u32[]{:S(2)}) async-start(bf16[8,512,128]{2,1,0:T(8,128)(2,1)} %bitcast.1), calls=%async_computation | async-start | bytes 2097152 | tf_op jit(solution)/shard_map/all_to_all | solution.py:397
  29.1 7.4 %collective-permute-start.4 = (bf16[2,2,6,6,512]{4,3,2,1,0:T(8,128)(2,1)S(1)}, bf16[2,2,6,6,512]{4,3,2,1,0:T(8,128)(2,1)S(1)}, u32[]{:S(2)}, u32[]{:S(2)}) collective-permute-start(bf16[2,2,6,6,512]{4,3,2,1,0:T(8,128)(2,1)S(1)} %get-tuple-element.39), channel_id=1, source_target_pairs={{0,7},{1,0},{2,1},{3,2},{4,3},{5,4},{6,5},{7,6},{8,15},{9,8},{10,9... | collective-permute-start | bytes 442376 | tf_op jit(solution)/shard_map/ppermute | solution.py:351
  47.5 17.6 %all-to-all-start.1 = ((bf16[16,64,128]{2,1,0:T(8,128)(2,1)}), bf16[16,64,128]{2,1,0:T(8,128)(2,1)S(1)}, u32[]{:S(2)}, u32[]{:S(2)}) async-start(bf16[16,64,128]{2,1,0:T(8,128)(2,1)} %bitcast.2), calls=%async_computation.1 | async-start | bytes 524288 | tf_op jit(solution)/shard_map/all_to_all | solution.py:400
  55.1 5.0 %collective-permute-start.5 = (bf16[2,2,3,24,512]{4,3,2,1,0:T(8,128)(2,1)S(1)}, bf16[2,2,3,24,512]{4,3,2,1,0:T(8,128)(2,1)S(1)}, u32[]{:S(2)}, u32[]{:S(2)}) collective-permute-start(bf16[2,2,3,24,512]{4,3,2,1,0:T(8,128)(2,1)S(1)} %halo_rows.1), channel_id=1, source_target_pairs={{0,120},{8,0},{16,8},{24,16},{32,24},{40,32},{48,40},{56,48},{64,5... | collective-permute-start | bytes 884744 | tf_op jit(solution)/shard_map/ppermute | solution.py:351

commit v10 on v7

--- a/solution.py
+++ b/solution.py
@@ -200,7 +200,10 @@
 
 
 def add_kernel(own_ref, got_ref, sum_ref):
-    sum_ref[...] = (own_ref[...] + got_ref[...].astype(jnp.float32)).astype(jnp.bfloat16)
+    for yh in range(own_ref.shape[0]):
+        for x in range(own_ref.shape[1]):
+            total = own_ref[yh, x] + got_ref[yh, x].astype(jnp.float32)
+            sum_ref[x, yh] = total.astype(jnp.bfloat16)
 
 
 def added(parts_ref):
@@ -211,9 +214,9 @@
 
 
 def sum_kernel(parts_ref, sum_ref):
-    total = added(parts_ref).astype(jnp.bfloat16)
-    sum_ref[0] = total
-    sum_ref[1] = total
+    total = added(parts_ref).astype(jnp.bfloat16).reshape(8, 64, 128)
+    sum_ref[:, 0] = total
+    sum_ref[:, 1] = total
 
 
 def last_kernel(parts_ref, qkv_ref, proj_ref):
@@ -392,12 +395,16 @@
         nkeep, mkeep, gp, u, x, mix, w_qkv, w_proj,
         dtypes=(jnp.float32,) + (jnp.bfloat16,) * 2, any_args=(6, 7), limit=16,
     )
-    (sums,) = call(add_kernel, "add_halves", (send.shape,), (), 1_000_000, half, got, placed=True)
+    ranks = (2, 4, 8, 64, 128)
+    (sums,) = call(
+        add_kernel, "add_halves", ((4, 2, 8, 64, 128),), (), 1_000_000,
+        half.reshape(ranks), got.reshape(ranks), placed=True,
+    )
     right = passed_along(left, "lon", -1)
-    spread = lax.all_to_all(sums.reshape(8, 512, 128), ("yh", "x"), 0, 0, tiled=True)
+    spread = lax.all_to_all(sums.reshape(8, 512, 128), ("x", "yh"), 0, 0, tiled=True)
     spread, right = lax.optimization_barrier((spread, right))
-    (sums,) = call(sum_kernel, "sum_parts", ((2, 512, 128),), (), 1_000_000, spread, placed=True)
-    spread = lax.all_to_all(sums.reshape(16, 64, 128), ("dp", "lon"), 0, 0, tiled=True)
+    (sums,) = call(sum_kernel, "sum_parts", ((8, 2, 64, 128),), (), 1_000_000, spread, placed=True)
+    spread = lax.all_to_all(sums.reshape(16, 64, 128), ("lon", "dp"), 0, 0, tiled=True)
     grad_qkv, grad_proj = call(
         last_kernel, "last_sum", ((4, 3 * D), (4, D)), (), 1000, spread,
         dtypes=(jnp.float32,) * 2, limit=4,

time: 66 us -> 66.3 us (level)
  the two profiles are of different devices: /device:TPU:32 before, /device:TPU:4 now
where the time goes in v10:
time: 66.3 us; the launch traced here: 66 us
  waiting for transfers between devices  25.9 us (39%)
  starting transfers between devices  23.4 us (35%)
  Pallas kernels  12.2 us (18%)
  local copies, waits for them, and re-layouts  2.96 us (4%)
  between operations  0.79 us (1%)
  other arithmetic  0.76 us (1%)
    pallas_call x8, Pallas kernels, call(): pl.pallas_call(kernel, out_shape=tuple((make(shape, dtype) for shape, dty...  12 us
    ppermute x5, waiting for transfers between devices, passed_along(): return lax.ppermute(value, axis, pairs)  11.2 us
    all_to_all x1, starting transfers between devices, per_device(): lax.all_to_all(sums.reshape(16, 64, 128), ('lon', 'dp'), 0, 0, tiled=True)  7.81 us
    all_to_all x1, waiting for transfers between devices, per_device(): lax.all_to_all(sums.reshape(8, 512, 128), ('x', 'yh'), 0, 0, tiled=True)  7.74 us
    all_to_all x1, starting transfers between devices, per_device(): lax.all_to_all(sums.reshape(8, 512, 128), ('x', 'yh'), 0, 0, tiled=True)  7.44 us
    all_to_all x1, waiting for transfers between devices, per_device(): lax.all_to_all(sums.reshape(16, 64, 128), ('lon', 'dp'), 0, 0, tiled=True)  6.97 us
    ppermute x5, starting transfers between devices, passed_along(): return lax.ppermute(value, axis, pairs)  6.73 us
    unnamed x12, local copies, waits for them, and re-layouts  2.47 us
  transfers between devices with their start and end apart: 8, of which 6 were waited for; matrix products, arithmetic and copies ran while one was open for 2% of the time, Pallas kernels for 5%

profile of v10, /device:TPU:4, one launch (start us, length us, event | category | flops | bytes accessed | tf_op | source)
XLA Modules:
  0.0 66.0 jit_solution(8647409488565174391)
XLA Ops:
  0.7 1.2 %cut_halos.1 = (bf16[2,2,3,18,512]{4,3,2,1,0:T(8,128)(2,1)S(1)}, bf16[2,2,3,6,512]{4,3,2,1,0:T(8,128)(2,1)S(1)}, bf16[2,2,3,6,512]{4,3,2,1,0:T(8,128)(2,1)S(1)}) custom-call(bf16[1,2,6,24,512]{4,3,2,1,0:T(8,128)(2,1)} %own_x_ref.1, bf16[1,2,6,24,512]{4,3,2,1,0:T(8,128)(2,1)} %own_u_ref.1), custom_call_target="tpu_custom_call" | custom-call | flops 1000 | bytes 737280 | tf_op jit(solution)/shard_map/cut_halos/pallas_call | solution.py:302
  1.9 1.4 %collective-permute-start.1 = (bf16[2,2,3,6,512]{4,3,2,1,0:T(8,128)(2,1)S(1)}, bf16[2,2,3,6,512]{4,3,2,1,0:T(8,128)(2,1)S(1)}, u32[]{:S(2)}, u32[]{:S(2)}) collective-permute-start(bf16[2,2,3,6,512]{4,3,2,1,0:T(8,128)(2,1)S(1)} %get-tuple-element.26), channel_id=1, source_target_pairs={{0,9},{1,10},{2,11},{3,12},{4,13},{5,14},{6,15},{7,8},{8,17},{9,18... | collective-permute-start | bytes 221192 | tf_op jit(solution)/shard_map/ppermute | solution.py:364
  3.3 1.9 %collective-permute-start.2 = (bf16[2,2,3,6,512]{4,3,2,1,0:T(8,128)(2,1)S(1)}, bf16[2,2,3,6,512]{4,3,2,1,0:T(8,128)(2,1)S(1)}, u32[]{:S(2)}, u32[]{:S(2)}) collective-permute-start(bf16[2,2,3,6,512]{4,3,2,1,0:T(8,128)(2,1)S(1)} %get-tuple-element.27), channel_id=1, source_target_pairs={{0,1},{1,2},{2,3},{3,4},{4,5},{5,6},{6,7},{7,0},{8,9},{9,10},{10,1... | collective-permute-start | bytes 221192 | tf_op jit(solution)/shard_map/ppermute | solution.py:354
  5.3 1.0 %collective-permute-start = (bf16[2,2,3,18,512]{4,3,2,1,0:T(8,128)(2,1)S(1)}, bf16[2,2,3,18,512]{4,3,2,1,0:T(8,128)(2,1)S(1)}, u32[]{:S(2)}, u32[]{:S(2)}) collective-permute-start(bf16[2,2,3,18,512]{4,3,2,1,0:T(8,128)(2,1)S(1)} %get-tuple-element.25), channel_id=1, source_target_pairs={{0,8},{8,16},{16,24},{24,32},{32,40},{40,48},{48,56},{56,64},{64,7... | collective-permute-start | bytes 663560 | tf_op jit(solution)/shard_map/ppermute | solution.py:354
  6.3 0.8 %broadcast_add_fusion = s32[6,24]{1,0:T(8,128)S(1)} fusion(s32[6,24]{1,0:T(8,128)} %param.7, s32[6]{0:T(128)S(1)} %and_select_fusion), kind=kLoop, calls=%fused_computation.2 | loop fusion | flops 144 | bytes 1176 | tf_op jit(solution)/shard_map/add | solution.py:381
  7.1 0.1 reshape.41
  7.1 0.1 tile.21
  7.2 0.1 tile.23
  7.3 0.1 tile.27.lcol_ref
  7.5 0.1 tile.25
  7.6 1.4 %copy-done = bf16[512,1536]{1,0:T(8,128)(2,1)S(1)} copy-done((bf16[512,1536]{1,0:T(8,128)(2,1)S(1)}, bf16[512,1536]{1,0:T(8,128)(2,1)}, u32[]{:S(2)}) %copy-start) | copy-done | bytes 1572888
  9.0 1.0 %copy-done.2 = bf16[512,512]{1,0:T(8,128)(2,1)S(1)} copy-done((bf16[512,512]{1,0:T(8,128)(2,1)S(1)}, bf16[512,512]{1,0:T(8,128)(2,1)}, u32[]{:S(2)}) %copy-start.2) | copy-done | bytes 524312
  10.0 0.2 stage_weights.1
  10.2 2.5 %collective-permute-done.2.left_ref = bf16[2,2,3,6,512]{4,3,2,1,0:T(8,128)(2,1)S(1)} collective-permute-done((bf16[2,2,3,6,512]{4,3,2,1,0:T(8,128)(2,1)S(1)}, bf16[2,2,3,6,512]{4,3,2,1,0:T(8,128)(2,1)S(1)}, u32[]{:S(2)}, u32[]{:S(2)}) %collective-permute-start.2) | collective-permute-done | bytes 73760 | tf_op jit(solution)/shard_map/ppermute | solution.py:354
  12.8 0.0 copy-start.1
  12.8 0.0 copy-start.3
  12.8 5.1 %window_attention.1 = (bf16[32,2,64,128]{3,2,1,0:T(8,128)(2,1)S(1)}, bf16[288,1536]{1,0:T(8,128)(2,1)S(1)}, bf16[288,512]{1,0:T(8,128)(2,1)S(1)}, bf16[256,288]{...) custom-call(bf16[1,2,6,24,512]{4,3,2,1,0:T(8,128)(2,1)S(1)} %copy-do, ...), custom_call_target="tpu_custom_call" | custom-call | flops 5000000000 | bytes 6225920 | tf_op jit(solution)/shard_map/window_attention/pallas_call | solution.py:302
  17.9 0.1 collective-permute-start.3
  18.0 2.1 %own_half_and_outputs.1 = (f32[32,2,64,128]{3,2,1,0:T(8,128)S(1)}, bf16[2,2,6,18,512]{4,3,2,1,0:T(8,128)(2,1)S(1)}, bf16[2,2,6,6,512]{4,3,2,1,0:T(8,128)(2,1)S(1)}) custom-call(bf16[256,288]{1,0:T(8,128)(2,1)S(1)} %get-tuple-element.30.n_ref, bf16[256,288]{1,0:T(8,128)(2,1)S(1)} %get-tuple-element.31.m_ref, bf16[288,1536]{1,0:T(8,128)(2,1)S(1)} %get-tuple-element.32.gp_ref, ...), custom_call_target="tpu_custom_call" | custom-call | flops 600000000 | bytes 3276800 | tf_op jit(solution)/shard_map/own_half_and_outputs/pallas_call | solution.py:302
  20.1 0.5 collective-permute-done.3
  20.6 1.2 %add_halves.1 = bf16[4,2,8,64,128]{4,3,2,1,0:T(8,128)(2,1)} custom-call(f32[2,4,8,64,128]{4,3,2,1,0:T(8,128)S(1)} %bitcast.7, bf16[2,4,8,64,128]{4,3,2,1,0:T(8,128)(2,1)S(1)} %bitcast.8), custom_call_target="tpu_custom_call" | custom-call | flops 1000000 | bytes 2097152 | tf_op jit(solution)/shard_map/add_halves/pallas_call | solution.py:302
  21.8 7.4 %all-to-all-start = ((bf16[8,512,128]{2,1,0:T(8,128)(2,1)}), bf16[8,512,128]{2,1,0:T(8,128)(2,1)S(1)}, u32[]{:S(2)}, u32[]{:S(2)}) async-start(bf16[8,512,128]{2,1,0:T(8,128)(2,1)} %bitcast.3), calls=%async_computation | async-start | bytes 2097152 | tf_op jit(solution)/shard_map/all_to_all | solution.py:404
  29.2 3.6 %collective-permute-start.4 = (bf16[2,2,6,6,512]{4,3,2,1,0:T(8,128)(2,1)S(1)}, bf16[2,2,6,6,512]{4,3,2,1,0:T(8,128)(2,1)S(1)}, u32[]{:S(2)}, u32[]{:S(2)}) collective-permute-start(bf16[2,2,6,6,512]{4,3,2,1,0:T(8,128)(2,1)S(1)} %get-tuple-element.39), channel_id=1, source_target_pairs={{0,7},{1,0},{2,1},{3,2},{4,3},{5,4},{6,5},{7,6},{8,15},{9,8},{10,9... | collective-permute-start | bytes 442376 | tf_op jit(solution)/shard_map/ppermute | solution.py:354
  32.8 3.9 %collective-permute-done.4.right_ref = bf16[2,2,6,6,512]{4,3,2,1,0:T(8,128)(2,1)S(1)} collective-permute-done((bf16[2,2,6,6,512]{4,3,2,1,0:T(8,128)(2,1)S(1)}, bf16[2,2,6,6,512]{4,3,2,1,0:T(8,128)(2,1)S(1)}, u32[]{:S(2)}, u32[]{:S(2)}) %collective-permute-start.4) | collective-permute-done | bytes 147488 | tf_op jit(solution)/shard_map/ppermute | solution.py:354
  36.7 7.7 %all-to-all-done.parts_ref = bf16[8,512,128]{2,1,0:T(8,128)(2,1)S(1)} async-done(((bf16[8,512,128]{2,1,0:T(8,128)(2,1)}), bf16[8,512,128]{2,1,0:T(8,128)(2,1)S(1)}, u32[]{:S(2)}, u32[]{:S(2)}) %all-to-all-start) | async-done | bytes 1048608 | tf_op jit(solution)/shard_map/all_to_all | solution.py:404
  44.5 0.8 %sum_parts.1 = bf16[8,2,64,128]{3,2,1,0:T(8,128)(2,1)} custom-call(bf16[8,512,128]{2,1,0:T(8,128)(2,1)S(1)} %all-to-all-done.parts_ref), custom_call_target="tpu_custom_call" | custom-call | flops 1000000 | bytes 524288 | tf_op jit(solution)/shard_map/sum_parts/pallas_call | solution.py:302
  45.3 7.8 %all-to-all-start.1 = ((bf16[16,64,128]{2,1,0:T(8,128)(2,1)}), bf16[16,64,128]{2,1,0:T(8,128)(2,1)S(1)}, u32[]{:S(2)}, u32[]{:S(2)}) async-start(bf16[16,64,128]{2,1,0:T(8,128)(2,1)} %bitcast.4), calls=%async_computation.1 | async-start | bytes 524288 | tf_op jit(solution)/shard_map/all_to_all | solution.py:407
  53.2 0.1 collective-permute-start.5
  53.3 4.2 %collective-permute-done.5.lower_ref = bf16[2,2,3,24,512]{4,3,2,1,0:T(8,128)(2,1)S(1)} collective-permute-done((bf16[2,2,3,24,512]{4,3,2,1,0:T(8,128)(2,1)S(1)}, bf16[2,2,3,24,512]{4,3,2,1,0:T(8,128)(2,1)S(1)}, u32[]{:S(2)}, u32[]{:S(2)}) %collective-permute-start.5) | collective-permute-done | bytes 294944 | tf_op jit(solution)/shard_map/ppermute | solution.py:354
  57.5 0.9 %join_outputs.1 = (bf16[1,2,6,24,512]{4,3,2,1,0:T(8,128)(2,1)}, bf16[1,2,6,24,512]{4,3,2,1,0:T(8,128)(2,1)}) custom-call(bf16[2,2,6,18,512]{4,3,2,1,0:T(8,128)(2,1)S(1)} %get-tuple-element.36.own_ref, bf16[2,2,6,6,512]{4,3,2,1,0:T(8,128)(2,1)S(1)} %collective-permute-done.4.right_ref, bf16[2,2,3,24,512]{4,3,2,1,0:T(8,128)(2,1)S(1)} %collective-permute-done.5.lower_ref), custom_call_target="tpu_custom_call" | custom-call | flops 1000 | bytes 1179648 | tf_op jit(solution)/shard_map/join_outputs/pallas_call | solution.py:302
  58.4 7.0 %all-to-all-done.1.parts_ref = bf16[16,64,128]{2,1,0:T(8,128)(2,1)S(1)} async-done(((bf16[16,64,128]{2,1,0:T(8,128)(2,1)}), bf16[16,64,128]{2,1,0:T(8,128)(2,1)S(1)}, u32[]{:S(2)}, u32[]{:S(2)}) %all-to-all-start.1) | async-done | bytes 262176 | tf_op jit(solution)/shard_map/all_to_all | solution.py:407
  65.3 0.6 last_sum.1
  (18 shorter events, 0.1 us)
Async XLA Ops:
  0.6 12.1 %copy-start.5 = (bf16[1,2,6,24,512]{4,3,2,1,0:T(8,128)(2,1)S(1)}, bf16[1,2,6,24,512]{4,3,2,1,0:T(8,128)(2,1)}, u32[]{:S(2)}) copy-start(bf16[1,2,6,24,512]{4,3,2,1,0:T(8,128)(2,1)} %own_u_ref.1) | copy-start | bytes 884740
  0.6 12.1 %copy-start.4 = (bf16[1,2,6,24,512]{4,3,2,1,0:T(8,128)(2,1)S(1)}, bf16[1,2,6,24,512]{4,3,2,1,0:T(8,128)(2,1)}, u32[]{:S(2)}) copy-start(bf16[1,2,6,24,512]{4,3,2,1,0:T(8,128)(2,1)} %own_x_ref.1) | copy-start | bytes 884740
  1.9 8.3 %collective-permute-start.1 = (bf16[2,2,3,6,512]{4,3,2,1,0:T(8,128)(2,1)S(1)}, bf16[2,2,3,6,512]{4,3,2,1,0:T(8,128)(2,1)S(1)}, u32[]{:S(2)}, u32[]{:S(2)}) collective-permute-start(bf16[2,2,3,6,512]{4,3,2,1,0:T(8,128)(2,1)S(1)} %get-tuple-element.26), channel_id=1, source_target_pairs={{0,9},{1,10},{2,11},{3,12},{4,13},{5,14},{6,15},{7,8},{8,17},{9,18... | collective-permute-start | bytes 221192 | tf_op jit(solution)/shard_map/ppermute | solution.py:364
  3.3 9.4 %collective-permute-start.2 = (bf16[2,2,3,6,512]{4,3,2,1,0:T(8,128)(2,1)S(1)}, bf16[2,2,3,6,512]{4,3,2,1,0:T(8,128)(2,1)S(1)}, u32[]{:S(2)}, u32[]{:S(2)}) collective-permute-start(bf16[2,2,3,6,512]{4,3,2,1,0:T(8,128)(2,1)S(1)} %get-tuple-element.27), channel_id=1, source_target_pairs={{0,1},{1,2},{2,3},{3,4},{4,5},{5,6},{6,7},{7,0},{8,9},{9,10},{10,1... | collective-permute-start | bytes 221192 | tf_op jit(solution)/shard_map/ppermute | solution.py:354
  5.3 7.5 %collective-permute-start = (bf16[2,2,3,18,512]{4,3,2,1,0:T(8,128)(2,1)S(1)}, bf16[2,2,3,18,512]{4,3,2,1,0:T(8,128)(2,1)S(1)}, u32[]{:S(2)}, u32[]{:S(2)}) collective-permute-start(bf16[2,2,3,18,512]{4,3,2,1,0:T(8,128)(2,1)S(1)} %get-tuple-element.25), channel_id=1, source_target_pairs={{0,8},{8,16},{16,24},{24,32},{32,40},{40,48},{48,56},{56,64},{64,7... | collective-permute-start | bytes 663560 | tf_op jit(solution)/shard_map/ppermute | solution.py:354
  7.6 1.4 %copy-start = (bf16[512,1536]{1,0:T(8,128)(2,1)S(1)}, bf16[512,1536]{1,0:T(8,128)(2,1)}, u32[]{:S(2)}) copy-start(bf16[512,1536]{1,0:T(8,128)(2,1)} %qkv_ref.3) | copy-start | bytes 4718596
  9.0 1.0 %copy-start.2 = (bf16[512,512]{1,0:T(8,128)(2,1)S(1)}, bf16[512,512]{1,0:T(8,128)(2,1)}, u32[]{:S(2)}) copy-start(bf16[512,512]{1,0:T(8,128)(2,1)} %proj_ref.3) | copy-start | bytes 1572868
  12.8 5.2 %copy-start.1 = (bf16[512,1536]{1,0:T(8,128)(2,1)S(1)}, bf16[512,1536]{1,0:T(8,128)(2,1)}, u32[]{:S(2)}) copy-start(bf16[512,1536]{1,0:T(8,128)(2,1)} %qkv_ref.3) | copy-start | bytes 4718596
  12.8 5.2 %copy-start.3 = (bf16[512,512]{1,0:T(8,128)(2,1)S(1)}, bf16[512,512]{1,0:T(8,128)(2,1)}, u32[]{:S(2)}) copy-start(bf16[512,512]{1,0:T(8,128)(2,1)} %proj_ref.3) | copy-start | bytes 1572868
  17.9 2.7 %collective-permute-start.3 = (bf16[32,2,64,128]{3,2,1,0:T(8,128)(2,1)S(1)}, bf16[32,2,64,128]{3,2,1,0:T(8,128)(2,1)S(1)}, u32[]{:S(2)}, u32[]{:S(2)}) collective-permute-start(bf16[32,2,64,128]{3,2,1,0:T(8,128)(2,1)S(1)} %get-tuple-element.38), channel_id=1, source_target_pairs={{0,8},{8,0},{1,9},{9,1},{2,10},{10,2},{3,11},{11,3},{4,12},{12,4},... | collective-permute-start | bytes 3145736 | tf_op jit(solution)/shard_map/ppermute | solution.py:354
  21.8 22.7 %all-to-all-start = ((bf16[8,512,128]{2,1,0:T(8,128)(2,1)}), bf16[8,512,128]{2,1,0:T(8,128)(2,1)S(1)}, u32[]{:S(2)}, u32[]{:S(2)}) async-start(bf16[8,512,128]{2,1,0:T(8,128)(2,1)} %bitcast.3), calls=%async_computation | async-start | bytes 2097152 | tf_op jit(solution)/shard_map/all_to_all | solution.py:404
  29.2 7.5 %collective-permute-start.4 = (bf16[2,2,6,6,512]{4,3,2,1,0:T(8,128)(2,1)S(1)}, bf16[2,2,6,6,512]{4,3,2,1,0:T(8,128)(2,1)S(1)}, u32[]{:S(2)}, u32[]{:S(2)}) collective-permute-start(bf16[2,2,6,6,512]{4,3,2,1,0:T(8,128)(2,1)S(1)} %get-tuple-element.39), channel_id=1, source_target_pairs={{0,7},{1,0},{2,1},{3,2},{4,3},{5,4},{6,5},{7,6},{8,15},{9,8},{10,9... | collective-permute-start | bytes 442376 | tf_op jit(solution)/shard_map/ppermute | solution.py:354
  45.3 20.0 %all-to-all-start.1 = ((bf16[16,64,128]{2,1,0:T(8,128)(2,1)}), bf16[16,64,128]{2,1,0:T(8,128)(2,1)S(1)}, u32[]{:S(2)}, u32[]{:S(2)}) async-start(bf16[16,64,128]{2,1,0:T(8,128)(2,1)} %bitcast.4), calls=%async_computation.1 | async-start | bytes 524288 | tf_op jit(solution)/shard_map/all_to_all | solution.py:407
  53.2 4.3 %collective-permute-start.5 = (bf16[2,2,3,24,512]{4,3,2,1,0:T(8,128)(2,1)S(1)}, bf16[2,2,3,24,512]{4,3,2,1,0:T(8,128)(2,1)S(1)}, u32[]{:S(2)}, u32[]{:S(2)}) collective-permute-start(bf16[2,2,3,24,512]{4,3,2,1,0:T(8,128)(2,1)S(1)} %halo_rows.1), channel_id=1, source_target_pairs={{0,120},{8,0},{16,8},{24,16},{32,24},{40,32},{48,40},{56,48},{64,5... | collective-permute-start | bytes 884744 | tf_op jit(solution)/shard_map/ppermute | solution.py:354

commit v11 on v10

--- a/solution.py
+++ b/solution.py
@@ -214,9 +214,9 @@
 
 
 def sum_kernel(parts_ref, sum_ref):
-    total = added(parts_ref).astype(jnp.bfloat16).reshape(8, 64, 128)
-    sum_ref[:, 0] = total
-    sum_ref[:, 1] = total
+    total = added(parts_ref).astype(jnp.bfloat16)
+    sum_ref[0] = total
+    sum_ref[1] = total
 
 
 def last_kernel(parts_ref, qkv_ref, proj_ref):
@@ -403,8 +403,8 @@
     right = passed_along(left, "lon", -1)
     spread = lax.all_to_all(sums.reshape(8, 512, 128), ("x", "yh"), 0, 0, tiled=True)
     spread, right = lax.optimization_barrier((spread, right))
-    (sums,) = call(sum_kernel, "sum_parts", ((8, 2, 64, 128),), (), 1_000_000, spread, placed=True)
-    spread = lax.all_to_all(sums.reshape(16, 64, 128), ("lon", "dp"), 0, 0, tiled=True)
+    (sums,) = call(sum_kernel, "sum_parts", ((2, 512, 128),), (), 1_000_000, spread, placed=True)
+    spread = lax.all_to_all(sums.reshape(16, 64, 128), ("dp", "lon"), 0, 0, tiled=True)
     grad_qkv, grad_proj = call(
         last_kernel, "last_sum", ((4, 3 * D), (4, D)), (), 1000, spread,
         dtypes=(jnp.float32,) * 2, limit=4,

time: 66.3 us -> 65 us (0.980)
  the two profiles are of different devices: /device:TPU:4 before, /device:TPU:32 now
where the time goes in v11:
time: 65 us; the launch traced here: 64.6 us
  waiting for transfers between devices  28.8 us (44%)
  starting transfers between devices  19.2 us (30%)
  Pallas kernels  12.2 us (19%)
  local copies, waits for them, and re-layouts  2.95 us (5%)
  other arithmetic  0.76 us (1%)
  between operations  0.75 us (1%)
    ppermute x5, waiting for transfers between devices, passed_along(): return lax.ppermute(value, axis, pairs)  16.3 us
    pallas_call x8, Pallas kernels, call(): pl.pallas_call(kernel, out_shape=tuple((make(shape, dtype) for shape, dty...  12 us
    all_to_all x1, waiting for transfers between devices, per_device(): lax.all_to_all(sums.reshape(8, 512, 128), ('x', 'yh'), 0, 0, tiled=True)  8.45 us
    all_to_all x1, starting transfers between devices, per_device(): lax.all_to_all(sums.reshape(16, 64, 128), ('dp', 'lon'), 0, 0, tiled=True)  8.44 us
    ppermute x5, starting transfers between devices, passed_along(): return lax.ppermute(value, axis, pairs)  4.84 us
    all_to_all x1, starting transfers between devices, per_device(): lax.all_to_all(sums.reshape(8, 512, 128), ('x', 'yh'), 0, 0, tiled=True)  4.47 us
    all_to_all x1, waiting for transfers between devices, per_device(): lax.all_to_all(sums.reshape(16, 64, 128), ('dp', 'lon'), 0, 0, tiled=True)  3.29 us
    unnamed x12, local copies, waits for them, and re-layouts  2.47 us
  transfers between devices with their start and end apart: 8, of which 7 were waited for; matrix products, arithmetic and copies ran while one was open for 2% of the time, Pallas kernels for 5%

profile of v11, /device:TPU:32, one launch (start us, length us, event | category | flops | bytes accessed | tf_op | source)
XLA Modules:
  0.0 64.6 jit_solution(16364629172380571962)
XLA Ops:
  0.7 1.2 %cut_halos.1 = (bf16[2,2,3,18,512]{4,3,2,1,0:T(8,128)(2,1)S(1)}, bf16[2,2,3,6,512]{4,3,2,1,0:T(8,128)(2,1)S(1)}, bf16[2,2,3,6,512]{4,3,2,1,0:T(8,128)(2,1)S(1)}) custom-call(bf16[1,2,6,24,512]{4,3,2,1,0:T(8,128)(2,1)} %own_x_ref.1, bf16[1,2,6,24,512]{4,3,2,1,0:T(8,128)(2,1)} %own_u_ref.1), custom_call_target="tpu_custom_call" | custom-call | flops 1000 | bytes 737280 | tf_op jit(solution)/shard_map/cut_halos/pallas_call | solution.py:302
  1.9 1.4 %collective-permute-start.1 = (bf16[2,2,3,6,512]{4,3,2,1,0:T(8,128)(2,1)S(1)}, bf16[2,2,3,6,512]{4,3,2,1,0:T(8,128)(2,1)S(1)}, u32[]{:S(2)}, u32[]{:S(2)}) collective-permute-start(bf16[2,2,3,6,512]{4,3,2,1,0:T(8,128)(2,1)S(1)} %get-tuple-element.26), channel_id=1, source_target_pairs={{0,9},{1,10},{2,11},{3,12},{4,13},{5,14},{6,15},{7,8},{8,17},{9,18... | collective-permute-start | bytes 221192 | tf_op jit(solution)/shard_map/ppermute | solution.py:364
  3.3 1.9 %collective-permute-start.2 = (bf16[2,2,3,6,512]{4,3,2,1,0:T(8,128)(2,1)S(1)}, bf16[2,2,3,6,512]{4,3,2,1,0:T(8,128)(2,1)S(1)}, u32[]{:S(2)}, u32[]{:S(2)}) collective-permute-start(bf16[2,2,3,6,512]{4,3,2,1,0:T(8,128)(2,1)S(1)} %get-tuple-element.27), channel_id=1, source_target_pairs={{0,1},{1,2},{2,3},{3,4},{4,5},{5,6},{6,7},{7,0},{8,9},{9,10},{10,1... | collective-permute-start | bytes 221192 | tf_op jit(solution)/shard_map/ppermute | solution.py:354
  5.3 1.3 %collective-permute-start = (bf16[2,2,3,18,512]{4,3,2,1,0:T(8,128)(2,1)S(1)}, bf16[2,2,3,18,512]{4,3,2,1,0:T(8,128)(2,1)S(1)}, u32[]{:S(2)}, u32[]{:S(2)}) collective-permute-start(bf16[2,2,3,18,512]{4,3,2,1,0:T(8,128)(2,1)S(1)} %get-tuple-element.25), channel_id=1, source_target_pairs={{0,8},{8,16},{16,24},{24,32},{32,40},{40,48},{48,56},{56,64},{64,7... | collective-permute-start | bytes 663560 | tf_op jit(solution)/shard_map/ppermute | solution.py:354
  6.6 0.8 %broadcast_add_fusion = s32[6,24]{1,0:T(8,128)S(1)} fusion(s32[6,24]{1,0:T(8,128)} %param.7, s32[6]{0:T(128)S(1)} %and_select_fusion), kind=kLoop, calls=%fused_computation.2 | loop fusion | flops 144 | bytes 1176 | tf_op jit(solution)/shard_map/add | solution.py:381
  7.3 0.1 reshape.41
  7.4 0.1 tile.21
  7.5 0.1 tile.23
  7.6 0.1 tile.27.lcol_ref
  7.8 0.1 tile.25
  7.9 1.4 %copy-done = bf16[512,1536]{1,0:T(8,128)(2,1)S(1)} copy-done((bf16[512,1536]{1,0:T(8,128)(2,1)S(1)}, bf16[512,1536]{1,0:T(8,128)(2,1)}, u32[]{:S(2)}) %copy-start) | copy-done | bytes 1572888
  9.3 1.0 %copy-done.2 = bf16[512,512]{1,0:T(8,128)(2,1)S(1)} copy-done((bf16[512,512]{1,0:T(8,128)(2,1)S(1)}, bf16[512,512]{1,0:T(8,128)(2,1)}, u32[]{:S(2)}) %copy-start.2) | copy-done | bytes 524312
  10.3 0.2 stage_weights.1
  10.5 0.8 %collective-permute-done.1.corner_ref = bf16[2,2,3,6,512]{4,3,2,1,0:T(8,128)(2,1)S(1)} collective-permute-done((bf16[2,2,3,6,512]{4,3,2,1,0:T(8,128)(2,1)S(1)}, bf16[2,2,3,6,512]{4,3,2,1,0:T(8,128)(2,1)S(1)}, u32[]{:S(2)}, u32[]{:S(2)}) %collective-permute-start.1) | collective-permute-done | bytes 73760 | tf_op jit(solution)/shard_map/ppermute | solution.py:364
  11.3 0.0 collective-permute-done.2.left_ref
  11.3 3.8 %collective-permute-done.upper_ref = bf16[2,2,3,18,512]{4,3,2,1,0:T(8,128)(2,1)S(1)} collective-permute-done((bf16[2,2,3,18,512]{4,3,2,1,0:T(8,128)(2,1)S(1)}, bf16[2,2,3,18,512]{4,3,2,1,0:T(8,128)(2,1)S(1)}, u32[]{:S(2)}, u32[]{:S(2)}) %collective-permute-start) | collective-permute-done | bytes 221216 | tf_op jit(solution)/shard_map/ppermute | solution.py:354
  15.0 5.1 %window_attention.1 = (bf16[32,2,64,128]{3,2,1,0:T(8,128)(2,1)S(1)}, bf16[288,1536]{1,0:T(8,128)(2,1)S(1)}, bf16[288,512]{1,0:T(8,128)(2,1)S(1)}, bf16[256,288]{...) custom-call(bf16[1,2,6,24,512]{4,3,2,1,0:T(8,128)(2,1)S(1)} %copy-do, ...), custom_call_target="tpu_custom_call" | custom-call | flops 5000000000 | bytes 6225920 | tf_op jit(solution)/shard_map/window_attention/pallas_call | solution.py:302
  20.1 0.1 collective-permute-start.3
  20.3 2.1 %own_half_and_outputs.1 = (f32[32,2,64,128]{3,2,1,0:T(8,128)S(1)}, bf16[2,2,6,18,512]{4,3,2,1,0:T(8,128)(2,1)S(1)}, bf16[2,2,6,6,512]{4,3,2,1,0:T(8,128)(2,1)S(1)}) custom-call(bf16[256,288]{1,0:T(8,128)(2,1)S(1)} %get-tuple-element.30.n_ref, bf16[256,288]{1,0:T(8,128)(2,1)S(1)} %get-tuple-element.31.m_ref, bf16[288,1536]{1,0:T(8,128)(2,1)S(1)} %get-tuple-element.32.gp_ref, ...), custom_call_target="tpu_custom_call" | custom-call | flops 600000000 | bytes 3276800 | tf_op jit(solution)/shard_map/own_half_and_outputs/pallas_call | solution.py:302
  22.4 0.5 collective-permute-done.3
  22.9 1.2 %add_halves.1 = bf16[4,2,8,64,128]{4,3,2,1,0:T(8,128)(2,1)} custom-call(f32[2,4,8,64,128]{4,3,2,1,0:T(8,128)S(1)} %bitcast.7, bf16[2,4,8,64,128]{4,3,2,1,0:T(8,128)(2,1)S(1)} %bitcast.8), custom_call_target="tpu_custom_call" | custom-call | flops 1000000 | bytes 2097152 | tf_op jit(solution)/shard_map/add_halves/pallas_call | solution.py:302
  24.0 4.5 %all-to-all-start = ((bf16[8,512,128]{2,1,0:T(8,128)(2,1)}), bf16[8,512,128]{2,1,0:T(8,128)(2,1)S(1)}, u32[]{:S(2)}, u32[]{:S(2)}) async-start(bf16[8,512,128]{2,1,0:T(8,128)(2,1)} %bitcast.3), calls=%async_computation | async-start | bytes 2097152 | tf_op jit(solution)/shard_map/all_to_all | solution.py:404
  28.5 0.4 collective-permute-start.4
  28.9 7.7 %collective-permute-done.4.right_ref = bf16[2,2,6,6,512]{4,3,2,1,0:T(8,128)(2,1)S(1)} collective-permute-done((bf16[2,2,6,6,512]{4,3,2,1,0:T(8,128)(2,1)S(1)}, bf16[2,2,6,6,512]{4,3,2,1,0:T(8,128)(2,1)S(1)}, u32[]{:S(2)}, u32[]{:S(2)}) %collective-permute-start.4) | collective-permute-done | bytes 147488 | tf_op jit(solution)/shard_map/ppermute | solution.py:354
  36.6 8.4 %all-to-all-done.parts_ref = bf16[8,512,128]{2,1,0:T(8,128)(2,1)S(1)} async-done(((bf16[8,512,128]{2,1,0:T(8,128)(2,1)}), bf16[8,512,128]{2,1,0:T(8,128)(2,1)S(1)}, u32[]{:S(2)}, u32[]{:S(2)}) %all-to-all-start) | async-done | bytes 1048608 | tf_op jit(solution)/shard_map/all_to_all | solution.py:404
  45.0 0.8 %sum_parts.1 = bf16[2,512,128]{2,1,0:T(8,128)(2,1)} custom-call(bf16[8,512,128]{2,1,0:T(8,128)(2,1)S(1)} %all-to-all-done.parts_ref), custom_call_target="tpu_custom_call" | custom-call | flops 1000000 | bytes 524288 | tf_op jit(solution)/shard_map/sum_parts/pallas_call | solution.py:302
  45.8 8.4 %all-to-all-start.1 = ((bf16[16,64,128]{2,1,0:T(8,128)(2,1)}), bf16[16,64,128]{2,1,0:T(8,128)(2,1)S(1)}, u32[]{:S(2)}, u32[]{:S(2)}) async-start(bf16[16,64,128]{2,1,0:T(8,128)(2,1)} %bitcast.4), calls=%async_computation.1 | async-start | bytes 524288 | tf_op jit(solution)/shard_map/all_to_all | solution.py:407
  54.3 1.1 %collective-permute-start.5 = (bf16[2,2,3,24,512]{4,3,2,1,0:T(8,128)(2,1)S(1)}, bf16[2,2,3,24,512]{4,3,2,1,0:T(8,128)(2,1)S(1)}, u32[]{:S(2)}, u32[]{:S(2)}) collective-permute-start(bf16[2,2,3,24,512]{4,3,2,1,0:T(8,128)(2,1)S(1)} %halo_rows.1), channel_id=1, source_target_pairs={{0,120},{8,0},{16,8},{24,16},{32,24},{40,32},{48,40},{56,48},{64,5... | collective-permute-start | bytes 884744 | tf_op jit(solution)/shard_map/ppermute | solution.py:354
  55.5 4.4 %collective-permute-done.5.lower_ref = bf16[2,2,3,24,512]{4,3,2,1,0:T(8,128)(2,1)S(1)} collective-permute-done((bf16[2,2,3,24,512]{4,3,2,1,0:T(8,128)(2,1)S(1)}, bf16[2,2,3,24,512]{4,3,2,1,0:T(8,128)(2,1)S(1)}, u32[]{:S(2)}, u32[]{:S(2)}) %collective-permute-start.5) | collective-permute-done | bytes 294944 | tf_op jit(solution)/shard_map/ppermute | solution.py:354
  59.8 0.9 %join_outputs.1 = (bf16[1,2,6,24,512]{4,3,2,1,0:T(8,128)(2,1)}, bf16[1,2,6,24,512]{4,3,2,1,0:T(8,128)(2,1)}) custom-call(bf16[2,2,6,18,512]{4,3,2,1,0:T(8,128)(2,1)S(1)} %get-tuple-element.36.own_ref, bf16[2,2,6,6,512]{4,3,2,1,0:T(8,128)(2,1)S(1)} %collective-permute-done.4.right_ref, bf16[2,2,3,24,512]{4,3,2,1,0:T(8,128)(2,1)S(1)} %collective-permute-done.5.lower_ref), custom_call_target="tpu_custom_call" | custom-call | flops 1000 | bytes 1179648 | tf_op jit(solution)/shard_map/join_outputs/pallas_call | solution.py:302
  60.7 3.3 %all-to-all-done.1.parts_ref = bf16[16,64,128]{2,1,0:T(8,128)(2,1)S(1)} async-done(((bf16[16,64,128]{2,1,0:T(8,128)(2,1)}), bf16[16,64,128]{2,1,0:T(8,128)(2,1)S(1)}, u32[]{:S(2)}, u32[]{:S(2)}) %all-to-all-start.1) | async-done | bytes 262176 | tf_op jit(solution)/shard_map/all_to_all | solution.py:407
  64.0 0.6 %last_sum.1 = (f32[4,1536]{1,0:T(4,128)}, f32[4,512]{1,0:T(4,128)}) custom-call(bf16[16,64,128]{2,1,0:T(8,128)(2,1)S(1)} %all-to-all-done.1.parts_ref), custom_call_target="tpu_custom_call" | custom-call | flops 1000 | bytes 32768 | tf_op jit(solution)/shard_map/last_sum/pallas_call | solution.py:302
  (18 shorter events, 0.1 us)
Async XLA Ops:
  0.6 14.4 %copy-start.5 = (bf16[1,2,6,24,512]{4,3,2,1,0:T(8,128)(2,1)S(1)}, bf16[1,2,6,24,512]{4,3,2,1,0:T(8,128)(2,1)}, u32[]{:S(2)}) copy-start(bf16[1,2,6,24,512]{4,3,2,1,0:T(8,128)(2,1)} %own_u_ref.1) | copy-start | bytes 884740
  0.6 14.4 %copy-start.4 = (bf16[1,2,6,24,512]{4,3,2,1,0:T(8,128)(2,1)S(1)}, bf16[1,2,6,24,512]{4,3,2,1,0:T(8,128)(2,1)}, u32[]{:S(2)}) copy-start(bf16[1,2,6,24,512]{4,3,2,1,0:T(8,128)(2,1)} %own_x_ref.1) | copy-start | bytes 884740
  1.9 9.4 %collective-permute-start.1 = (bf16[2,2,3,6,512]{4,3,2,1,0:T(8,128)(2,1)S(1)}, bf16[2,2,3,6,512]{4,3,2,1,0:T(8,128)(2,1)S(1)}, u32[]{:S(2)}, u32[]{:S(2)}) collective-permute-start(bf16[2,2,3,6,512]{4,3,2,1,0:T(8,128)(2,1)S(1)} %get-tuple-element.26), channel_id=1, source_target_pairs={{0,9},{1,10},{2,11},{3,12},{4,13},{5,14},{6,15},{7,8},{8,17},{9,18... | collective-permute-start | bytes 221192 | tf_op jit(solution)/shard_map/ppermute | solution.py:364
  3.3 7.9 %collective-permute-start.2 = (bf16[2,2,3,6,512]{4,3,2,1,0:T(8,128)(2,1)S(1)}, bf16[2,2,3,6,512]{4,3,2,1,0:T(8,128)(2,1)S(1)}, u32[]{:S(2)}, u32[]{:S(2)}) collective-permute-start(bf16[2,2,3,6,512]{4,3,2,1,0:T(8,128)(2,1)S(1)} %get-tuple-element.27), channel_id=1, source_target_pairs={{0,1},{1,2},{2,3},{3,4},{4,5},{5,6},{6,7},{7,0},{8,9},{9,10},{10,1... | collective-permute-start | bytes 221192 | tf_op jit(solution)/shard_map/ppermute | solution.py:354
  5.3 9.8 %collective-permute-start = (bf16[2,2,3,18,512]{4,3,2,1,0:T(8,128)(2,1)S(1)}, bf16[2,2,3,18,512]{4,3,2,1,0:T(8,128)(2,1)S(1)}, u32[]{:S(2)}, u32[]{:S(2)}) collective-permute-start(bf16[2,2,3,18,512]{4,3,2,1,0:T(8,128)(2,1)S(1)} %get-tuple-element.25), channel_id=1, source_target_pairs={{0,8},{8,16},{16,24},{24,32},{32,40},{40,48},{48,56},{56,64},{64,7... | collective-permute-start | bytes 663560 | tf_op jit(solution)/shard_map/ppermute | solution.py:354
  7.9 1.4 %copy-start = (bf16[512,1536]{1,0:T(8,128)(2,1)S(1)}, bf16[512,1536]{1,0:T(8,128)(2,1)}, u32[]{:S(2)}) copy-start(bf16[512,1536]{1,0:T(8,128)(2,1)} %qkv_ref.3) | copy-start | bytes 4718596
  9.3 1.0 %copy-start.2 = (bf16[512,512]{1,0:T(8,128)(2,1)S(1)}, bf16[512,512]{1,0:T(8,128)(2,1)}, u32[]{:S(2)}) copy-start(bf16[512,512]{1,0:T(8,128)(2,1)} %proj_ref.3) | copy-start | bytes 1572868
  15.0 5.2 %copy-start.1 = (bf16[512,1536]{1,0:T(8,128)(2,1)S(1)}, bf16[512,1536]{1,0:T(8,128)(2,1)}, u32[]{:S(2)}) copy-start(bf16[512,1536]{1,0:T(8,128)(2,1)} %qkv_ref.3) | copy-start | bytes 4718596
  15.0 5.2 %copy-start.3 = (bf16[512,512]{1,0:T(8,128)(2,1)S(1)}, bf16[512,512]{1,0:T(8,128)(2,1)}, u32[]{:S(2)}) copy-start(bf16[512,512]{1,0:T(8,128)(2,1)} %proj_ref.3) | copy-start | bytes 1572868
  20.1 2.7 %collective-permute-start.3 = (bf16[32,2,64,128]{3,2,1,0:T(8,128)(2,1)S(1)}, bf16[32,2,64,128]{3,2,1,0:T(8,128)(2,1)S(1)}, u32[]{:S(2)}, u32[]{:S(2)}) collective-permute-start(bf16[32,2,64,128]{3,2,1,0:T(8,128)(2,1)S(1)} %get-tuple-element.38), channel_id=1, source_target_pairs={{0,8},{8,0},{1,9},{9,1},{2,10},{10,2},{3,11},{11,3},{4,12},{12,4},... | collective-permute-start | bytes 3145736 | tf_op jit(solution)/shard_map/ppermute | solution.py:354
  24.0 21.0 %all-to-all-start = ((bf16[8,512,128]{2,1,0:T(8,128)(2,1)}), bf16[8,512,128]{2,1,0:T(8,128)(2,1)S(1)}, u32[]{:S(2)}, u32[]{:S(2)}) async-start(bf16[8,512,128]{2,1,0:T(8,128)(2,1)} %bitcast.3), calls=%async_computation | async-start | bytes 2097152 | tf_op jit(solution)/shard_map/all_to_all | solution.py:404
  28.5 8.1 %collective-permute-start.4 = (bf16[2,2,6,6,512]{4,3,2,1,0:T(8,128)(2,1)S(1)}, bf16[2,2,6,6,512]{4,3,2,1,0:T(8,128)(2,1)S(1)}, u32[]{:S(2)}, u32[]{:S(2)}) collective-permute-start(bf16[2,2,6,6,512]{4,3,2,1,0:T(8,128)(2,1)S(1)} %get-tuple-element.39), channel_id=1, source_target_pairs={{0,7},{1,0},{2,1},{3,2},{4,3},{5,4},{6,5},{7,6},{8,15},{9,8},{10,9... | collective-permute-start | bytes 442376 | tf_op jit(solution)/shard_map/ppermute | solution.py:354
  45.8 18.1 %all-to-all-start.1 = ((bf16[16,64,128]{2,1,0:T(8,128)(2,1)}), bf16[16,64,128]{2,1,0:T(8,128)(2,1)S(1)}, u32[]{:S(2)}, u32[]{:S(2)}) async-start(bf16[16,64,128]{2,1,0:T(8,128)(2,1)} %bitcast.4), calls=%async_computation.1 | async-start | bytes 524288 | tf_op jit(solution)/shard_map/all_to_all | solution.py:407
  54.3 5.5 %collective-permute-start.5 = (bf16[2,2,3,24,512]{4,3,2,1,0:T(8,128)(2,1)S(1)}, bf16[2,2,3,24,512]{4,3,2,1,0:T(8,128)(2,1)S(1)}, u32[]{:S(2)}, u32[]{:S(2)}) collective-permute-start(bf16[2,2,3,24,512]{4,3,2,1,0:T(8,128)(2,1)S(1)} %halo_rows.1), channel_id=1, source_target_pairs={{0,120},{8,0},{16,8},{24,16},{32,24},{40,32},{48,40},{56,48},{64,5... | collective-permute-start | bytes 884744 | tf_op jit(solution)/shard_map/ppermute | solution.py:354

commit v12 on v11

--- a/solution.py
+++ b/solution.py
@@ -42,10 +42,9 @@
             copies.append(pltpu.make_async_copy(ref.at[0, level], held_ref.at[at, level], sems.at[at, level]))
     for copy in copies:
         copy.start()
-    for copy in copies:
-        copy.wait()
     for at in range(2):
         for level in range(LEV):
+            copies[at * LEV + level].wait()
             for row in range(WLAT):
                 tokens = held_ref[at, level, row].astype(jnp.float32)
                 side = tokens[-SLON:].astype(jnp.bfloat16)

time: 65 us -> 64.9 us (level)
  no operation moved by 1% of the time
where the time goes in v12:
time: 64.9 us; the launch traced here: 64.6 us
  waiting for transfers between devices  28.8 us (44%)
  starting transfers between devices  19.2 us (30%)
  Pallas kernels  12.1 us (19%)
  local copies, waits for them, and re-layouts  2.95 us (5%)
  other arithmetic  0.76 us (1%)
  between operations  0.75 us (1%)
    ppermute x5, waiting for transfers between devices, passed_along(): return lax.ppermute(value, axis, pairs)  16.3 us
    pallas_call x8, Pallas kernels, call(): pl.pallas_call(kernel, out_shape=tuple((make(shape, dtype) for shape, dty...  12 us
    all_to_all x1, waiting for transfers between devices, per_device(): lax.all_to_all(sums.reshape(8, 512, 128), ('x', 'yh'), 0, 0, tiled=True)  8.45 us
    all_to_all x1, starting transfers between devices, per_device(): lax.all_to_all(sums.reshape(16, 64, 128), ('dp', 'lon'), 0, 0, tiled=True)  8.4 us
    ppermute x5, starting transfers between devices, passed_along(): return lax.ppermute(value, axis, pairs)  4.84 us
    all_to_all x1, starting transfers between devices, per_device(): lax.all_to_all(sums.reshape(8, 512, 128), ('x', 'yh'), 0, 0, tiled=True)  4.47 us
    all_to_all x1, waiting for transfers between devices, per_device(): lax.all_to_all(sums.reshape(16, 64, 128), ('dp', 'lon'), 0, 0, tiled=True)  3.27 us
    unnamed x12, local copies, waits for them, and re-layouts  2.47 us
  transfers between devices with their start and end apart: 8, of which 7 were waited for; matrix products, arithmetic and copies ran while one was open for 2% of the time, Pallas kernels for 5%

profile of v12, /device:TPU:32, one launch (start us, length us, event | category | flops | bytes accessed | tf_op | source)
XLA Modules:
  0.0 64.6 jit_solution(10731497261489801933)
XLA Ops:
  0.7 1.2 %cut_halos.1 = (bf16[2,2,3,18,512]{4,3,2,1,0:T(8,128)(2,1)S(1)}, bf16[2,2,3,6,512]{4,3,2,1,0:T(8,128)(2,1)S(1)}, bf16[2,2,3,6,512]{4,3,2,1,0:T(8,128)(2,1)S(1)}) custom-call(bf16[1,2,6,24,512]{4,3,2,1,0:T(8,128)(2,1)} %own_x_ref.1, bf16[1,2,6,24,512]{4,3,2,1,0:T(8,128)(2,1)} %own_u_ref.1), custom_call_target="tpu_custom_call" | custom-call | flops 1000 | bytes 737280 | tf_op jit(solution)/shard_map/cut_halos/pallas_call | solution.py:301
  1.9 1.4 %collective-permute-start.1 = (bf16[2,2,3,6,512]{4,3,2,1,0:T(8,128)(2,1)S(1)}, bf16[2,2,3,6,512]{4,3,2,1,0:T(8,128)(2,1)S(1)}, u32[]{:S(2)}, u32[]{:S(2)}) collective-permute-start(bf16[2,2,3,6,512]{4,3,2,1,0:T(8,128)(2,1)S(1)} %get-tuple-element.26), channel_id=1, source_target_pairs={{0,9},{1,10},{2,11},{3,12},{4,13},{5,14},{6,15},{7,8},{8,17},{9,18... | collective-permute-start | bytes 221192 | tf_op jit(solution)/shard_map/ppermute | solution.py:363
  3.3 1.9 %collective-permute-start.2 = (bf16[2,2,3,6,512]{4,3,2,1,0:T(8,128)(2,1)S(1)}, bf16[2,2,3,6,512]{4,3,2,1,0:T(8,128)(2,1)S(1)}, u32[]{:S(2)}, u32[]{:S(2)}) collective-permute-start(bf16[2,2,3,6,512]{4,3,2,1,0:T(8,128)(2,1)S(1)} %get-tuple-element.27), channel_id=1, source_target_pairs={{0,1},{1,2},{2,3},{3,4},{4,5},{5,6},{6,7},{7,0},{8,9},{9,10},{10,1... | collective-permute-start | bytes 221192 | tf_op jit(solution)/shard_map/ppermute | solution.py:353
  5.2 1.3 %collective-permute-start = (bf16[2,2,3,18,512]{4,3,2,1,0:T(8,128)(2,1)S(1)}, bf16[2,2,3,18,512]{4,3,2,1,0:T(8,128)(2,1)S(1)}, u32[]{:S(2)}, u32[]{:S(2)}) collective-permute-start(bf16[2,2,3,18,512]{4,3,2,1,0:T(8,128)(2,1)S(1)} %get-tuple-element.25), channel_id=1, source_target_pairs={{0,8},{8,16},{16,24},{24,32},{32,40},{40,48},{48,56},{56,64},{64,7... | collective-permute-start | bytes 663560 | tf_op jit(solution)/shard_map/ppermute | solution.py:353
  6.6 0.8 %broadcast_add_fusion = s32[6,24]{1,0:T(8,128)S(1)} fusion(s32[6,24]{1,0:T(8,128)} %param.7, s32[6]{0:T(128)S(1)} %and_select_fusion), kind=kLoop, calls=%fused_computation.2 | loop fusion | flops 144 | bytes 1176 | tf_op jit(solution)/shard_map/add | solution.py:380
  7.3 0.1 reshape.41
  7.4 0.1 tile.21
  7.5 0.1 tile.23
  7.6 0.1 tile.27.lcol_ref
  7.7 0.1 tile.25
  7.8 1.4 %copy-done = bf16[512,1536]{1,0:T(8,128)(2,1)S(1)} copy-done((bf16[512,1536]{1,0:T(8,128)(2,1)S(1)}, bf16[512,1536]{1,0:T(8,128)(2,1)}, u32[]{:S(2)}) %copy-start) | copy-done | bytes 1572888
  9.2 1.0 %copy-done.2 = bf16[512,512]{1,0:T(8,128)(2,1)S(1)} copy-done((bf16[512,512]{1,0:T(8,128)(2,1)S(1)}, bf16[512,512]{1,0:T(8,128)(2,1)}, u32[]{:S(2)}) %copy-start.2) | copy-done | bytes 524312
  10.3 0.2 stage_weights.1
  10.5 0.8 %collective-permute-done.1.corner_ref = bf16[2,2,3,6,512]{4,3,2,1,0:T(8,128)(2,1)S(1)} collective-permute-done((bf16[2,2,3,6,512]{4,3,2,1,0:T(8,128)(2,1)S(1)}, bf16[2,2,3,6,512]{4,3,2,1,0:T(8,128)(2,1)S(1)}, u32[]{:S(2)}, u32[]{:S(2)}) %collective-permute-start.1) | collective-permute-done | bytes 73760 | tf_op jit(solution)/shard_map/ppermute | solution.py:363
  11.2 0.0 collective-permute-done.2.left_ref
  11.2 3.8 %collective-permute-done.upper_ref = bf16[2,2,3,18,512]{4,3,2,1,0:T(8,128)(2,1)S(1)} collective-permute-done((bf16[2,2,3,18,512]{4,3,2,1,0:T(8,128)(2,1)S(1)}, bf16[2,2,3,18,512]{4,3,2,1,0:T(8,128)(2,1)S(1)}, u32[]{:S(2)}, u32[]{:S(2)}) %collective-permute-start) | collective-permute-done | bytes 221216 | tf_op jit(solution)/shard_map/ppermute | solution.py:353
  15.0 5.1 %window_attention.1 = (bf16[32,2,64,128]{3,2,1,0:T(8,128)(2,1)S(1)}, bf16[288,1536]{1,0:T(8,128)(2,1)S(1)}, bf16[288,512]{1,0:T(8,128)(2,1)S(1)}, bf16[256,288]{...) custom-call(bf16[1,2,6,24,512]{4,3,2,1,0:T(8,128)(2,1)S(1)} %copy-do, ...), custom_call_target="tpu_custom_call" | custom-call | flops 5000000000 | bytes 6225920 | tf_op jit(solution)/shard_map/window_attention/pallas_call | solution.py:301
  20.1 0.1 collective-permute-start.3
  20.2 2.1 %own_half_and_outputs.1 = (f32[32,2,64,128]{3,2,1,0:T(8,128)S(1)}, bf16[2,2,6,18,512]{4,3,2,1,0:T(8,128)(2,1)S(1)}, bf16[2,2,6,6,512]{4,3,2,1,0:T(8,128)(2,1)S(1)}) custom-call(bf16[256,288]{1,0:T(8,128)(2,1)S(1)} %get-tuple-element.30.n_ref, bf16[256,288]{1,0:T(8,128)(2,1)S(1)} %get-tuple-element.31.m_ref, bf16[288,1536]{1,0:T(8,128)(2,1)S(1)} %get-tuple-element.32.gp_ref, ...), custom_call_target="tpu_custom_call" | custom-call | flops 600000000 | bytes 3276800 | tf_op jit(solution)/shard_map/own_half_and_outputs/pallas_call | solution.py:301
  22.4 0.5 collective-permute-done.3
  22.9 1.2 %add_halves.1 = bf16[4,2,8,64,128]{4,3,2,1,0:T(8,128)(2,1)} custom-call(f32[2,4,8,64,128]{4,3,2,1,0:T(8,128)S(1)} %bitcast.7, bf16[2,4,8,64,128]{4,3,2,1,0:T(8,128)(2,1)S(1)} %bitcast.8), custom_call_target="tpu_custom_call" | custom-call | flops 1000000 | bytes 2097152 | tf_op jit(solution)/shard_map/add_halves/pallas_call | solution.py:301
  24.0 4.5 %all-to-all-start = ((bf16[8,512,128]{2,1,0:T(8,128)(2,1)}), bf16[8,512,128]{2,1,0:T(8,128)(2,1)S(1)}, u32[]{:S(2)}, u32[]{:S(2)}) async-start(bf16[8,512,128]{2,1,0:T(8,128)(2,1)} %bitcast.3), calls=%async_computation | async-start | bytes 2097152 | tf_op jit(solution)/shard_map/all_to_all | solution.py:403
  28.5 0.4 collective-permute-start.4
  28.8 7.7 %collective-permute-done.4.right_ref = bf16[2,2,6,6,512]{4,3,2,1,0:T(8,128)(2,1)S(1)} collective-permute-done((bf16[2,2,6,6,512]{4,3,2,1,0:T(8,128)(2,1)S(1)}, bf16[2,2,6,6,512]{4,3,2,1,0:T(8,128)(2,1)S(1)}, u32[]{:S(2)}, u32[]{:S(2)}) %collective-permute-start.4) | collective-permute-done | bytes 147488 | tf_op jit(solution)/shard_map/ppermute | solution.py:353
  36.5 8.5 %all-to-all-done.parts_ref = bf16[8,512,128]{2,1,0:T(8,128)(2,1)S(1)} async-done(((bf16[8,512,128]{2,1,0:T(8,128)(2,1)}), bf16[8,512,128]{2,1,0:T(8,128)(2,1)S(1)}, u32[]{:S(2)}, u32[]{:S(2)}) %all-to-all-start) | async-done | bytes 1048608 | tf_op jit(solution)/shard_map/all_to_all | solution.py:403
  45.0 0.8 %sum_parts.1 = bf16[2,512,128]{2,1,0:T(8,128)(2,1)} custom-call(bf16[8,512,128]{2,1,0:T(8,128)(2,1)S(1)} %all-to-all-done.parts_ref), custom_call_target="tpu_custom_call" | custom-call | flops 1000000 | bytes 524288 | tf_op jit(solution)/shard_map/sum_parts/pallas_call | solution.py:301
  45.8 8.4 %all-to-all-start.1 = ((bf16[16,64,128]{2,1,0:T(8,128)(2,1)}), bf16[16,64,128]{2,1,0:T(8,128)(2,1)S(1)}, u32[]{:S(2)}, u32[]{:S(2)}) async-start(bf16[16,64,128]{2,1,0:T(8,128)(2,1)} %bitcast.4), calls=%async_computation.1 | async-start | bytes 524288 | tf_op jit(solution)/shard_map/all_to_all | solution.py:406
  54.3 1.2 %collective-permute-start.5 = (bf16[2,2,3,24,512]{4,3,2,1,0:T(8,128)(2,1)S(1)}, bf16[2,2,3,24,512]{4,3,2,1,0:T(8,128)(2,1)S(1)}, u32[]{:S(2)}, u32[]{:S(2)}) collective-permute-start(bf16[2,2,3,24,512]{4,3,2,1,0:T(8,128)(2,1)S(1)} %halo_rows.1), channel_id=1, source_target_pairs={{0,120},{8,0},{16,8},{24,16},{32,24},{40,32},{48,40},{56,48},{64,5... | collective-permute-start | bytes 884744 | tf_op jit(solution)/shard_map/ppermute | solution.py:353
  55.4 4.4 %collective-permute-done.5.lower_ref = bf16[2,2,3,24,512]{4,3,2,1,0:T(8,128)(2,1)S(1)} collective-permute-done((bf16[2,2,3,24,512]{4,3,2,1,0:T(8,128)(2,1)S(1)}, bf16[2,2,3,24,512]{4,3,2,1,0:T(8,128)(2,1)S(1)}, u32[]{:S(2)}, u32[]{:S(2)}) %collective-permute-start.5) | collective-permute-done | bytes 294944 | tf_op jit(solution)/shard_map/ppermute | solution.py:353
  59.8 0.9 %join_outputs.1 = (bf16[1,2,6,24,512]{4,3,2,1,0:T(8,128)(2,1)}, bf16[1,2,6,24,512]{4,3,2,1,0:T(8,128)(2,1)}) custom-call(bf16[2,2,6,18,512]{4,3,2,1,0:T(8,128)(2,1)S(1)} %get-tuple-element.36.own_ref, bf16[2,2,6,6,512]{4,3,2,1,0:T(8,128)(2,1)S(1)} %collective-permute-done.4.right_ref, bf16[2,2,3,24,512]{4,3,2,1,0:T(8,128)(2,1)S(1)} %collective-permute-done.5.lower_ref), custom_call_target="tpu_custom_call" | custom-call | flops 1000 | bytes 1179648 | tf_op jit(solution)/shard_map/join_outputs/pallas_call | solution.py:301
  60.6 3.3 %all-to-all-done.1.parts_ref = bf16[16,64,128]{2,1,0:T(8,128)(2,1)S(1)} async-done(((bf16[16,64,128]{2,1,0:T(8,128)(2,1)}), bf16[16,64,128]{2,1,0:T(8,128)(2,1)S(1)}, u32[]{:S(2)}, u32[]{:S(2)}) %all-to-all-start.1) | async-done | bytes 262176 | tf_op jit(solution)/shard_map/all_to_all | solution.py:406
  63.9 0.6 %last_sum.1 = (f32[4,1536]{1,0:T(4,128)}, f32[4,512]{1,0:T(4,128)}) custom-call(bf16[16,64,128]{2,1,0:T(8,128)(2,1)S(1)} %all-to-all-done.1.parts_ref), custom_call_target="tpu_custom_call" | custom-call | flops 1000 | bytes 32768 | tf_op jit(solution)/shard_map/last_sum/pallas_call | solution.py:301
  (18 shorter events, 0.1 us)
Async XLA Ops:
  0.6 14.4 %copy-start.5 = (bf16[1,2,6,24,512]{4,3,2,1,0:T(8,128)(2,1)S(1)}, bf16[1,2,6,24,512]{4,3,2,1,0:T(8,128)(2,1)}, u32[]{:S(2)}) copy-start(bf16[1,2,6,24,512]{4,3,2,1,0:T(8,128)(2,1)} %own_u_ref.1) | copy-start | bytes 884740
  0.6 14.4 %copy-start.4 = (bf16[1,2,6,24,512]{4,3,2,1,0:T(8,128)(2,1)S(1)}, bf16[1,2,6,24,512]{4,3,2,1,0:T(8,128)(2,1)}, u32[]{:S(2)}) copy-start(bf16[1,2,6,24,512]{4,3,2,1,0:T(8,128)(2,1)} %own_x_ref.1) | copy-start | bytes 884740
  1.9 9.4 %collective-permute-start.1 = (bf16[2,2,3,6,512]{4,3,2,1,0:T(8,128)(2,1)S(1)}, bf16[2,2,3,6,512]{4,3,2,1,0:T(8,128)(2,1)S(1)}, u32[]{:S(2)}, u32[]{:S(2)}) collective-permute-start(bf16[2,2,3,6,512]{4,3,2,1,0:T(8,128)(2,1)S(1)} %get-tuple-element.26), channel_id=1, source_target_pairs={{0,9},{1,10},{2,11},{3,12},{4,13},{5,14},{6,15},{7,8},{8,17},{9,18... | collective-permute-start | bytes 221192 | tf_op jit(solution)/shard_map/ppermute | solution.py:363
  3.3 7.9 %collective-permute-start.2 = (bf16[2,2,3,6,512]{4,3,2,1,0:T(8,128)(2,1)S(1)}, bf16[2,2,3,6,512]{4,3,2,1,0:T(8,128)(2,1)S(1)}, u32[]{:S(2)}, u32[]{:S(2)}) collective-permute-start(bf16[2,2,3,6,512]{4,3,2,1,0:T(8,128)(2,1)S(1)} %get-tuple-element.27), channel_id=1, source_target_pairs={{0,1},{1,2},{2,3},{3,4},{4,5},{5,6},{6,7},{7,0},{8,9},{9,10},{10,1... | collective-permute-start | bytes 221192 | tf_op jit(solution)/shard_map/ppermute | solution.py:353
  5.2 9.8 %collective-permute-start = (bf16[2,2,3,18,512]{4,3,2,1,0:T(8,128)(2,1)S(1)}, bf16[2,2,3,18,512]{4,3,2,1,0:T(8,128)(2,1)S(1)}, u32[]{:S(2)}, u32[]{:S(2)}) collective-permute-start(bf16[2,2,3,18,512]{4,3,2,1,0:T(8,128)(2,1)S(1)} %get-tuple-element.25), channel_id=1, source_target_pairs={{0,8},{8,16},{16,24},{24,32},{32,40},{40,48},{48,56},{56,64},{64,7... | collective-permute-start | bytes 663560 | tf_op jit(solution)/shard_map/ppermute | solution.py:353
  7.8 1.4 %copy-start = (bf16[512,1536]{1,0:T(8,128)(2,1)S(1)}, bf16[512,1536]{1,0:T(8,128)(2,1)}, u32[]{:S(2)}) copy-start(bf16[512,1536]{1,0:T(8,128)(2,1)} %qkv_ref.3) | copy-start | bytes 4718596
  9.2 1.0 %copy-start.2 = (bf16[512,512]{1,0:T(8,128)(2,1)S(1)}, bf16[512,512]{1,0:T(8,128)(2,1)}, u32[]{:S(2)}) copy-start(bf16[512,512]{1,0:T(8,128)(2,1)} %proj_ref.3) | copy-start | bytes 1572868
  15.0 5.2 %copy-start.1 = (bf16[512,1536]{1,0:T(8,128)(2,1)S(1)}, bf16[512,1536]{1,0:T(8,128)(2,1)}, u32[]{:S(2)}) copy-start(bf16[512,1536]{1,0:T(8,128)(2,1)} %qkv_ref.3) | copy-start | bytes 4718596
  15.0 5.2 %copy-start.3 = (bf16[512,512]{1,0:T(8,128)(2,1)S(1)}, bf16[512,512]{1,0:T(8,128)(2,1)}, u32[]{:S(2)}) copy-start(bf16[512,512]{1,0:T(8,128)(2,1)} %proj_ref.3) | copy-start | bytes 1572868
  20.1 2.7 %collective-permute-start.3 = (bf16[32,2,64,128]{3,2,1,0:T(8,128)(2,1)S(1)}, bf16[32,2,64,128]{3,2,1,0:T(8,128)(2,1)S(1)}, u32[]{:S(2)}, u32[]{:S(2)}) collective-permute-start(bf16[32,2,64,128]{3,2,1,0:T(8,128)(2,1)S(1)} %get-tuple-element.38), channel_id=1, source_target_pairs={{0,8},{8,0},{1,9},{9,1},{2,10},{10,2},{3,11},{11,3},{4,12},{12,4},... | collective-permute-start | bytes 3145736 | tf_op jit(solution)/shard_map/ppermute | solution.py:353
  24.0 21.0 %all-to-all-start = ((bf16[8,512,128]{2,1,0:T(8,128)(2,1)}), bf16[8,512,128]{2,1,0:T(8,128)(2,1)S(1)}, u32[]{:S(2)}, u32[]{:S(2)}) async-start(bf16[8,512,128]{2,1,0:T(8,128)(2,1)} %bitcast.3), calls=%async_computation | async-start | bytes 2097152 | tf_op jit(solution)/shard_map/all_to_all | solution.py:403
  28.5 8.1 %collective-permute-start.4 = (bf16[2,2,6,6,512]{4,3,2,1,0:T(8,128)(2,1)S(1)}, bf16[2,2,6,6,512]{4,3,2,1,0:T(8,128)(2,1)S(1)}, u32[]{:S(2)}, u32[]{:S(2)}) collective-permute-start(bf16[2,2,6,6,512]{4,3,2,1,0:T(8,128)(2,1)S(1)} %get-tuple-element.39), channel_id=1, source_target_pairs={{0,7},{1,0},{2,1},{3,2},{4,3},{5,4},{6,5},{7,6},{8,15},{9,8},{10,9... | collective-permute-start | bytes 442376 | tf_op jit(solution)/shard_map/ppermute | solution.py:353
  45.8 18.1 %all-to-all-start.1 = ((bf16[16,64,128]{2,1,0:T(8,128)(2,1)}), bf16[16,64,128]{2,1,0:T(8,128)(2,1)S(1)}, u32[]{:S(2)}, u32[]{:S(2)}) async-start(bf16[16,64,128]{2,1,0:T(8,128)(2,1)} %bitcast.4), calls=%async_computation.1 | async-start | bytes 524288 | tf_op jit(solution)/shard_map/all_to_all | solution.py:406
  54.3 5.5 %collective-permute-start.5 = (bf16[2,2,3,24,512]{4,3,2,1,0:T(8,128)(2,1)S(1)}, bf16[2,2,3,24,512]{4,3,2,1,0:T(8,128)(2,1)S(1)}, u32[]{:S(2)}, u32[]{:S(2)}) collective-permute-start(bf16[2,2,3,24,512]{4,3,2,1,0:T(8,128)(2,1)S(1)} %halo_rows.1), channel_id=1, source_target_pairs={{0,120},{8,0},{16,8},{24,16},{32,24},{40,32},{48,40},{56,48},{64,5... | collective-permute-start | bytes 884744 | tf_op jit(solution)/shard_map/ppermute | solution.py:353
